TPU v7x, 256 devices: a whole 4x4x8 slice. The times are simulated.
256 devices in a mesh: dp: 4 (over y_hi, core), seq: 64 (over z, y_lo, x).
Axes of the slice: x: 4, y: 4 (y_hi: 2, y_lo: 2; y = y_hi * 2 + y_lo), z: 8, core: 2. Of those that a mesh axis runs over, the one named last changes fastest.
Arguments:
- hidden: bfloat16 [4, 64, 128, 1152], P('dp', 'seq'), may hold values from -6 to 6
- query_space: bfloat16 [4, 64, 128, 1152], P('dp', 'seq'), may hold values from -42 to 42
- key_space: bfloat16 [4, 64, 128, 1152], P('dp', 'seq'), may hold values from -42 to 42
- value_space: bfloat16 [4, 64, 128, 1152], P('dp', 'seq'), may hold values from -6 to 6
- positions: int32 [3, 4, 64, 128], P(None, 'dp'), may hold values from 0 to 252, as said below
- proj_space: bfloat16 [1152, 1152], P('dp'), may hold values from -0.1875 to 0.1875
- shift_time: float32 [4, 1152], P('dp'), may hold values from -3 to 3
- scale_time: float32 [4, 1152], P('dp'), may hold values from -1.8 to 1.8
- qkv_time: bfloat16 [1152, 3456], P('dp'), may hold values from -0.35355339 to 0.35355339
- grad_attn_time: bfloat16 [4, 64, 128, 1152], P('dp', None, 'seq'), may hold values from -6 to 6
- grad_resid: bfloat16 [4, 64, 128, 1152], P('dp', 'seq'), may hold values from -6 to 6
Outputs:
- grad_hidden: bfloat16 [4, 64, 128, 1152], P('dp', 'seq')
- grad_query: bfloat16 [4, 64, 128, 1152], P('dp', 'seq')
- grad_key: bfloat16 [4, 64, 128, 1152], P('dp', 'seq')
- grad_value: bfloat16 [4, 64, 128, 1152], P('dp', 'seq')
- grad_proj_space: float32 [1152, 1152], P('dp', 'seq')
- grad_qkv_time: float32 [1152, 3456], P('dp', 'seq')
- grad_shift: float32 [4, 1152], P('dp')
- grad_scale: float32 [4, 1152], P('dp')
Inputs may be any that keep to these rules, and one draw needn't show every extreme that they name: positions[0] is s * f for frame f with a stride s of 1 to 4 per clip, 4 in the first clip; positions[1] and positions[2] are the token's row p // 16 and column p % 16 within the frame plus an offset of 0 to 8 per clip, 8 in the first clip.
All inputs are finite; a program needn't handle non-finite values.
Results may differ from a plain program's by a relative error of at most 0.02.
The roundings to bfloat16 on the way count: a program that leaves them out, or rounds other values in their place, can miss the bound.
Values may be sent and summed in bfloat16 or wider, within the bound.
A program may use at most 128 MiB of HBM per device.

v0:
```python
import math

import jax
import jax.numpy as jnp
from jax import lax
from jax.sharding import PartitionSpec as P

HEADS = 16


epsilon = 1e-06


def rotate(values, places, direction):
    half_width = values.shape[-1] // 2
    frequency = 10000.0 ** (-jnp.arange(half_width, dtype=jnp.float32) / half_width)
    angles = places.astype(jnp.float32)[..., None] * frequency
    cosine = jnp.cos(angles)[..., None, :]
    sine_part = direction * jnp.sin(angles)[..., None, :]
    first_half = values[..., :half_width]
    second = values[..., half_width:]
    return jnp.concatenate(
        [first_half * cosine - second * sine_part, second * cosine + first_half * sine_part],
        axis=-1,
    )


def rotate_space(values, row_places, col_places, direction):
    half_width = values.shape[-1] // 2
    return jnp.concatenate(
        [
            rotate(values[..., :half_width], row_places, direction),
            rotate(values[..., half_width:], col_places, direction),
        ],
        axis=-1,
    )


def attend(query_rows, key_rows, value_rows):
    factor = 1.0 / math.sqrt(query_rows.shape[-1])
    scores = (
        jnp.einsum("gqhe,gkhe->ghqk", query_rows, key_rows, preferred_element_type=jnp.float32)
        * factor
    )
    exponent = jnp.exp(scores - jnp.max(scores, axis=-1, keepdims=True))
    weights = exponent / jnp.sum(exponent, axis=-1, keepdims=True)
    rounded = weights.astype(jnp.bfloat16)
    output = jnp.einsum("ghqk,gkhe->gqhe", rounded, value_rows, preferred_element_type=jnp.float32)
    return (weights, rounded, output)


def attend_back(query_rows, key_rows, value_rows, weights, rounded, output, grad_rows):
    factor = 1.0 / math.sqrt(query_rows.shape[-1])
    row_delta = jnp.einsum("gqhe,gqhe->ghq", grad_rows.astype(jnp.float32), output)
    grad_value = jnp.einsum(
        "ghqk,gqhe->gkhe", rounded, grad_rows, preferred_element_type=jnp.float32
    )
    grad_weights = jnp.einsum(
        "gqhe,gkhe->ghqk", grad_rows, value_rows, preferred_element_type=jnp.float32
    )
    grad_scores = (weights * (grad_weights - row_delta[..., None]) * factor).astype(jnp.bfloat16)
    grad_query = jnp.einsum(
        "ghqk,gkhe->gqhe", grad_scores, key_rows, preferred_element_type=jnp.float32
    )
    grad_key = jnp.einsum(
        "ghqk,gqhe->gkhe", grad_scores, query_rows, preferred_element_type=jnp.float32
    )
    return (grad_query, grad_key, grad_value)


def add_columns(left_side, piece_rows):
    return jnp.dot(left_side, piece_rows, preferred_element_type=jnp.float32)


def place_columns(right_side, piece_rows):
    product = lax.dot_general(
        right_side, piece_rows, (((1,), (1,)), ((), ())), preferred_element_type=jnp.float32
    )
    return product


def transposed_product(left_side, right_side):
    return lax.dot_general(
        left_side, right_side, (((0,), (0,)), ((), ())), preferred_element_type=jnp.float32
    )


def body(
    hidden,
    query_space,
    key_space,
    value_space,
    positions,
    proj_space,
    shift_time,
    scale_time,
    qkv_time,
    grad_attn_time,
    grad_resid,
):
    frames_dev, spot_count, model_width = (hidden.shape[1], hidden.shape[2], hidden.shape[3])
    frames, spots_dev = (grad_attn_time.shape[1], grad_attn_time.shape[2])
    head_count = HEADS
    head_size = model_width // head_count
    token_count = frames * spots_dev
    seq_place = lax.axis_index("seq")
    row_places = lax.dynamic_slice_in_dim(positions[1, 0], seq_place * frames_dev, frames_dev, 0)
    col_places = lax.dynamic_slice_in_dim(positions[2, 0], seq_place * frames_dev, frames_dev, 0)
    frame_places = lax.dynamic_slice_in_dim(positions[0, 0], seq_place * spots_dev, spots_dev, 1).T
    per_frame = (frames_dev, spot_count, head_count, head_size)
    space_query = rotate_space(
        query_space.reshape(per_frame).astype(jnp.float32), row_places, col_places, 1.0
    ).astype(jnp.bfloat16)
    space_key = rotate_space(
        key_space.reshape(per_frame).astype(jnp.float32), row_places, col_places, 1.0
    ).astype(jnp.bfloat16)
    space_value = value_space.reshape(per_frame)
    space_weights, space_rounded, space_out = attend(space_query, space_key, space_value)
    space_mixed = space_out.astype(jnp.bfloat16).reshape(frames_dev * spot_count, model_width)
    full_proj = lax.all_gather(proj_space, "dp", axis=0, tiled=True)
    resid = (
        hidden.reshape(-1, model_width).astype(jnp.float32)
        + jnp.dot(space_mixed, full_proj, preferred_element_type=jnp.float32)
    ).astype(jnp.bfloat16)
    resid_space = lax.all_to_all(
        resid.reshape(1, frames_dev, spot_count, model_width),
        "seq",
        split_axis=2,
        concat_axis=1,
        tiled=True,
    )
    resid_wide = resid_space.reshape(token_count, model_width).astype(jnp.float32)
    centered = resid_wide - jnp.mean(resid_wide, axis=-1, keepdims=True)
    inverse = lax.rsqrt(jnp.mean(centered * centered, axis=-1, keepdims=True) + epsilon)
    normed = centered * inverse
    modulated = (normed * (1.0 + scale_time) + shift_time).astype(jnp.bfloat16)
    projected = add_columns(modulated, lax.all_gather(qkv_time, "dp", axis=0, tiled=True))

    def arrange(values):
        return jnp.transpose(values.reshape(frames, spots_dev, head_count, head_size), (1, 0, 2, 3))

    def restore(values):
        return jnp.transpose(values, (1, 0, 2, 3)).reshape(token_count, model_width)

    time_query = rotate(arrange(projected[:, :model_width]), frame_places, 1.0).astype(jnp.bfloat16)
    time_key = rotate(
        arrange(projected[:, model_width : 2 * model_width]), frame_places, 1.0
    ).astype(jnp.bfloat16)
    time_value = arrange(projected[:, 2 * model_width :]).astype(jnp.bfloat16)
    time_weights, time_rounded, time_out = attend(time_query, time_key, time_value)
    grad_time = arrange(grad_attn_time.reshape(token_count, model_width))
    grad_time_query, grad_time_key, grad_time_value = attend_back(
        time_query, time_key, time_value, time_weights, time_rounded, time_out, grad_time
    )
    grad_projected = jnp.concatenate(
        [
            restore(rotate(grad_time_query, frame_places, -1.0)),
            restore(rotate(grad_time_key, frame_places, -1.0)),
            restore(grad_time_value),
        ],
        axis=-1,
    ).astype(jnp.bfloat16)
    grad_modulated = place_columns(
        grad_projected, lax.all_gather(qkv_time, "dp", axis=0, tiled=True)
    )
    grad_shift, grad_scale = lax.psum(
        (
            jnp.sum(grad_modulated, axis=0, keepdims=True),
            jnp.sum(grad_modulated * normed, axis=0, keepdims=True),
        ),
        "seq",
    )
    grad_normed = grad_modulated * (1.0 + scale_time)
    resid_back = (
        (
            grad_normed
            - jnp.mean(grad_normed, axis=-1, keepdims=True)
            - normed * jnp.mean(grad_normed * normed, axis=-1, keepdims=True)
        )
        * inverse
    ).astype(jnp.bfloat16)
    back_frames = lax.all_to_all(
        resid_back.reshape(1, frames, spots_dev, model_width),
        "seq",
        split_axis=1,
        concat_axis=2,
        tiled=True,
    )
    grad_hidden = (grad_resid.astype(jnp.float32) + back_frames.astype(jnp.float32)).astype(
        jnp.bfloat16
    )
    grad_flat = grad_hidden.reshape(-1, model_width)
    grad_space_out = (
        lax.dot_general(
            grad_flat, full_proj, (((1,), (1,)), ((), ())), preferred_element_type=jnp.float32
        )
        .astype(jnp.bfloat16)
        .reshape(per_frame)
    )
    grad_space_query, grad_space_key, grad_space_value = attend_back(
        space_query, space_key, space_value, space_weights, space_rounded, space_out, grad_space_out
    )
    full_shape = hidden.shape
    grad_query = (
        rotate_space(grad_space_query, row_places, col_places, -1.0)
        .astype(jnp.bfloat16)
        .reshape(full_shape)
    )
    grad_key = (
        rotate_space(grad_space_key, row_places, col_places, -1.0)
        .astype(jnp.bfloat16)
        .reshape(full_shape)
    )
    grad_value = grad_space_value.astype(jnp.bfloat16).reshape(full_shape)
    proj_flipped = transposed_product(grad_flat, space_mixed)
    qkv_flipped = transposed_product(grad_projected, modulated)
    partial_sums = (
        lax.psum_scatter(proj_flipped, "seq", scatter_dimension=0, tiled=True),
        lax.psum_scatter(qkv_flipped, "seq", scatter_dimension=0, tiled=True),
    )
    proj_block, qkv_block = (
        lax.psum_scatter(
            partial_sums[0].astype(jnp.bfloat16), "dp", scatter_dimension=1, tiled=True
        ).astype(jnp.float32),
        lax.psum_scatter(
            partial_sums[1].astype(jnp.bfloat16), "dp", scatter_dimension=1, tiled=True
        ).astype(jnp.float32),
    )
    grad_proj_space = proj_block.T
    grad_qkv_time = qkv_block.T
    return (
        grad_hidden,
        grad_query,
        grad_key,
        grad_value,
        grad_proj_space,
        grad_qkv_time,
        grad_shift,
        grad_scale,
    )


def solution(mesh):
    in_specs = (
        P("dp", "seq", None, None),
        P("dp", "seq", None, None),
        P("dp", "seq", None, None),
        P("dp", "seq", None, None),
        P(None, "dp", None, None),
        P("dp", None),
        P("dp", None),
        P("dp", None),
        P("dp", None),
        P("dp", None, "seq", None),
        P("dp", "seq", None, None),
    )
    out_specs = (
        P("dp", "seq", None, None),
        P("dp", "seq", None, None),
        P("dp", "seq", None, None),
        P("dp", "seq", None, None),
        P("dp", "seq"),
        P("dp", "seq"),
        P("dp", None),
        P("dp", None),
    )
    return jax.shard_map(body, mesh=mesh, in_specs=in_specs, out_specs=out_specs, check_vma=False)
```

profile of v0, /device:TPU:1, one launch (start us, length us, event | category | flops | bytes accessed | tf_op | source)
XLA Modules:
  0.0 907.7 jit_solution(2345650515361503754)
XLA Ops:
  12.3 34.1 %all-gather.3.cloned.1.call-done = bf16[1152,1152]{1,0:T(8,128)(2,1)} async-done(((bf16[288,1152]{1,0:T(8,128)(2,1)}), bf16[1152,1152]{1,0:T(8,128)(2,1)}) %all-gather.3.cloned.1.call-update) | async-done | bytes 2654224 | tf_op jit(solution)/shard_map/all_gather | solution.py:120
  46.5 2.4 fusion.4
  49.9 2.4 reduce.15
  53.1 10.2 %all-to-all-start = ((bf16[64,2,1152]{2,1,0:T(2,128)(2,1)}), bf16[64,2,1152]{2,1,0:T(2,128)(2,1)S(1)}, u32[]{:S(2)}, u32[]{:S(2)}) async-start(bf16[64,2,1152]{2,1,0:T(2,128)(2,1)} %reshape.584), calls=%async_computation | async-start | bytes 589824 | tf_op jit(solution)/shard_map/all_to_all | solution.py:125
  63.5 1.9 reshape_reshape.3
  67.7 8.0 all-to-all-done
  76.5 36.9 %all-gather.5.cloned.1.call-done = bf16[1152,3456]{1,0:T(8,128)(2,1)} async-done(((bf16[288,3456]{1,0:T(8,128)(2,1)}), bf16[1152,3456]{1,0:T(8,128)(2,1)}) %all-gather.5.cloned.1.call-update) | async-done | bytes 7962640 | tf_op jit(solution)/shard_map/all_gather | solution.py:137
  113.4 4.7 fusion.71
  124.6 2.4 fusion.83
  136.9 7.8 fusion.69
  144.7 217.6 %fusion = f32[64,1152]{1,0:T(8,128)S(1)} fusion(f32[3456,1152]{1,0:T(8,128)} %fusion.69), kind=kCustom, calls=%all-reduce-scatter | all-reduce-scatter fusion | flops 4718593 | bytes 16221184
  368.2 5.9 fusion.31
  375.4 1.9 collective-permute-done.9
  377.3 15.8 %collective-permute-start.5 = (bf16[64,1152]{1,0:T(8,128)(2,1)}, bf16[64,1152]{1,0:T(8,128)(2,1)}, u32[]{:S(2)}, u32[]{:S(2)}) collective-permute-start(bf16[64,1152]{1,0:T(8,128)(2,1)} %convert.198), channel_id=1, source_target_pairs={{0,6},{1,7},{2,8},{3,9},{4,10},{5,11},{6,12},{7,13},{8,14},{9,15},... | collective-permute-start | bytes 442376
  393.1 4.9 collective-permute-start.6
  398.0 6.2 collective-permute-start.7
  404.2 2.0 collective-permute-start.8
  406.1 3.4 collective-permute-start
  410.6 6.8 all-to-all-start.1
  417.6 17.7 %concatenate.81 = bf16[694,1152]{1,0:T(8,128)(2,1)} concatenate(bf16[54,1152]{1,0:T(8,128)(2,1)} %copy-done.34, bf16[64,1152]{1,0:T(8,128)(2,1)} %collective-permute-done.8, bf16[64,1152]{1,0:T(8,128)(2,1)} %collective-permute-done.7, bf16[64,1152]{1,0:T(8,128)(2,1)} %collective-permute-done.6, bf16[64,1152]{1,0:T(8,128)(2,1)} %collective-permute-done.5, ...), dimensions={0} | concatenate | bytes 3345408
  439.3 54.0 %reduce-scatter.11.cloned.1.call-done = bf16[288,54]{1,0:T(8,128)(2,1)} async-done(((bf16[1152,54]{1,0:T(8,128)(2,1)}), bf16[288,54]{1,0:T(8,128)(2,1)}) %reduce-scatter.11.cloned.1.call-update) | async-done | bytes 31120
  502.1 3.2 fusion.45
  507.5 311.8 %all-reduce.5 = (bf16[1152,1152]{1,0:T(8,128)(2,1)}, f32[1,1152]{1,0:T(1,128)}, f32[1,1152]{1,0:T(1,128)}) all-reduce(f32[1152,1152]{1,0:T(8,128)} %fusion.45, f32[1,1152]{1,0:T(1,128)S(1)} %copy-done.39, f32[1,1152]{1,0:T(1,128)S(1)} %copy-done.38), channel_id=2, replica_groups=mesh['dp'=4,'seq'=64] {'seq'}, use_global_device_ids=true, to_apply=%region_8.0.clone | all-reduce | flops 1329408 | bytes 7981056
  822.2 77.3 %reduce-scatter.9.cloned.1.call-done = bf16[288,18]{1,0:T(8,128)(2,1)} async-done(((bf16[1152,18]{1,0:T(8,128)(2,1)}), bf16[288,18]{1,0:T(8,128)(2,1)}) %reduce-scatter.9.cloned.1.call-update) | async-done | bytes 10384
  (204 shorter events, 52.4 us)
Async XLA Ops:
  7.2 39.2 %all-gather.3.cloned.1.call-start = ((), (), s32[]{:S(2)}) async-start(), calls=%async_computation.4 | async-start | bytes 3317760 | tf_op jit(solution)/shard_map/all_gather | solution.py:120
  7.9 105.4 %all-gather.5.cloned.1.call-start = ((), (), s32[]{:S(2)}) async-start(), calls=%async_computation.5 | async-start | bytes 9953280 | tf_op jit(solution)/shard_map/all_gather | solution.py:137
  11.1 35.4 %copy-start.47 = (f32[16,128]{1,0:T(8,128)}, f32[16,128]{1,0:T(8,128)S(1)}, u32[]{:S(2)}) copy-start(f32[16,128]{1,0:T(8,128)S(1)} %get-tuple-element.113) | copy-start | bytes 24580
  11.1 37.8 %copy-start.45 = (f32[16,128,128]{1,2,0:T(8,128)}, f32[16,128,128]{1,2,0:T(8,128)S(1)}, u32[]{:S(2)}) copy-start(f32[16,128,128]{1,2,0:T(8,128)S(1)} %get-tuple-element.114) | copy-start | bytes 3145732
  11.1 35.3 %copy-start.26 = (bf16[1,1,128,1152]{3,2,1,0:T(8,128)(2,1)S(1)}, bf16[1,1,128,1152]{3,2,1,0:T(8,128)(2,1)}, u32[]{:S(2)}) copy-start(bf16[1,1,128,1152]{3,2,1,0:T(8,128)(2,1)} %param.11) | copy-start | bytes 884740
  12.3 34.1 %copy-start.2 = (bf16[1,128,16,72]{1,3,2,0:T(8,128)(2,1)}, bf16[1,128,16,72]{1,3,2,0:T(8,128)(2,1)S(1)}, u32[]{:S(2)}) copy-start(bf16[1,128,16,72]{1,3,2,0:T(8,128)(2,1)S(1)} %get-tuple-element.115) | copy-start | bytes 884740
  48.9 17.7 %copy-start.41 = (f32[1,1152]{1,0:T(1,128)S(1)}, f32[1,1152]{1,0:T(1,128)}, u32[]{:S(2)}) copy-start(f32[1,1152]{1,0:T(1,128)} %param.17) | copy-start | bytes 13828
  48.9 17.7 %copy-start.40 = (f32[1,1152]{1,0:T(1,128)S(1)}, f32[1,1152]{1,0:T(1,128)}, u32[]{:S(2)}) copy-start(f32[1,1152]{1,0:T(1,128)} %param.18) | copy-start | bytes 13828
  53.1 22.5 %all-to-all-start = ((bf16[64,2,1152]{2,1,0:T(2,128)(2,1)}), bf16[64,2,1152]{2,1,0:T(2,128)(2,1)S(1)}, u32[]{:S(2)}, u32[]{:S(2)}) async-start(bf16[64,2,1152]{2,1,0:T(2,128)(2,1)} %reshape.584), calls=%async_computation | async-start | bytes 589824 | tf_op jit(solution)/shard_map/all_to_all | solution.py:125
  363.0 30.1 %collective-permute-start.1 = (bf16[64,1152]{1,0:T(8,128)(2,1)}, bf16[64,1152]{1,0:T(8,128)(2,1)S(1)}, u32[]{:S(2)}, u32[]{:S(2)}) collective-permute-start(bf16[64,1152]{1,0:T(8,128)(2,1)} %convert.198), channel_id=1, source_target_pairs={{0,2},{1,3},{2,4},{3,5},{4,6},{5,7},{6,8},{7,9},{8,10},{9,11},{10,... | collective-permute-start | bytes 442376
  364.3 33.7 %collective-permute-start.2 = (bf16[64,1152]{1,0:T(8,128)(2,1)}, bf16[64,1152]{1,0:T(8,128)(2,1)S(1)}, u32[]{:S(2)}, u32[]{:S(2)}) collective-permute-start(bf16[64,1152]{1,0:T(8,128)(2,1)} %convert.198), channel_id=1, source_target_pairs={{0,3},{1,4},{2,5},{3,6},{4,7},{5,8},{6,9},{7,10},{8,11},{9,12},{10... | collective-permute-start | bytes 442376
  365.6 38.6 %collective-permute-start.3 = (bf16[64,1152]{1,0:T(8,128)(2,1)}, bf16[64,1152]{1,0:T(8,128)(2,1)S(1)}, u32[]{:S(2)}, u32[]{:S(2)}) collective-permute-start(bf16[64,1152]{1,0:T(8,128)(2,1)} %convert.198), channel_id=1, source_target_pairs={{0,4},{1,5},{2,6},{3,7},{4,8},{5,9},{6,10},{7,11},{8,12},{9,13},{1... | collective-permute-start | bytes 442376
  366.9 39.2 %collective-permute-start.4 = (bf16[64,1152]{1,0:T(8,128)(2,1)}, bf16[64,1152]{1,0:T(8,128)(2,1)S(1)}, u32[]{:S(2)}, u32[]{:S(2)}) collective-permute-start(bf16[64,1152]{1,0:T(8,128)(2,1)} %convert.198), channel_id=1, source_target_pairs={{0,5},{1,6},{2,7},{3,8},{4,9},{5,10},{6,11},{7,12},{8,13},{9,14},{... | collective-permute-start | bytes 442376
  374.1 3.2 collective-permute-start.9
  377.3 33.4 %copy-start.34 = (bf16[54,1152]{1,0:T(8,128)(2,1)}, bf16[54,1152]{1,0:T(8,128)(2,1)S(1)}, u32[]{:S(2)}) copy-start(bf16[54,1152]{1,0:T(8,128)(2,1)S(1)} %collective-permute-done.9) | copy-start | bytes 373252
  377.3 40.2 %collective-permute-start.5 = (bf16[64,1152]{1,0:T(8,128)(2,1)}, bf16[64,1152]{1,0:T(8,128)(2,1)}, u32[]{:S(2)}, u32[]{:S(2)}) collective-permute-start(bf16[64,1152]{1,0:T(8,128)(2,1)} %convert.198), channel_id=1, source_target_pairs={{0,6},{1,7},{2,8},{3,9},{4,10},{5,11},{6,12},{7,13},{8,14},{9,15},... | collective-permute-start | bytes 442376
  393.1 24.4 %collective-permute-start.6 = (bf16[64,1152]{1,0:T(8,128)(2,1)}, bf16[64,1152]{1,0:T(8,128)(2,1)}, u32[]{:S(2)}, u32[]{:S(2)}) collective-permute-start(bf16[64,1152]{1,0:T(8,128)(2,1)} %convert.198), channel_id=1, source_target_pairs={{0,7},{1,8},{2,9},{3,10},{4,11},{5,12},{6,13},{7,14},{8,15},{9,16}... | collective-permute-start | bytes 442376
  398.0 19.6 %collective-permute-start.7 = (bf16[64,1152]{1,0:T(8,128)(2,1)}, bf16[64,1152]{1,0:T(8,128)(2,1)}, u32[]{:S(2)}, u32[]{:S(2)}) collective-permute-start(bf16[64,1152]{1,0:T(8,128)(2,1)} %convert.198), channel_id=1, source_target_pairs={{0,8},{1,9},{2,10},{3,11},{4,12},{5,13},{6,14},{7,15},{8,16},{9,17... | collective-permute-start | bytes 442376
  404.2 13.4 %collective-permute-start.8 = (bf16[64,1152]{1,0:T(8,128)(2,1)}, bf16[64,1152]{1,0:T(8,128)(2,1)}, u32[]{:S(2)}, u32[]{:S(2)}) collective-permute-start(bf16[64,1152]{1,0:T(8,128)(2,1)} %convert.198), channel_id=1, source_target_pairs={{0,9},{1,10},{2,11},{3,12},{4,13},{5,14},{6,15},{7,16},{8,17},{9,1... | collective-permute-start | bytes 442376
  406.1 11.4 %collective-permute-start = (bf16[64,1152]{1,0:T(8,128)(2,1)}, bf16[64,1152]{1,0:T(8,128)(2,1)}, u32[]{:S(2)}, u32[]{:S(2)}) collective-permute-start(bf16[64,1152]{1,0:T(8,128)(2,1)} %convert.198), channel_id=1, source_target_pairs={{0,1},{1,2},{2,3},{3,4},{4,5},{5,6},{6,7},{7,8},{8,9},{9,10},{10,1... | collective-permute-start | bytes 442376
  410.6 84.3 %all-to-all-start.1 = ((bf16[1,64,2,1152]{3,2,0,1:T(2,128)(2,1)}), bf16[1,64,2,1152]{3,2,0,1:T(2,128)(2,1)}, u32[]{:S(2)}, u32[]{:S(2)}) async-start(bf16[1,64,2,1152]{3,2,0,1:T(2,128)(2,1)} %bitcast.40), calls=%async_computation.1 | async-start | bytes 589824 | tf_op jit(solution)/shard_map/all_to_all | solution.py:182
  417.4 79.6 %copy-start = (bf16[1152,1152]{1,0:T(8,128)(2,1)S(1)}, bf16[1152,1152]{1,0:T(8,128)(2,1)}, u32[]{:S(2)}) copy-start(bf16[1152,1152]{1,0:T(8,128)(2,1)} %all-gather.3.cloned.1.call-done) | copy-start | bytes 7962628
  417.4 75.9 %reduce-scatter.11.cloned.1.call-start = ((), (), s32[]{:S(2)}) async-start(), calls=%async_computation.7 | async-start | bytes 368640
  437.2 462.4 %reduce-scatter.9.cloned.1.call-start = ((), (), s32[]{:S(2)}) async-start(), calls=%async_computation.6 | async-start | bytes 368640
  (41 other events, 113.7 us)
Sparse Core Ops, SparseCore 0:
  9.9 36.5 all-gather.2
  48.3 65.0 all-gather.4
  437.3 55.9 reduce-scatter.10
  821.3 78.1 reduce-scatter.8
where the time goes:
time: 909 us; the launch traced here: 908 us
  blocking collectives  529 us (58%)
  waiting for transfers between devices  214 us (24%)
  starting transfers between devices  56 us (6%)
  local copies, waits for them, and re-layouts  43.9 us (5%)
  matrix products  35.9 us (4%)
  between operations  16 us (2%)
  other arithmetic  12.7 us (1%)
    unnamed x2, blocking collectives  529 us
    unnamed x16, waiting for transfers between devices  135 us
    unnamed x12, starting transfers between devices  39 us
    all_gather x1, waiting for transfers between devices, body(): lax.all_gather(qkv_time, 'dp', axis=0, tiled=True)  36.9 us
    all_gather x1, waiting for transfers between devices, body(): full_proj = lax.all_gather(proj_space, 'dp', axis=0, tiled=True)  34.1 us
    unnamed x115, local copies, waits for them, and re-layouts  27.7 us
  transfers between devices with their start and end apart: 16, of which 6 were waited for; matrix products, arithmetic and copies ran while one was open for 5% of the time, Pallas kernels for 0%

commit v1 on v0

--- a/solution.py
+++ b/solution.py
@@ -3,6 +3,8 @@
 import jax
 import jax.numpy as jnp
 from jax import lax
+from jax.experimental import pallas as pl
+from jax.experimental.pallas import tpu as pltpu
 from jax.sharding import PartitionSpec as P
 
 HEADS = 16
@@ -79,10 +81,207 @@
     return product
 
 
-def transposed_product(left_side, right_side):
-    return lax.dot_general(
-        left_side, right_side, (((0,), (0,)), ((), ())), preferred_element_type=jnp.float32
-    )
+MESH = pl.DeviceIdType.MESH
+
+PIECE_ROWS = 80
+HALF_LANES = 640
+KEEP_LANES = 384
+ORDER = ("x_near", "y_near", "x_far", "z_near")
+
+
+def place():
+    dp, seq = lax.axis_index("dp"), lax.axis_index("seq")
+    hi, core = dp // 2, dp % 2
+    z, lo, x = seq // 8, (seq // 4) % 2, seq % 4
+    return hi, core, z, lo, x
+
+
+def device(hi, core, z, lo, x):
+    return (hi * 2 + core, z * 8 + lo * 4 + x)
+
+
+def order_of(group):
+    return [ORDER[(group + step) % 4] for step in range(4)]
+
+
+def piece_of(group, block):
+    bits = {name: (block // (8 >> step)) % 2 for step, name in enumerate(order_of(group))}
+    x = bits["x_far"] * 2 + (bits["x_near"] + bits["x_far"]) % 2
+    return (group * 2 + bits["z_near"]) * 8 + bits["y_near"] * 4 + x
+
+
+def sum_kernel(
+    left_ref, right_ref, out_ref, twin_left, twin_right, work, got0, got1, got2, got3, last, final,
+    twin_send, twin_recv, step_send, step_recv, final_send, final_recv,
+):
+    hi, core, z, lo, x = place()
+    near, pair = z % 2, z // 2
+    bits = {"x_near": (x % 2 + x // 2) % 2, "x_far": x // 2, "y_near": lo, "z_near": near}
+    partners = {
+        "x_near": device(hi, core, z, lo, x + 1 - 2 * (x % 2)),
+        "x_far": device(hi, core, z, lo, 3 - x),
+        "y_near": device(hi, core, z, 1 - lo, x),
+        "z_near": device(hi, core, z + 1 - 2 * near, lo, x),
+    }
+    twin = device(hi, 1 - core, z, lo, x)
+    others = []
+    for step_hi in range(2):
+        for step_pair in range(4):
+            if step_hi + step_pair > 0:
+                to_hi, to_pair = (hi + step_hi) % 2, (pair + step_pair) % 4
+                others.append(
+                    (step_hi * 4 + step_pair, to_hi, to_pair,
+                     device(to_hi, core, to_pair * 2 + near, lo, x))
+                )
+
+    barrier = pltpu.get_barrier_semaphore()
+    everyone = [twin] + list(partners.values()) + [other[3] for other in others]
+    for peer in everyone:
+        pl.semaphore_signal(barrier, inc=1, device_id=peer, device_id_type=MESH)
+    pl.semaphore_wait(barrier, len(everyone))
+
+    def send(source, target, send_sem, recv_sem, peer):
+        copy = pltpu.make_async_remote_copy(
+            src_ref=source, dst_ref=target, send_sem=send_sem, recv_sem=recv_sem,
+            device_id=peer, device_id_type=MESH,
+        )
+        copy.start()
+        return copy
+
+    twin_copies = [
+        send(right_ref.at[1 - core], twin_right, twin_send.at[0], twin_recv.at[0], twin),
+        send(left_ref, twin_left, twin_send.at[1], twin_recv.at[1], twin),
+    ]
+    for copy in twin_copies:
+        copy.wait_recv()
+
+    got = [got0, got1, got2, got3]
+    copies = {}
+
+    def fill(group, start):
+        def quarter(at, _):
+            first = start + at * 4
+            pieces = [piece_of(group, first + j) for j in range(4)]
+            own = jnp.concatenate([left_ref[piece] for piece in pieces], axis=0)
+            other = jnp.concatenate([twin_left[piece] for piece in pieces], axis=0)
+            total = jnp.dot(own, right_ref[core], preferred_element_type=jnp.float32)
+            total += jnp.dot(other, twin_right[...], preferred_element_type=jnp.float32)
+            work[group, pl.ds(first, 4)] = total.astype(jnp.bfloat16).reshape(
+                4, PIECE_ROWS, HALF_LANES
+            )
+            return 0
+
+        lax.fori_loop(0, 2, quarter, 0)
+
+    def take(group, step, start, count, offset):
+        def one(at, _):
+            total = work[group, start + at].astype(jnp.float32)
+            total += got[step][group, offset + at].astype(jnp.float32)
+            work[group, start + at] = total.astype(jnp.bfloat16)
+            return 0
+
+        lax.fori_loop(0, count, one, 0)
+
+    base = [0, 0, 0, 0]
+    for group in range(4):
+        name = order_of(group)[0]
+        away = (1 - bits[name]) * 8
+        fill(group, away)
+        copies[group, 0] = send(
+            work.at[group, pl.ds(away, 8)], got[0].at[group],
+            step_send.at[group, 0], step_recv.at[group, 0], partners[name],
+        )
+    for group in range(4):
+        base[group] = bits[order_of(group)[0]] * 8
+        fill(group, base[group])
+    for step in range(1, 4):
+        half = 8 >> step
+        for group in range(4):
+            name = order_of(group)[step]
+            away = (1 - bits[name]) * half
+            copies[group, step - 1].wait_recv()
+            take(group, step - 1, base[group] + away, half, away)
+            copies[group, step] = send(
+                work.at[group, pl.ds(base[group] + away, half)], got[step].at[group],
+                step_send.at[group, step], step_recv.at[group, step], partners[name],
+            )
+            mine = bits[name] * half
+            take(group, step - 1, base[group] + mine, half, mine)
+            base[group] = base[group] + mine
+    for group in range(4):
+        copies[group, 3].wait_recv()
+        total = work[group, base[group]].astype(jnp.float32) + got3[group, 0].astype(jnp.float32)
+        total = total.astype(jnp.bfloat16)
+        last[group, 0] = total[:, :KEEP_LANES]
+        last[group, 1] = total[:, HALF_LANES - KEEP_LANES :]
+    ends = []
+    for slot, to_hi, to_pair, peer in others:
+        ends.append(
+            send(
+                last.at[to_pair, to_hi], final.at[slot], final_send.at[slot], final_recv.at[slot], peer
+            )
+        )
+    total = last[pair, hi].astype(jnp.float32)
+    for (slot, _, _, _), copy in zip(others, ends):
+        copy.wait_recv()
+        total += final[slot].astype(jnp.float32)
+    out_ref[...] = total
+    for copy in twin_copies + list(copies.values()) + ends:
+        copy.wait_send()
+
+
+def sum_products(left, right):
+    depth = left.shape[2]
+    block = (PIECE_ROWS, HALF_LANES)
+    return pl.pallas_call(
+        sum_kernel,
+        out_shape=jax.ShapeDtypeStruct((PIECE_ROWS, KEEP_LANES), jnp.float32),
+        in_specs=[pl.BlockSpec(memory_space=pltpu.VMEM)] * 2,
+        out_specs=pl.BlockSpec(memory_space=pltpu.VMEM),
+        scratch_shapes=[
+            pltpu.VMEM(left.shape, jnp.bfloat16),
+            pltpu.VMEM((depth, HALF_LANES), jnp.bfloat16),
+            pltpu.VMEM((4, 16) + block, jnp.bfloat16),
+            pltpu.VMEM((4, 8) + block, jnp.bfloat16),
+            pltpu.VMEM((4, 4) + block, jnp.bfloat16),
+            pltpu.VMEM((4, 2) + block, jnp.bfloat16),
+            pltpu.VMEM((4, 1) + block, jnp.bfloat16),
+            pltpu.VMEM((4, 2, PIECE_ROWS, KEEP_LANES), jnp.bfloat16),
+            pltpu.VMEM((8, PIECE_ROWS, KEEP_LANES), jnp.bfloat16),
+            pltpu.SemaphoreType.DMA((2,)),
+            pltpu.SemaphoreType.DMA((2,)),
+            pltpu.SemaphoreType.DMA((4, 4)),
+            pltpu.SemaphoreType.DMA((4, 4)),
+            pltpu.SemaphoreType.DMA((8,)),
+            pltpu.SemaphoreType.DMA((8,)),
+        ],
+        compiler_params=pltpu.CompilerParams(
+            collective_id=3, has_side_effects=True, vmem_limit_bytes=40 * 1024 * 1024
+        ),
+    )(left, right)
+
+
+def weight_gradients(grad_projected, modulated, grad_flat, space_mixed):
+    tokens, width = modulated.shape
+    qkv_rows = grad_projected.T.reshape(64, -1, tokens)
+    proj_rows = grad_flat.T.reshape(64, -1, tokens)
+    n_qkv, n_proj = qkv_rows.shape[1], proj_rows.shape[1]
+    left = jnp.concatenate(
+        [
+            jnp.pad(qkv_rows, ((0, 0), (0, PIECE_ROWS - n_qkv), (0, 0))),
+            jnp.pad(proj_rows, ((0, 0), (n_qkv, PIECE_ROWS - n_qkv - n_proj), (0, 0))),
+        ],
+        axis=2,
+    )
+    part = width // 4
+    right = jnp.concatenate([modulated, space_mixed], axis=0).reshape(2 * tokens, 2, 2, part)
+    right = jnp.transpose(right, (2, 0, 1, 3)).reshape(2, 2 * tokens, 2 * part)
+    right = jnp.pad(right, ((0, 0), (0, 0), (0, HALF_LANES - 2 * part)))
+    summed = sum_products(left, right)
+    hi = lax.axis_index("dp") // 2
+    start = hi * (part + KEEP_LANES - HALF_LANES)
+    kept = lax.dynamic_slice(summed, (0, start), (n_qkv + n_proj, part)).T
+    return kept[:, n_qkv:], kept[:, :n_qkv]
 
 
 def body(
@@ -212,22 +411,9 @@
         .reshape(full_shape)
     )
     grad_value = grad_space_value.astype(jnp.bfloat16).reshape(full_shape)
-    proj_flipped = transposed_product(grad_flat, space_mixed)
-    qkv_flipped = transposed_product(grad_projected, modulated)
-    partial_sums = (
-        lax.psum_scatter(proj_flipped, "seq", scatter_dimension=0, tiled=True),
-        lax.psum_scatter(qkv_flipped, "seq", scatter_dimension=0, tiled=True),
-    )
-    proj_block, qkv_block = (
-        lax.psum_scatter(
-            partial_sums[0].astype(jnp.bfloat16), "dp", scatter_dimension=1, tiled=True
-        ).astype(jnp.float32),
-        lax.psum_scatter(
-            partial_sums[1].astype(jnp.bfloat16), "dp", scatter_dimension=1, tiled=True
-        ).astype(jnp.float32),
-    )
-    grad_proj_space = proj_block.T
-    grad_qkv_time = qkv_block.T
+    grad_proj_space, grad_qkv_time = weight_gradients(
+        grad_projected, modulated, grad_flat, space_mixed
+    )
     return (
         grad_hidden,
         grad_query,

time: 909 us -> 407 us (0.45)
  blocking collectives: 529 us -> 134 us
  waiting for transfers between devices: 214 us -> 81.7 us
  Pallas kernels: 0 us -> 88.4 us
  starting transfers between devices: 56 us -> 20.7 us
  local copies, waits for them, and re-layouts: 43.9 us -> 28.2 us
  matrix products: 35.9 us -> 26.7 us
    unnamed x2 -> x0, blocking collectives: 529 us -> none
    psum x0 -> x1, blocking collectives: none -> 134 us  [body(): lax.psum((jnp.sum(grad_modulated, axis=0, keepdims=True), jnp.sum(grad_mo...]
    unnamed x16 -> x2, waiting for transfers between devices: 135 us -> 1.38 us
    pallas_call x0 -> x1, Pallas kernels: none -> 88.4 us  [sum_products(): pl.pallas_call(sum_kernel, out_shape=jax.ShapeDtypeStruct((PIECE_ROWS, KE...]
    unnamed x12 -> x0, starting transfers between devices: 39 us -> none
    unnamed x115 -> x102, local copies, waits for them, and re-layouts: 27.7 us -> 6.31 us
    dot_general x2 -> x0, matrix products: 11 us -> none  [transposed_product(): lax.dot_general(left_side, right_side, (((0,), (0,)), ((), ())), preferre...]
  transfers between devices with their start and end apart: 16 -> 4, of which waited for: 6 -> 3; matrix products, arithmetic and copies ran while one was open for 5% -> 5% of each run, Pallas kernels for 0% -> 0%
where the time goes in v1:
time: 407 us
  blocking collectives  134 us (33%)
  Pallas kernels  88.4 us (22%)
  waiting for transfers between devices  81.7 us (20%)
  local copies, waits for them, and re-layouts  28.2 us (7%)
  matrix products  26.7 us (7%)
  starting transfers between devices  20.7 us (5%)
  between operations  14.9 us (4%)
  other arithmetic  11.8 us (3%)
    psum x1, blocking collectives, body(): lax.psum((jnp.sum(grad_modulated, axis=0, keepdims=True), jnp.sum(grad_mo...  134 us
    pallas_call x1, Pallas kernels, sum_products(): pl.pallas_call(sum_kernel, out_shape=jax.ShapeDtypeStruct((PIECE_ROWS, KE...  88.4 us
    all_gather x1, waiting for transfers between devices, body(): lax.all_gather(qkv_time, 'dp', axis=0, tiled=True)  36.9 us
    all_gather x1, waiting for transfers between devices, body(): full_proj = lax.all_gather(proj_space, 'dp', axis=0, tiled=True)  34.1 us
    all_to_all x1, starting transfers between devices, body(): lax.all_to_all(resid_back.reshape(1, frames, spots_dev, model_width), 'se...  10.4 us
    all_to_all x1, starting transfers between devices, body(): lax.all_to_all(resid.reshape(1, frames_dev, spot_count, model_width), 'se...  10.2 us
    all_to_all x1, waiting for transfers between devices, body(): lax.all_to_all(resid.reshape(1, frames_dev, spot_count, model_width), 'se...  9.28 us
  transfers between devices with their start and end apart: 4, of which 3 were waited for; matrix products, arithmetic and copies ran while one was open for 5% of the time, Pallas kernels for 0%

profile of v1, /device:TPU:1, one launch (start us, length us, event | category | flops | bytes accessed | tf_op | source)
XLA Modules:
  0.0 406.8 jit_solution(3114278929010196000)
XLA Ops:
  12.4 34.1 %all-gather.3.cloned.1.call-done = bf16[1152,1152]{1,0:T(8,128)(2,1)} async-done(((bf16[288,1152]{1,0:T(8,128)(2,1)}), bf16[1152,1152]{1,0:T(8,128)(2,1)}) %all-gather.3.cloned.1.call-update) | async-done | bytes 2654224 | tf_op jit(solution)/shard_map/all_gather | solution.py:319
  46.5 2.4 fusion.6
  49.9 2.4 reduce.17
  53.1 10.2 %all-to-all-start = ((bf16[64,2,1152]{2,1,0:T(2,128)(2,1)}), bf16[64,2,1152]{2,1,0:T(2,128)(2,1)S(1)}, u32[]{:S(2)}, u32[]{:S(2)}) async-start(bf16[64,2,1152]{2,1,0:T(2,128)(2,1)} %reshape.621), calls=%async_computation | async-start | bytes 589824 | tf_op jit(solution)/shard_map/all_to_all | solution.py:324
  63.5 1.9 reshape_reshape.3
  66.4 9.3 %all-to-all-done = bf16[64,2,1152]{2,1,0:T(2,128)(2,1)S(1)} async-done(((bf16[64,2,1152]{2,1,0:T(2,128)(2,1)}), bf16[64,2,1152]{2,1,0:T(2,128)(2,1)S(1)}, u32[]{:S(2)}, u32[]{:S(2)}) %all-to-all-start) | async-done | bytes 294944 | tf_op jit(solution)/shard_map/all_to_all | solution.py:324
  76.5 36.9 %all-gather.5.cloned.1.call-done = bf16[1152,3456]{1,0:T(8,128)(2,1)} async-done(((bf16[288,3456]{1,0:T(8,128)(2,1)}), bf16[1152,3456]{1,0:T(8,128)(2,1)}) %all-gather.5.cloned.1.call-update) | async-done | bytes 7962640 | tf_op jit(solution)/shard_map/all_gather | solution.py:336
  113.4 4.7 %fusion.33 = f32[128,3456]{1,0:T(8,128)S(1)} fusion(bf16[1152,3456]{1,0:T(8,128)(2,1)} %all-gather.5.cloned.1.call-done, bf16[1,1,128,1152]{3,2,1,0:T(8,128)(2,1)S(1)} %get-tuple-element.47, f32[1152]{0:T(1024)S(1)} %reduce.11, f32[1152]{0:T(1024)S(1)} %add_reduce_fusion, f32[128]{0:T(128)S(1)} %add_rsqrt_fusion, f32[128]{0:T(128)S(1)} %broadcast_multiply_fusion.5), kind=kOutput, calls=%fused_computation.78 | convolution fusion | flops 1020100608 | bytes 10037248 | tf_op jit(solution)/shard_map/dot_general | solution.py:74
  118.2 1.7 convert_element_type.233
  122.9 1.7 subtract_convert_fusion.3
  124.6 2.5 fusion.68
  127.1 1.7 fusion.20
  131.4 1.2 reshape.596
  132.6 1.6 subtract_convert_fusion
  136.9 6.2 %multiply_reduce_fusion = (f32[1152]{0:T(1024)S(1)}, f32[128]{0:T(128)S(1)}, f32[128]{0:T(128)S(1)}, f32[1152]{0:T(1024)S(1)}, f32[128,1152]{1,0:T(8,128)S(1)}) fusion(bf16[1,1,128,1152]{3,2,1,0:T(8,128)(2,1)S(1)} %get-tuple-element.47, f32[128]{0:T(128)S(1)} %add_rsqrt_fusion, f32[128]{0:T(128)S(1)} %broadcast_multiply_fusion.5, ...), kind=kOutput, calls=%fused_computation.53 | convolution fusion | flops 1020687872 | bytes 9747968 | tf_op jit(solution)/shard_map/dot_general | solution.py:78
  144.3 10.4 %all-to-all-start.1 = ((bf16[1,64,2,1152]{3,2,0,1:T(2,128)(2,1)}), bf16[1,64,2,1152]{3,2,0,1:T(2,128)(2,1)}, u32[]{:S(2)}, u32[]{:S(2)}) async-start(bf16[1,64,2,1152]{3,2,0,1:T(2,128)(2,1)} %bitcast.40), calls=%async_computation.1 | async-start | bytes 589824 | tf_op jit(solution)/shard_map/all_to_all | solution.py:381
  156.0 2.4 copy.122
  158.3 2.2 reshape.602
  160.5 134.5 %all-reduce.3 = (f32[1,1152]{1,0:T(1,128)}, f32[1,1152]{1,0:T(1,128)}) all-reduce(f32[1,1152]{1,0:T(1,128)S(1)} %broadcast_in_dim.4, f32[1,1152]{1,0:T(1,128)S(1)} %broadcast_in_dim.5), channel_id=1, replica_groups=mesh['dp'=4,'seq'=64] {'seq'}, use_global_device_ids=true, to_apply=%region_9.0 | all-reduce | flops 2304 | bytes 18432 | tf_op jit(solution)/shard_map/psum | solution.py:365
  295.0 1.9 reshape.609
  298.8 1.6 convolution_convert_fusion
  300.4 1.2 copy.117
  301.7 2.5 convolution_convert_fusion.2
  307.0 88.4 %shard_map.170 = f32[80,384]{1,0:T(8,128)S(1)} custom-call(bf16[64,80,256]{2,1,0:T(8,128)(2,1)S(1)} %fusion.4.left_ref, bf16[2,256,640]{2,1,0:T(8,128)(2,1)S(1)} %pad.14.right_ref), custom_call_target="tpu_custom_call" | custom-call | tf_op jit(solution)/shard_map/pallas_call | solution.py:236
  (174 shorter events, 28.4 us)
Async XLA Ops:
  7.2 2.1 copy-start.37
  7.2 39.2 %all-gather.3.cloned.1.call-start = ((), (), s32[]{:S(2)}) async-start(), calls=%async_computation.2 | async-start | bytes 3317760 | tf_op jit(solution)/shard_map/all_gather | solution.py:319
  7.9 105.5 %all-gather.5.cloned.1.call-start = ((), (), s32[]{:S(2)}) async-start(), calls=%async_computation.3 | async-start | bytes 9953280 | tf_op jit(solution)/shard_map/all_gather | solution.py:336
  8.9 2.2 copy-start.32
  11.1 35.4 %copy-start.44 = (f32[16,128]{1,0:T(8,128)}, f32[16,128]{1,0:T(8,128)S(1)}, u32[]{:S(2)}) copy-start(f32[16,128]{1,0:T(8,128)S(1)} %get-tuple-element.101) | copy-start | bytes 24580
  11.1 37.8 %copy-start.42 = (f32[16,128,128]{1,2,0:T(8,128)}, f32[16,128,128]{1,2,0:T(8,128)S(1)}, u32[]{:S(2)}) copy-start(f32[16,128,128]{1,2,0:T(8,128)S(1)} %get-tuple-element.102) | copy-start | bytes 3145732
  11.1 35.4 %copy-start.27 = (bf16[1,1,128,1152]{3,2,1,0:T(8,128)(2,1)S(1)}, bf16[1,1,128,1152]{3,2,1,0:T(8,128)(2,1)}, u32[]{:S(2)}) copy-start(bf16[1,1,128,1152]{3,2,1,0:T(8,128)(2,1)} %param.11) | copy-start | bytes 884740
  12.3 34.1 %copy-start.5 = (bf16[1,128,16,72]{1,3,2,0:T(8,128)(2,1)}, bf16[1,128,16,72]{1,3,2,0:T(8,128)(2,1)S(1)}, u32[]{:S(2)}) copy-start(bf16[1,128,16,72]{1,3,2,0:T(8,128)(2,1)S(1)} %get-tuple-element.103) | copy-start | bytes 884740
  46.5 17.0 %copy-start.30 = (bf16[1,64,2,1152]{3,2,1,0:T(2,128)(2,1)S(1)}, bf16[1,64,2,1152]{3,2,1,0:T(2,128)(2,1)}, u32[]{:S(2)}) copy-start(bf16[1,64,2,1152]{3,2,1,0:T(2,128)(2,1)} %param.20) | copy-start | bytes 884740
  48.9 16.4 %copy-start.39 = (f32[1,1152]{1,0:T(1,128)S(1)}, f32[1,1152]{1,0:T(1,128)}, u32[]{:S(2)}) copy-start(f32[1,1152]{1,0:T(1,128)} %param.17) | copy-start | bytes 13828
  48.9 16.5 %copy-start.38 = (f32[1,1152]{1,0:T(1,128)S(1)}, f32[1,1152]{1,0:T(1,128)}, u32[]{:S(2)}) copy-start(f32[1,1152]{1,0:T(1,128)} %param.18) | copy-start | bytes 13828
  53.1 22.5 %all-to-all-start = ((bf16[64,2,1152]{2,1,0:T(2,128)(2,1)}), bf16[64,2,1152]{2,1,0:T(2,128)(2,1)S(1)}, u32[]{:S(2)}, u32[]{:S(2)}) async-start(bf16[64,2,1152]{2,1,0:T(2,128)(2,1)} %reshape.621), calls=%async_computation | async-start | bytes 589824 | tf_op jit(solution)/shard_map/all_to_all | solution.py:324
  124.6 2.5 copy-start.9
  136.9 18.7 %copy-start.1 = (bf16[128,3456]{1,0:T(8,128)(2,1)}, bf16[128,3456]{1,0:T(8,128)(2,1)S(1)}, u32[]{:S(2)}) copy-start(bf16[128,3456]{1,0:T(8,128)(2,1)S(1)} %constant_dynamic-update-slice_fusion) | copy-start | bytes 2654212
  143.1 12.4 %copy-start.6 = (bf16[1,128,16,72]{1,3,2,0:T(8,128)(2,1)S(1)}, bf16[1,128,16,72]{1,3,2,0:T(8,128)(2,1)}, u32[]{:S(2)}) copy-start(bf16[1,128,16,72]{1,3,2,0:T(8,128)(2,1)} %copy-done.5) | copy-start | bytes 884740
  144.3 150.7 %all-to-all-start.1 = ((bf16[1,64,2,1152]{3,2,0,1:T(2,128)(2,1)}), bf16[1,64,2,1152]{3,2,0,1:T(2,128)(2,1)}, u32[]{:S(2)}, u32[]{:S(2)}) async-start(bf16[1,64,2,1152]{3,2,0,1:T(2,128)(2,1)} %bitcast.40), calls=%async_computation.1 | async-start | bytes 589824 | tf_op jit(solution)/shard_map/all_to_all | solution.py:381
  155.9 142.8 %copy-start = (bf16[1152,1152]{1,0:T(8,128)(2,1)S(1)}, bf16[1152,1152]{1,0:T(8,128)(2,1)}, u32[]{:S(2)}) copy-start(bf16[1152,1152]{1,0:T(8,128)(2,1)} %all-gather.3.cloned.1.call-done) | copy-start | bytes 7962628
  296.8 4.8 %copy-start.45 = (f32[16,128]{1,0:T(8,128)S(1)}, f32[16,128]{1,0:T(8,128)}, u32[]{:S(2)}) copy-start(f32[16,128]{1,0:T(8,128)} %copy-done.44) | copy-start | bytes 24580
  300.4 3.8 copy-start.8
  300.4 3.9 copy-start.33
  301.6 2.7 copy-start.43
  306.9 89.8 %copy-start.34 = (bf16[16,72,128]{2,1,0:T(8,128)(2,1)S(1)}, bf16[16,72,128]{2,1,0:T(8,128)(2,1)}, u32[]{:S(2)}) copy-start(bf16[16,72,128]{2,1,0:T(8,128)(2,1)} %convolution_convert_fusion.2) | copy-start | bytes 884740
  306.9 90.7 %copy-start.35 = (f32[128,18]{0,1:T(8,128)S(1)}, f32[128,18]{0,1:T(8,128)}, u32[]{:S(2)}) copy-start(f32[128,18]{0,1:T(8,128)} %get-tuple-element.92) | copy-start | bytes 27652
  307.0 90.7 %copy-start.36 = (f32[128,18]{0,1:T(8,128)S(1)}, f32[128,18]{0,1:T(8,128)}, u32[]{:S(2)}) copy-start(f32[128,18]{0,1:T(8,128)} %get-tuple-element.100) | copy-start | bytes 27652
  (26 other events, 40.2 us)
Sparse Core Ops, SparseCore 0:
  9.9 36.5 all-gather.2
  48.3 65.0 all-gather.4

commit v2 on v1

--- a/solution.py
+++ b/solution.py
@@ -98,6 +98,22 @@
 
 def device(hi, core, z, lo, x):
     return (hi * 2 + core, z * 8 + lo * 4 + x)
+
+
+def send(source, target, sends, recvs, at, peer):
+    copy = pltpu.make_async_remote_copy(
+        src_ref=source, dst_ref=target, send_sem=sends.at[at], recv_sem=recvs.at[at],
+        device_id=peer, device_id_type=MESH,
+    )
+    copy.start()
+    return copy
+
+
+def meet(peers):
+    barrier = pltpu.get_barrier_semaphore()
+    for peer in peers:
+        pl.semaphore_signal(barrier, inc=1, device_id=peer, device_id_type=MESH)
+    pl.semaphore_wait(barrier, len(peers))
 
 
 def order_of(group):
@@ -134,23 +150,10 @@
                      device(to_hi, core, to_pair * 2 + near, lo, x))
                 )
 
-    barrier = pltpu.get_barrier_semaphore()
-    everyone = [twin] + list(partners.values()) + [other[3] for other in others]
-    for peer in everyone:
-        pl.semaphore_signal(barrier, inc=1, device_id=peer, device_id_type=MESH)
-    pl.semaphore_wait(barrier, len(everyone))
-
-    def send(source, target, send_sem, recv_sem, peer):
-        copy = pltpu.make_async_remote_copy(
-            src_ref=source, dst_ref=target, send_sem=send_sem, recv_sem=recv_sem,
-            device_id=peer, device_id_type=MESH,
-        )
-        copy.start()
-        return copy
-
+    meet([twin] + list(partners.values()) + [other[3] for other in others])
     twin_copies = [
-        send(right_ref.at[1 - core], twin_right, twin_send.at[0], twin_recv.at[0], twin),
-        send(left_ref, twin_left, twin_send.at[1], twin_recv.at[1], twin),
+        send(right_ref.at[1 - core], twin_right, twin_send, twin_recv, 0, twin),
+        send(left_ref, twin_left, twin_send, twin_recv, 1, twin),
     ]
     for copy in twin_copies:
         copy.wait_recv()
@@ -189,7 +192,7 @@
         fill(group, away)
         copies[group, 0] = send(
             work.at[group, pl.ds(away, 8)], got[0].at[group],
-            step_send.at[group, 0], step_recv.at[group, 0], partners[name],
+            step_send, step_recv, (group, 0), partners[name],
         )
     for group in range(4):
         base[group] = bits[order_of(group)[0]] * 8
@@ -203,7 +206,7 @@
             take(group, step - 1, base[group] + away, half, away)
             copies[group, step] = send(
                 work.at[group, pl.ds(base[group] + away, half)], got[step].at[group],
-                step_send.at[group, step], step_recv.at[group, step], partners[name],
+                step_send, step_recv, (group, step), partners[name],
             )
             mine = bits[name] * half
             take(group, step - 1, base[group] + mine, half, mine)
@@ -218,7 +221,7 @@
     for slot, to_hi, to_pair, peer in others:
         ends.append(
             send(
-                last.at[to_pair, to_hi], final.at[slot], final_send.at[slot], final_recv.at[slot], peer
+                last.at[to_pair, to_hi], final.at[slot], final_send, final_recv, slot, peer
             )
         )
     total = last[pair, hi].astype(jnp.float32)
@@ -282,6 +285,250 @@
     start = hi * (part + KEEP_LANES - HALF_LANES)
     kept = lax.dynamic_slice(summed, (0, start), (n_qkv + n_proj, part)).T
     return kept[:, n_qkv:], kept[:, :n_qkv]
+
+
+def near_peers():
+    hi, core, z, lo, x = place()
+    group = lo * 4 + x
+    plane = [(hi * 2 + core, z * 8 + (group + step) % 8) for step in range(1, 8)]
+    line = [(hi * 2 + core, ((z + step) % 8) * 8 + group) for step in range(1, 8)]
+    return plane, line
+
+
+def swap_eights(rows):
+    count = rows.shape[0]
+    at = lax.broadcasted_iota(jnp.int32, (count, count), 0)
+    origin = lax.broadcasted_iota(jnp.int32, (count, count), 1)
+    wanted = (at // 2 % 8) * 16 + at // 16 * 2 + at % 2
+    chosen = jnp.where(origin == wanted, 1.0, 0.0).astype(jnp.bfloat16)
+    moved = jnp.dot(chosen, rows, preferred_element_type=jnp.float32)
+    return moved.astype(jnp.bfloat16)
+
+
+class Exchange:
+    def __init__(self, first, got_first, second, got_second, sends, recvs):
+        self.first, self.got_first = first, got_first
+        self.second, self.got_second = second, got_second
+        self.sends, self.recvs = sends, recvs
+        self.plane, self.line = near_peers()
+        _, _, self.z, lo, x = place()
+        self.group = lo * 4 + x
+
+    def start_plane(self, rows):
+        self.first[...] = swap_eights(rows).reshape(self.first.shape)
+        self.copies = [
+            send(
+                self.first.at[(self.group + step) % 8], self.got_first.at[self.group],
+                self.sends, self.recvs, step, self.plane[step - 1],
+            )
+            for step in range(1, 8)
+        ]
+        self.got_first[self.group] = self.first[self.group]
+
+    def start_line(self):
+        for copy in self.copies:
+            copy.wait_recv()
+        rows = self.got_first[...].reshape(128, -1)
+        self.second[...] = swap_eights(rows).reshape(self.second.shape)
+        more = [
+            send(
+                self.second.at[(self.z + step) % 8], self.got_second.at[self.z],
+                self.sends, self.recvs, 8 + step, self.line[step - 1],
+            )
+            for step in range(1, 8)
+        ]
+        self.got_second[self.z] = self.second[self.z]
+        self.copies = self.copies + more
+        return more
+
+    def finish(self):
+        for copy in self.copies[7:]:
+            copy.wait_recv()
+        for copy in self.copies:
+            copy.wait_send()
+        return self.got_second[...].reshape(128, -1)
+
+
+EXCHANGE_SCRATCH = [pltpu.VMEM((8, 16, 1152), jnp.bfloat16)] * 4 + [
+    pltpu.SemaphoreType.DMA((16,)),
+    pltpu.SemaphoreType.DMA((16,)),
+]
+
+
+class Gather:
+    def __init__(self, own, full, cut, sends, recvs, local):
+        self.own, self.full, self.cut = own, full, cut
+        self.sends, self.recvs = sends, recvs
+        self.hi, self.core, z, lo, self.x = place()
+        hi, core, x = self.hi, self.core, self.x
+        self.mine, self.far = hi * 2 + core, (1 - hi) * 2 + core
+        self.twin = device(hi, 1 - core, z, lo, x)
+        self.across = device(1 - hi, core, z, 1 - lo, x)
+        self.right = device(hi, core, z, lo, (x + 1) % 4)
+        self.left = device(hi, core, z, lo, (x + 3) % 4)
+        self.copies = {}
+        self.local = pltpu.make_async_copy(own, full.at[self.mine], local)
+
+    def go(self, at, source, target, peer):
+        self.copies[at] = send(source, target, self.sends, self.recvs, at, peer)
+
+    def same(self, at, ref, peer):
+        self.go(at, ref, ref, peer)
+
+    def start(self):
+        self.go(0, self.own.at[self.x], self.full.at[self.mine, self.x], self.across)
+        self.go(1, self.own, self.full.at[self.mine], self.twin)
+        self.local.start()
+
+    def spread(self):
+        self.copies[0].wait_recv()
+        piece = self.full.at[self.far, self.x]
+        self.same(2, piece, self.right)
+        self.same(3, piece, self.left)
+        self.same(4, piece, self.twin)
+
+    def pass_on(self):
+        cut, width = self.cut, self.full.shape[3]
+        self.copies[2].wait_recv()
+        from_left = (self.far, (self.x + 3) % 4)
+        self.same(5, self.full.at[from_left + (slice(None), pl.ds(0, cut))], self.right)
+        self.same(6, self.full.at[from_left], self.twin)
+        self.copies[3].wait_recv()
+        from_right = (self.far, (self.x + 1) % 4)
+        self.same(7, self.full.at[from_right + (slice(None), pl.ds(cut, width - cut))], self.left)
+        self.same(8, self.full.at[from_right], self.twin)
+
+    def last(self):
+        self.copies[5].wait_recv()
+        self.copies[7].wait_recv()
+        self.same(9, self.full.at[self.far, (self.x + 2) % 4], self.twin)
+
+    def arrive(self):
+        self.local.wait()
+        for at in (1, 4, 6, 8, 9):
+            self.copies[at].wait_recv()
+
+    def finish(self):
+        for copy in self.copies.values():
+            copy.wait_send()
+
+
+GATHER_SCRATCH = [
+    pltpu.SemaphoreType.DMA((10,)), pltpu.SemaphoreType.DMA((10,)), pltpu.SemaphoreType.DMA
+]
+
+
+def front_kernel(
+    mixed_ref, hidden_ref, proj_ref, qkv_ref, rows_ref, proj_full, qkv_full, *scratch
+):
+    proj = Gather(proj_ref, proj_full, 640, *scratch[:3])
+    qkv = Gather(qkv_ref, qkv_full, 1792, *scratch[3:6])
+    exchange = Exchange(*scratch[6:])
+    meet([proj.twin, proj.across] + exchange.plane + exchange.line)
+    proj.start()
+    qkv.start()
+    proj.spread()
+    proj.pass_on()
+    proj.last()
+    proj.arrive()
+    weight = proj_full[...].reshape(-1, proj_full.shape[3])
+    resid = hidden_ref[...].astype(jnp.float32) + jnp.dot(
+        mixed_ref[...], weight, preferred_element_type=jnp.float32
+    )
+    exchange.start_plane(resid.astype(jnp.bfloat16))
+    qkv.spread()
+    exchange.start_line()
+    qkv.pass_on()
+    qkv.last()
+    rows_ref[...] = exchange.finish()
+    qkv.arrive()
+    proj.finish()
+    qkv.finish()
+
+
+def front(mixed, hidden, proj, qkv):
+    def whole(weight):
+        return jax.ShapeDtypeStruct((4,) + weight.shape, weight.dtype)
+
+    vmem, anywhere = pl.BlockSpec(memory_space=pltpu.VMEM), pl.BlockSpec(memory_space=pl.ANY)
+    return pl.pallas_call(
+        front_kernel,
+        out_shape=(
+            jax.ShapeDtypeStruct(hidden.shape, jnp.bfloat16), whole(proj), whole(qkv)
+        ),
+        in_specs=[vmem, vmem, anywhere, anywhere],
+        out_specs=(vmem, vmem, anywhere),
+        scratch_shapes=GATHER_SCRATCH + GATHER_SCRATCH + EXCHANGE_SCRATCH,
+        compiler_params=pltpu.CompilerParams(
+            collective_id=1, has_side_effects=True, vmem_limit_bytes=24 * 1024 * 1024
+        ),
+    )(mixed, hidden, proj, qkv)
+
+
+def back_kernel(rows_ref, sums_ref, out_ref, total_ref, plane_sums, line_sums, *scratch):
+    sum_sends, sum_recvs = scratch[:2]
+    exchange = Exchange(*scratch[2:])
+    z, group = exchange.z, exchange.group
+    meet(exchange.plane + exchange.line)
+    exchange.start_plane(rows_ref[...])
+    copies = [
+        send(sums_ref, plane_sums.at[group], sum_sends, sum_recvs, step, exchange.plane[step - 1])
+        for step in range(1, 8)
+    ]
+    plane_sums[group] = sums_ref[...]
+    exchange.start_line()
+    for copy in copies:
+        copy.wait_recv()
+    line_sums[z] = jnp.sum(plane_sums[...], axis=0)
+    more = [
+        send(
+            line_sums.at[z], line_sums.at[z], sum_sends, sum_recvs, 8 + step,
+            exchange.line[step - 1],
+        )
+        for step in range(1, 8)
+    ]
+    out_ref[...] = exchange.finish()
+    for copy in more:
+        copy.wait_recv()
+    total_ref[...] = jnp.sum(line_sums[...], axis=0)
+    for copy in copies + more:
+        copy.wait_send()
+
+
+def back(rows, sums):
+    vmem = pl.BlockSpec(memory_space=pltpu.VMEM)
+    return pl.pallas_call(
+        back_kernel,
+        out_shape=(
+            jax.ShapeDtypeStruct(rows.shape, rows.dtype),
+            jax.ShapeDtypeStruct(sums.shape, sums.dtype),
+        ),
+        in_specs=[vmem] * 2,
+        out_specs=(vmem, vmem),
+        scratch_shapes=[
+            pltpu.VMEM((8,) + sums.shape, sums.dtype),
+            pltpu.VMEM((8,) + sums.shape, sums.dtype),
+            pltpu.SemaphoreType.DMA((16,)),
+            pltpu.SemaphoreType.DMA((16,)),
+        ] + EXCHANGE_SCRATCH,
+        compiler_params=pltpu.CompilerParams(
+            collective_id=2, has_side_effects=True, vmem_limit_bytes=16 * 1024 * 1024
+        ),
+    )(rows, sums)
+
+
+def pad_rows(weight):
+    return jnp.pad(weight.reshape(4, -1, weight.shape[1]), ((0, 0), (0, 8), (0, 0)))
+
+
+def pad_columns(rows):
+    count = rows.shape[0]
+    return jnp.pad(rows.reshape(count, 16, -1), ((0, 0), (0, 0), (0, 8))).reshape(count, -1)
+
+
+def cut_columns(rows):
+    count = rows.shape[0]
+    return rows.reshape(count, 16, -1)[:, :, :-8].reshape(count, -1)
 
 
 def body(
@@ -316,24 +563,17 @@
     space_value = value_space.reshape(per_frame)
     space_weights, space_rounded, space_out = attend(space_query, space_key, space_value)
     space_mixed = space_out.astype(jnp.bfloat16).reshape(frames_dev * spot_count, model_width)
-    full_proj = lax.all_gather(proj_space, "dp", axis=0, tiled=True)
-    resid = (
-        hidden.reshape(-1, model_width).astype(jnp.float32)
-        + jnp.dot(space_mixed, full_proj, preferred_element_type=jnp.float32)
-    ).astype(jnp.bfloat16)
-    resid_space = lax.all_to_all(
-        resid.reshape(1, frames_dev, spot_count, model_width),
-        "seq",
-        split_axis=2,
-        concat_axis=1,
-        tiled=True,
-    )
-    resid_wide = resid_space.reshape(token_count, model_width).astype(jnp.float32)
+    resid_space, proj_full, qkv_full = front(
+        pad_columns(space_mixed), hidden.reshape(-1, model_width), pad_rows(proj_space), pad_rows(qkv_time)
+    )
+    proj_full = proj_full.reshape(-1, model_width)
+    qkv_full = qkv_full.reshape(-1, qkv_time.shape[1])
+    resid_wide = resid_space.astype(jnp.float32)
     centered = resid_wide - jnp.mean(resid_wide, axis=-1, keepdims=True)
     inverse = lax.rsqrt(jnp.mean(centered * centered, axis=-1, keepdims=True) + epsilon)
     normed = centered * inverse
     modulated = (normed * (1.0 + scale_time) + shift_time).astype(jnp.bfloat16)
-    projected = add_columns(modulated, lax.all_gather(qkv_time, "dp", axis=0, tiled=True))
+    projected = add_columns(pad_columns(modulated), qkv_full)
 
     def arrange(values):
         return jnp.transpose(values.reshape(frames, spots_dev, head_count, head_size), (1, 0, 2, 3))
@@ -359,16 +599,8 @@
         ],
         axis=-1,
     ).astype(jnp.bfloat16)
-    grad_modulated = place_columns(
-        grad_projected, lax.all_gather(qkv_time, "dp", axis=0, tiled=True)
-    )
-    grad_shift, grad_scale = lax.psum(
-        (
-            jnp.sum(grad_modulated, axis=0, keepdims=True),
-            jnp.sum(grad_modulated * normed, axis=0, keepdims=True),
-        ),
-        "seq",
-    )
+    grad_modulated = cut_columns(place_columns(grad_projected, qkv_full))
+    sums = jnp.stack([jnp.sum(grad_modulated, axis=0), jnp.sum(grad_modulated * normed, axis=0)])
     grad_normed = grad_modulated * (1.0 + scale_time)
     resid_back = (
         (
@@ -378,24 +610,16 @@
         )
         * inverse
     ).astype(jnp.bfloat16)
-    back_frames = lax.all_to_all(
-        resid_back.reshape(1, frames, spots_dev, model_width),
-        "seq",
-        split_axis=1,
-        concat_axis=2,
-        tiled=True,
-    )
-    grad_hidden = (grad_resid.astype(jnp.float32) + back_frames.astype(jnp.float32)).astype(
-        jnp.bfloat16
-    )
+    back_frames, sums = back(resid_back, sums.reshape(8, -1))
+    sums = sums.reshape(2, model_width)
+    grad_shift, grad_scale = sums[:1], sums[1:]
+    grad_hidden = (
+        grad_resid.astype(jnp.float32) + back_frames.reshape(grad_resid.shape).astype(jnp.float32)
+    ).astype(jnp.bfloat16)
     grad_flat = grad_hidden.reshape(-1, model_width)
-    grad_space_out = (
-        lax.dot_general(
-            grad_flat, full_proj, (((1,), (1,)), ((), ())), preferred_element_type=jnp.float32
-        )
-        .astype(jnp.bfloat16)
-        .reshape(per_frame)
-    )
+    grad_space_out = cut_columns(
+        place_columns(grad_flat, proj_full).astype(jnp.bfloat16)
+    ).reshape(per_frame)
     grad_space_query, grad_space_key, grad_space_value = attend_back(
         space_query, space_key, space_value, space_weights, space_rounded, space_out, grad_space_out
     )

time: 407 us -> 227 us (0.56)
  blocking collectives: 134 us -> 0 us
  waiting for transfers between devices: 81.7 us -> 0 us
  Pallas kernels: 88.4 us -> 146 us
  starting transfers between devices: 20.7 us -> 0 us
  between operations: 14.9 us -> 1.5 us
  local copies, waits for them, and re-layouts: 28.2 us -> 37.2 us
    psum x1 -> x0, blocking collectives: 134 us -> none  [body(): lax.psum((jnp.sum(grad_modulated, axis=0, keepdims=True), jnp.sum(grad_mo...]
    pallas_call x0 -> x2, Pallas kernels: none -> 76.5 us  [the longest x1 56.5 us: front(): pl.pallas_call(front_kernel, out_shape=(jax.ShapeDtypeStruct(hidden.shape...]
    all_gather x2 -> x0, waiting for transfers between devices: 71 us -> none  [the longest x1 36.9 us: body(): lax.all_gather(qkv_time, 'dp', axis=0, tiled=True)]
    all_to_all x2 -> x0, starting transfers between devices: 20.6 us -> none  [the longest x1 10.4 us: body(): lax.all_to_all(resid_back.reshape(1, frames, spots_dev, model_width), 'se...]
    pallas_call x1, Pallas kernels: 88.4 us -> 69.8 us  [sum_products(): pl.pallas_call(sum_kernel, out_shape=jax.ShapeDtypeStruct((PIECE_ROWS, KE...]
    all_to_all x2 -> x0, waiting for transfers between devices: 9.29 us -> none  [the longest x1 9.28 us: body(): lax.all_to_all(resid.reshape(1, frames_dev, spot_count, model_width), 'se...]
    unnamed x102 -> x93, local copies, waits for them, and re-layouts: 6.31 us -> 9.16 us
    dot_general x1 -> x2, matrix products: 6.18 us -> 8.14 us  [place_columns(): lax.dot_general(right_side, piece_rows, (((1,), (1,)), ((), ())), preferr...]
  transfers between devices with their start and end apart: 4 -> 0, of which waited for: 3 -> 0; matrix products, arithmetic and copies ran while one was open for 5% -> 0% of each run, Pallas kernels for 0% -> 0%
where the time goes in v2:
time: 227 us; the launch traced here: 226 us
  Pallas kernels  146 us (64%)
  local copies, waits for them, and re-layouts  37.2 us (16%)
  matrix products  26.3 us (12%)
  other arithmetic  14.5 us (6%)
    pallas_call x1, Pallas kernels, sum_products(): pl.pallas_call(sum_kernel, out_shape=jax.ShapeDtypeStruct((PIECE_ROWS, KE...  69.8 us
    pallas_call x1, Pallas kernels, front(): pl.pallas_call(front_kernel, out_shape=(jax.ShapeDtypeStruct(hidden.shape...  56.5 us
    pallas_call x1, Pallas kernels, back(): pl.pallas_call(back_kernel, out_shape=(jax.ShapeDtypeStruct(rows.shape, r...  20 us
    unnamed x93, local copies, waits for them, and re-layouts  9.16 us
    dot_general x2, matrix products, place_columns(): lax.dot_general(right_side, piece_rows, (((1,), (1,)), ((), ())), preferr...  8.14 us
    dot_general x1, matrix products, add_columns(): return jnp.dot(left_side, piece_rows, preferred_element_type=jnp.float32)  4.91 us

profile of v2, /device:TPU:1, one launch (start us, length us, event | category | flops | bytes accessed | tf_op | source)
XLA Modules:
  0.0 225.9 jit_solution(17613828478390280497)
XLA Ops:
  6.7 2.9 %reshape_reshape.8 = bf16[64,2,16,72]{3,2,1,0:T(8,128)(2,1)} reshape(bf16[1,64,2,1152]{3,2,1,0:T(2,128)(2,1)} %param.20) | data formatting | bytes 589824 | tf_op jit(solution)/shard_map/reshape;reshape | solution.py:579
  11.4 1.5 fusion.81
  13.0 2.4 %bitcast_convert_fusion = (bf16[1,128,16,72]{1,3,2,0:T(8,128)(2,1)S(1)}, f32[16,128,72]{1,2,0:T(8,128)}) fusion(bf16[128,16,72]{0,2,1:T(8,128)(2,1)S(1)} %bitcast.172, f32[16,128,128]{1,2,0:T(8,128)} %get-tuple-element.102, f32[16,128]{1,0:T(8,128)S(1)} %get-tuple-element.101), kind=kOutput, calls=%fused_computation.66 | convolution fusion | flops 38420480 | bytes 2236416 | tf_op jit(solution)/shard_map/ghqk,gkhe->gqhe/dot_general | solution.py:50
  15.6 1.7 pad.29.qkv_ref
  17.3 56.5 %shard_map.170 = (bf16[128,1152]{1,0:T(8,128)(2,1)S(1)}, bf16[4,4,80,1152]{3,2,1,0:T(8,128)(2,1)S(1)}, bf16[4,4,80,3456]{3,2,1,0:T(8,128)(2,1)S(1)}) custom-call(bf16[128,1280]{1,0:T(8,128)(2,1)S(1)} %copy.78.mixed_ref, bf16[128,1152]{1,0:T(8,128)(2,1)S(1)} %bitcast.149, bf16[4,80,1152]{2,1,0:T(8,128)(2,1)S(1)} %pad.28.proj_ref, ...), custom_call_target="tpu_custom_call" | custom-call | tf_op jit(solution)/shard_map/pallas_call | solution.py:454
  73.8 3.4 %copy-done = bf16[4,4,80,3456]{3,2,1,0:T(8,128)(2,1)} copy-done((bf16[4,4,80,3456]{3,2,1,0:T(8,128)(2,1)}, bf16[4,4,80,3456]{3,2,1,0:T(8,128)(2,1)S(1)}, u32[]{:S(2)}) %copy-start) | copy-done | bytes 8847384
  77.2 1.6 copy-done.1
  81.0 4.9 %fusion.83 = f32[128,3456]{1,0:T(8,128)S(1)} fusion(bf16[128,1280]{0,1:T(8,128)(2,1)S(1)} %bitcast.158, bf16[1280,3456]{1,0:T(8,128)(2,1)} %bitcast.146), kind=kOutput, calls=%fused_computation.160 | convolution fusion | flops 1132462080 | bytes 10944512 | tf_op jit(solution)/shard_map/dot_general | solution.py:74
  86.0 1.8 convert_element_type.197
  90.8 1.7 subtract_convert_fusion.3
  92.5 2.5 %fusion.82 = (f32[2,16,64]{2,1,0:T(8,128)}, f32[2,16,64,64]{2,3,1,0:T(8,128)}) fusion(bf16[2,64,16,36]{3,1,2,0:T(8,128)(2,1)S(1)} %get-tuple-element.82, bf16[2,64,16,36]{3,1,2,0:T(8,128)(2,1)S(1)} %get-tuple-element.83, bf16[2,64,16,36]{3,1,2,0:T(8,128)(2,1)S(1)} %get-tuple-element.53, bf16[2,64,16,36]{3,1,2,0:T(8,128)(2,1)S(1)} %get-tuple-element.52), kind=kOutput, calls=%fused_computation.159 | convolution fusion | flops 20447296 | bytes 1122304 | tf_op jit(solution)/shard_map/sub | solution.py:47
  95.0 2.0 fusion.19
  98.3 1.2 reshape.562
  103.9 6.4 %fusion.77 = (f32[16,72]{1,0:T(8,128)S(1)}, f32[128]{0:T(128)S(1)}, f32[128,16,72]{0,2,1:T(8,128)}) fusion(f32[16,72]{1,0:T(8,128)S(1)} %copy-done.36, bf16[16,80,3456]{2,1,0:T(8,128)(2,1)} %bitcast.147, bf16[128,3456]{1,0:T(8,128)(2,1)S(1)} %constant_dynamic-update-slice_fusion), kind=kOutput, calls=%fused_computation.154 | convolution fusion | flops 1019656960 | bytes 9446912 | tf_op jit(solution)/shard_map/dot_general | solution.py:78
  110.5 1.3 copy.97
  112.3 2.3 %reshape.570 = bf16[64,54,128]{2,1,0:T(8,128)(2,1)} reshape(bf16[3456,128]{1,0:T(8,128)(2,1)} %copy.97) | data formatting | bytes 1769472 | tf_op jit(solution)/shard_map/reshape | solution.py:269
  114.6 2.1 copy.90
  116.8 1.4 fusion.34
  118.7 1.4 fusion.33.rows_ref
  120.9 20.0 %shard_map.171 = (bf16[128,1152]{1,0:T(8,128)(2,1)S(1)}, f32[8,288]{1,0:T(8,128)S(1)}) custom-call(bf16[128,1152]{1,0:T(8,128)(2,1)S(1)} %fusion.33.rows_ref, f32[8,288]{1,0:T(8,128)S(1)} %reshape.564.sums_ref), custom_call_target="tpu_custom_call" | custom-call | tf_op jit(solution)/shard_map/pallas_call | solution.py:500
  141.9 1.7 convolution_convert_fusion
  144.8 1.2 fusion.37
  147.4 1.7 fusion.17
  154.6 69.8 %shard_map.172 = f32[80,384]{1,0:T(8,128)S(1)} custom-call(bf16[64,80,256]{2,1,0:T(8,128)(2,1)S(1)} %fusion.6.left_ref, bf16[2,256,640]{2,1,0:T(8,128)(2,1)S(1)} %copy-done.3), custom_call_target="tpu_custom_call" | custom-call | tf_op jit(solution)/shard_map/pallas_call | solution.py:239
  (162 shorter events, 31.0 us)
Async XLA Ops:
  0.6 10.3 %copy-start.30 = (bf16[1,1,128,1152]{3,2,1,0:T(8,128)(2,1)S(1)}, bf16[1,1,128,1152]{3,2,1,0:T(8,128)(2,1)}, u32[]{:S(2)}) copy-start(bf16[1,1,128,1152]{3,2,1,0:T(8,128)(2,1)} %param.13) | copy-start | bytes 884740
  1.4 115.3 %copy-start.33 = (f32[1152]{0:T(1024)}, f32[1152]{0:T(1024)S(1)}, u32[]{:S(2)}) copy-start(f32[1152]{0:T(1024)S(1)} %add_reduce_fusion) | copy-start | bytes 13828
  4.6 6.8 %copy-start.28 = (f32[128,18]{0,1:T(8,128)}, f32[128,18]{0,1:T(8,128)S(1)}, u32[]{:S(2)}) copy-start(f32[128,18]{0,1:T(8,128)S(1)} %get-tuple-element.99) | copy-start | bytes 27652
  4.6 6.7 %copy-start.8 = (bf16[288,1152]{1,0:T(8,128)(2,1)S(1)}, bf16[288,1152]{1,0:T(8,128)(2,1)}, u32[]{:S(2)}) copy-start(bf16[288,1152]{1,0:T(8,128)(2,1)} %param.16) | copy-start | bytes 1990660
  6.7 6.3 %copy-start.31 = (bf16[1,1,128,1152]{2,3,1,0:T(8,128)(2,1)}, bf16[1,1,128,1152]{2,3,1,0:T(8,128)(2,1)S(1)}, u32[]{:S(2)}) copy-start(bf16[1,1,128,1152]{2,3,1,0:T(8,128)(2,1)S(1)} %copy.76) | copy-start | bytes 884740
  10.9 2.1 copy-start.12
  10.9 2.0 copy-start.14
  10.9 2.0 copy-start.16
  10.9 2.0 copy-start.18
  11.3 4.1 %copy-start.24 = (bf16[128,16,18]{0,2,1:T(8,128)(2,1)}, bf16[128,16,18]{0,2,1:T(8,128)(2,1)S(1)}, u32[]{:S(2)}) copy-start(bf16[128,16,18]{0,2,1:T(8,128)(2,1)S(1)} %get-tuple-element.78) | copy-start | bytes 221188
  11.3 4.1 %copy-start.26 = (bf16[128,16,18]{0,2,1:T(8,128)(2,1)}, bf16[128,16,18]{0,2,1:T(8,128)(2,1)S(1)}, u32[]{:S(2)}) copy-start(bf16[128,16,18]{0,2,1:T(8,128)(2,1)S(1)} %get-tuple-element.79) | copy-start | bytes 221188
  12.9 4.3 %copy-start.41 = (f32[16,128]{1,0:T(8,128)}, f32[16,128]{1,0:T(8,128)S(1)}, u32[]{:S(2)}) copy-start(f32[16,128]{1,0:T(8,128)S(1)} %get-tuple-element.101) | copy-start | bytes 24580
  73.8 3.4 %copy-start = (bf16[4,4,80,3456]{3,2,1,0:T(8,128)(2,1)}, bf16[4,4,80,3456]{3,2,1,0:T(8,128)(2,1)S(1)}, u32[]{:S(2)}) copy-start(bf16[4,4,80,3456]{3,2,1,0:T(8,128)(2,1)S(1)} %get-tuple-element.14) | copy-start | bytes 26542084
  79.2 37.6 %copy-start.37 = (f32[128]{0:T(128)}, f32[128]{0:T(128)S(1)}, u32[]{:S(2)}) copy-start(f32[128]{0:T(128)S(1)} %add_rsqrt_fusion) | copy-start | bytes 1540
  92.5 2.5 %copy-start.9 = (bf16[64,2,16,72]{3,2,1,0:T(8,128)(2,1)S(1)}, bf16[64,2,16,72]{3,2,1,0:T(8,128)(2,1)}, u32[]{:S(2)}) copy-start(bf16[64,2,16,72]{3,2,1,0:T(8,128)(2,1)} %reshape_reshape.8) | copy-start | bytes 884740
  92.5 2.5 %copy-start.10 = (bf16[64,2,16,72]{3,2,1,0:T(8,128)(2,1)S(1)}, bf16[64,2,16,72]{3,2,1,0:T(8,128)(2,1)}, u32[]{:S(2)}) copy-start(bf16[64,2,16,72]{3,2,1,0:T(8,128)(2,1)} %convert_element_type.197) | copy-start | bytes 884740
  112.3 29.6 %copy-start.2 = (bf16[4,4,80,1152]{3,2,1,0:T(8,128)(2,1)S(1)}, bf16[4,4,80,1152]{3,2,1,0:T(8,128)(2,1)}, u32[]{:S(2)}) copy-start(bf16[4,4,80,1152]{3,2,1,0:T(8,128)(2,1)} %copy-done.1) | copy-start | bytes 8847364
  141.9 12.0 %copy-start.6 = (bf16[1,1,128,1152]{3,2,1,0:T(8,128)(2,1)}, bf16[1,1,128,1152]{3,2,1,0:T(8,128)(2,1)S(1)}, u32[]{:S(2)}) copy-start(bf16[1,1,128,1152]{3,2,1,0:T(8,128)(2,1)S(1)} %fusion.36) | copy-start | bytes 884740
  144.8 4.3 %copy-start.40 = (f32[16,128,128]{1,2,0:T(8,128)S(1)}, f32[16,128,128]{1,2,0:T(8,128)}, u32[]{:S(2)}) copy-start(f32[16,128,128]{1,2,0:T(8,128)} %get-tuple-element.102) | copy-start | bytes 3145732
  144.8 4.3 %copy-start.42 = (f32[16,128]{1,0:T(8,128)S(1)}, f32[16,128]{1,0:T(8,128)}, u32[]{:S(2)}) copy-start(f32[16,128]{1,0:T(8,128)} %copy-done.41) | copy-start | bytes 24580
  149.2 2.3 %copy-start.29 = (f32[128,18]{0,1:T(8,128)S(1)}, f32[128,18]{0,1:T(8,128)}, u32[]{:S(2)}) copy-start(f32[128,18]{0,1:T(8,128)} %copy-done.28) | copy-start | bytes 27652
  149.2 2.3 %copy-start.34 = (f32[128,18]{0,1:T(8,128)S(1)}, f32[128,18]{0,1:T(8,128)}, u32[]{:S(2)}) copy-start(f32[128,18]{0,1:T(8,128)} %get-tuple-element.92) | copy-start | bytes 27652
  149.2 2.3 %copy-start.35 = (f32[128,18]{0,1:T(8,128)S(1)}, f32[128,18]{0,1:T(8,128)}, u32[]{:S(2)}) copy-start(f32[128,18]{0,1:T(8,128)} %get-tuple-element.100) | copy-start | bytes 27652
  151.5 2.7 %copy-start.5 = (bf16[64,54,128]{2,1,0:T(8,128)(2,1)S(1)}, bf16[64,54,128]{2,1,0:T(8,128)(2,1)}, u32[]{:S(2)}) copy-start(bf16[64,54,128]{2,1,0:T(8,128)(2,1)} %reshape.570) | copy-start | bytes 2654212
  (19 other events, 33.0 us)

commit v3 on v2

--- a/solution.py
+++ b/solution.py
@@ -11,74 +11,6 @@
 
 
 epsilon = 1e-06
-
-
-def rotate(values, places, direction):
-    half_width = values.shape[-1] // 2
-    frequency = 10000.0 ** (-jnp.arange(half_width, dtype=jnp.float32) / half_width)
-    angles = places.astype(jnp.float32)[..., None] * frequency
-    cosine = jnp.cos(angles)[..., None, :]
-    sine_part = direction * jnp.sin(angles)[..., None, :]
-    first_half = values[..., :half_width]
-    second = values[..., half_width:]
-    return jnp.concatenate(
-        [first_half * cosine - second * sine_part, second * cosine + first_half * sine_part],
-        axis=-1,
-    )
-
-
-def rotate_space(values, row_places, col_places, direction):
-    half_width = values.shape[-1] // 2
-    return jnp.concatenate(
-        [
-            rotate(values[..., :half_width], row_places, direction),
-            rotate(values[..., half_width:], col_places, direction),
-        ],
-        axis=-1,
-    )
-
-
-def attend(query_rows, key_rows, value_rows):
-    factor = 1.0 / math.sqrt(query_rows.shape[-1])
-    scores = (
-        jnp.einsum("gqhe,gkhe->ghqk", query_rows, key_rows, preferred_element_type=jnp.float32)
-        * factor
-    )
-    exponent = jnp.exp(scores - jnp.max(scores, axis=-1, keepdims=True))
-    weights = exponent / jnp.sum(exponent, axis=-1, keepdims=True)
-    rounded = weights.astype(jnp.bfloat16)
-    output = jnp.einsum("ghqk,gkhe->gqhe", rounded, value_rows, preferred_element_type=jnp.float32)
-    return (weights, rounded, output)
-
-
-def attend_back(query_rows, key_rows, value_rows, weights, rounded, output, grad_rows):
-    factor = 1.0 / math.sqrt(query_rows.shape[-1])
-    row_delta = jnp.einsum("gqhe,gqhe->ghq", grad_rows.astype(jnp.float32), output)
-    grad_value = jnp.einsum(
-        "ghqk,gqhe->gkhe", rounded, grad_rows, preferred_element_type=jnp.float32
-    )
-    grad_weights = jnp.einsum(
-        "gqhe,gkhe->ghqk", grad_rows, value_rows, preferred_element_type=jnp.float32
-    )
-    grad_scores = (weights * (grad_weights - row_delta[..., None]) * factor).astype(jnp.bfloat16)
-    grad_query = jnp.einsum(
-        "ghqk,gkhe->gqhe", grad_scores, key_rows, preferred_element_type=jnp.float32
-    )
-    grad_key = jnp.einsum(
-        "ghqk,gqhe->gkhe", grad_scores, query_rows, preferred_element_type=jnp.float32
-    )
-    return (grad_query, grad_key, grad_value)
-
-
-def add_columns(left_side, piece_rows):
-    return jnp.dot(left_side, piece_rows, preferred_element_type=jnp.float32)
-
-
-def place_columns(right_side, piece_rows):
-    product = lax.dot_general(
-        right_side, piece_rows, (((1,), (1,)), ((), ())), preferred_element_type=jnp.float32
-    )
-    return product
 
 
 MESH = pl.DeviceIdType.MESH
@@ -358,7 +290,7 @@
 class Gather:
     def __init__(self, own, full, cut, sends, recvs, local):
         self.own, self.full, self.cut = own, full, cut
-        self.sends, self.recvs = sends, recvs
+        self.sends, self.recvs, self.local = sends, recvs, local
         self.hi, self.core, z, lo, self.x = place()
         hi, core, x = self.hi, self.core, self.x
         self.mine, self.far = hi * 2 + core, (1 - hi) * 2 + core
@@ -367,7 +299,6 @@
         self.right = device(hi, core, z, lo, (x + 1) % 4)
         self.left = device(hi, core, z, lo, (x + 3) % 4)
         self.copies = {}
-        self.local = pltpu.make_async_copy(own, full.at[self.mine], local)
 
     def go(self, at, source, target, peer):
         self.copies[at] = send(source, target, self.sends, self.recvs, at, peer)
@@ -376,9 +307,15 @@
         self.go(at, ref, ref, peer)
 
     def start(self):
-        self.go(0, self.own.at[self.x], self.full.at[self.mine, self.x], self.across)
-        self.go(1, self.own, self.full.at[self.mine], self.twin)
-        self.local.start()
+        start = pl.multiple_of(self.x * 64 + self.x // 2 * 16, 16)
+        self.go(0, self.own.at[pl.ds(start, 80)], self.full.at[self.mine, self.x], self.across)
+        self.locals = []
+        for quarter, first in enumerate(STARTS):
+            source, target = self.own.at[pl.ds(first, 80)], self.full.at[self.mine, quarter]
+            self.go(10 + quarter, source, target, self.twin)
+            copy = pltpu.make_async_copy(source, target, self.local.at[quarter])
+            copy.start()
+            self.locals.append(copy)
 
     def spread(self):
         self.copies[0].wait_recv()
@@ -404,8 +341,9 @@
         self.same(9, self.full.at[self.far, (self.x + 2) % 4], self.twin)
 
     def arrive(self):
-        self.local.wait()
-        for at in (1, 4, 6, 8, 9):
+        for copy in self.locals:
+            copy.wait()
+        for at in (4, 6, 8, 9, 10, 11, 12, 13):
             self.copies[at].wait_recv()
 
     def finish(self):
@@ -413,13 +351,246 @@
             copy.wait_send()
 
 
+STARTS = (0, 64, 144, 208)
 GATHER_SCRATCH = [
-    pltpu.SemaphoreType.DMA((10,)), pltpu.SemaphoreType.DMA((10,)), pltpu.SemaphoreType.DMA
+    pltpu.SemaphoreType.DMA((14,)), pltpu.SemaphoreType.DMA((14,)), pltpu.SemaphoreType.DMA((4,))
 ]
 
 
+def weight_rows(full, columns):
+    return jnp.concatenate(
+        [
+            full[block, quarter, 16 * (quarter % 2) : 80, columns]
+            for block in range(4)
+            for quarter in range(4)
+        ],
+        axis=0,
+    )
+
+
+WIDTH = 1152
+HEAD = WIDTH // HEADS
+FACTOR = 1.0 / math.sqrt(HEAD)
+
+
+def across_rows(left, right):
+    return lax.dot_general(
+        left, right, (((1,), (1,)), ((), ())), preferred_element_type=jnp.float32
+    )
+
+
+def down_rows(left, right):
+    return lax.dot_general(
+        left, right, (((0,), (0,)), ((), ())), preferred_element_type=jnp.float32
+    )
+
+
+def turn_tables(angles, half):
+    lane = lax.broadcasted_iota(jnp.int32, (1, WIDTH), 1) % HEAD
+    first = lane % (2 * half) < half
+    origin = lane // (2 * half) * half + lane % half
+    row = lax.broadcasted_iota(jnp.int32, (128, WIDTH), 0)
+    cosine_at = jnp.where(row == origin, 1.0, 0.0).astype(jnp.bfloat16)
+    sine_at = jnp.where(row == origin + 36, 1.0, 0.0) * jnp.where(first, -1.0, 1.0)
+    sine_at = sine_at.astype(jnp.bfloat16)
+    cosine = jnp.zeros((128, WIDTH), jnp.float32)
+    sine = jnp.zeros((128, WIDTH), jnp.float32)
+    rest = angles
+    for _ in range(3):
+        part = rest.astype(jnp.bfloat16)
+        rest = rest - part.astype(jnp.float32)
+        cosine += jnp.dot(part, cosine_at, preferred_element_type=jnp.float32)
+        sine += jnp.dot(part, sine_at, preferred_element_type=jnp.float32)
+    return cosine, sine
+
+
+def turn(values, cosine, sine, half, direction):
+    lane = lax.broadcasted_iota(jnp.int32, (1, WIDTH), 1) % (2 * half)
+    partner = jnp.where(
+        lane < half, pltpu.roll(values, WIDTH - half, 1), pltpu.roll(values, half, 1)
+    )
+    return values * cosine + partner * (sine * direction)
+
+
+def head_window(head):
+    start = min(head * HEAD // 128 * 128, WIDTH - 256)
+    lane = lax.broadcasted_iota(jnp.int32, (1, 256), 1) + start
+    mask = jnp.where((lane >= head * HEAD) & (lane < (head + 1) * HEAD), 1.0, 0.0)
+    return slice(start, start + 256), mask.astype(jnp.bfloat16)
+
+
+def softmax_rows(scores):
+    exponent = jnp.exp(scores - jnp.max(scores, axis=-1, keepdims=True))
+    return exponent / jnp.sum(exponent, axis=-1, keepdims=True)
+
+
+def head_back(weights, query, key, value, grad, mask):
+    grad = grad * mask
+    rounded = weights.astype(jnp.bfloat16)
+    grad_weights = across_rows(grad, value)
+    delta = jnp.sum(rounded.astype(jnp.float32) * grad_weights, axis=-1, keepdims=True)
+    scores = (weights * (grad_weights - delta) * FACTOR).astype(jnp.bfloat16)
+    return (
+        jnp.dot(scores, key * mask, preferred_element_type=jnp.float32),
+        down_rows(scores, query * mask),
+        down_rows(rounded, grad),
+    )
+
+
+def space_forward(query_ref, key_ref, value_ref, angles_ref, turned_query, turned_key, weights_ref, mixed):
+    cosine, sine = turn_tables(angles_ref[...], HEAD // 4)
+    for source, target in ((query_ref, turned_query), (key_ref, turned_key)):
+        values = source[...].astype(jnp.float32)
+        target[...] = turn(values, cosine, sine, HEAD // 4, 1.0).astype(jnp.bfloat16)
+    mixed[...] = jnp.zeros_like(mixed)
+    for head in range(HEADS):
+        window, mask = head_window(head)
+        scores = across_rows(turned_query[:, window] * mask, turned_key[:, window]) * FACTOR
+        weights = softmax_rows(scores)
+        weights_ref[head] = weights
+        mixed[:, window] += jnp.dot(
+            weights.astype(jnp.bfloat16), value_ref[:, window] * mask,
+            preferred_element_type=jnp.float32,
+        )
+
+
+def space_back_kernel(
+    back_ref, resid_ref, proj_full, query_ref, key_ref, value_ref, weights_ref, angles_ref,
+    hidden_out, query_out, key_out, value_out, total_query, total_key, total_value, grad,
+):
+    hidden = resid_ref[...].astype(jnp.float32) + back_ref[...].astype(jnp.float32)
+    hidden = hidden.astype(jnp.bfloat16)
+    hidden_out[...] = hidden
+    for block in range(3):
+        columns = slice(block * 384, block * 384 + 384)
+        part = across_rows(hidden[:, columns], weight_rows(proj_full, columns))
+        if block == 0:
+            total_query[...] = part
+        else:
+            total_query[...] += part
+    grad[...] = total_query[...].astype(jnp.bfloat16)
+    totals = (total_query, total_key, total_value)
+    for total in totals:
+        total[...] = jnp.zeros_like(total)
+    for head in range(HEADS):
+        window, mask = head_window(head)
+        parts = head_back(
+            weights_ref[head], query_ref[:, window], key_ref[:, window], value_ref[:, window],
+            grad[:, window], mask,
+        )
+        for total, part in zip(totals, parts):
+            total[:, window] += part
+    cosine, sine = turn_tables(angles_ref[...], HEAD // 4)
+    for total, out in ((total_query, query_out), (total_key, key_out)):
+        out[...] = turn(total[...], cosine, sine, HEAD // 4, -1.0).astype(jnp.bfloat16)
+    value_out[...] = total_value[...].astype(jnp.bfloat16)
+
+
+def local_call(kernel, outs, scratch, megabytes, *args):
+    return pl.pallas_call(
+        kernel,
+        out_shape=tuple(jax.ShapeDtypeStruct(shape, kind) for shape, kind in outs),
+        in_specs=[pl.BlockSpec(memory_space=pltpu.VMEM)] * len(args),
+        out_specs=tuple(pl.BlockSpec(memory_space=pltpu.VMEM) for _ in outs),
+        scratch_shapes=[pltpu.VMEM(shape, kind) for shape, kind in scratch],
+        compiler_params=pltpu.CompilerParams(vmem_limit_bytes=megabytes * 1024 * 1024),
+    )(*args)
+
+
+ROWS = ((128, WIDTH), jnp.bfloat16)
+WIDE_ROWS = ((128, WIDTH), jnp.float32)
+
+
+def space_back(*args):
+    return local_call(
+        space_back_kernel, [ROWS] * 4, [WIDE_ROWS] * 3 + [ROWS], 24, *args
+    )
+
+
+def time_kernel(
+    rows_ref, qkv_full, scale_ref, shift_ref, grad_ref, angles_ref,
+    modulated_ref, projected_ref, back_ref, sums_ref,
+    normed_ref, wide, turned, total_back,
+):
+    rows = rows_ref[...].astype(jnp.float32)
+    centered = rows - jnp.mean(rows, axis=-1, keepdims=True)
+    inverse = lax.rsqrt(jnp.mean(centered * centered, axis=-1, keepdims=True) + epsilon)
+    normed = centered * inverse
+    normed_ref[...] = normed
+    scale = 1.0 + scale_ref[...]
+    modulated_ref[...] = (normed * scale + shift_ref[...]).astype(jnp.bfloat16)
+    for block in range(9):
+        columns = slice(block * 384, block * 384 + 384)
+        wide[:, columns] = jnp.dot(
+            modulated_ref[...], weight_rows(qkv_full, columns), preferred_element_type=jnp.float32
+        )
+    cosine, sine = turn_tables(angles_ref[...], HEAD // 2)
+    for block in range(2):
+        columns = slice(block * WIDTH, block * WIDTH + WIDTH)
+        turned[:, columns] = turn(wide[:, columns], cosine, sine, HEAD // 2, 1.0).astype(jnp.bfloat16)
+    turned[:, 2 * WIDTH :] = wide[:, 2 * WIDTH :].astype(jnp.bfloat16)
+    wide[...] = jnp.zeros_like(wide)
+    spot_row = lax.broadcasted_iota(jnp.int32, (128, 128), 0) % 2
+    spot_column = lax.broadcasted_iota(jnp.int32, (128, 128), 1) % 2
+    together = spot_row == spot_column
+    for head in range(HEADS):
+        window, mask = head_window(head)
+        windows = [slice(window.start + WIDTH * j, window.stop + WIDTH * j) for j in range(3)]
+        query, key, value = [turned[:, columns] for columns in windows]
+        scores = across_rows(query * mask, key) * FACTOR
+        weights = softmax_rows(jnp.where(together, scores, -jnp.inf))
+        parts = head_back(weights, query, key, value, grad_ref[:, window], mask)
+        for columns, part in zip(windows, parts):
+            wide[:, columns] += part
+    for block in range(2):
+        columns = slice(block * WIDTH, block * WIDTH + WIDTH)
+        projected_ref[:, columns] = turn(wide[:, columns], cosine, sine, HEAD // 2, -1.0).astype(
+            jnp.bfloat16
+        )
+    projected_ref[:, 2 * WIDTH :] = wide[:, 2 * WIDTH :].astype(jnp.bfloat16)
+    for block in range(9):
+        columns = slice(block * 384, block * 384 + 384)
+        part = across_rows(projected_ref[:, columns], weight_rows(qkv_full, columns))
+        if block == 0:
+            total_back[...] = part
+        else:
+            total_back[...] += part
+    grad = total_back[...]
+    normed = normed_ref[...]
+    sums_ref[...] = jnp.concatenate(
+        [
+            jnp.sum(grad, axis=0, keepdims=True),
+            jnp.sum(grad * normed, axis=0, keepdims=True),
+            jnp.zeros((6, WIDTH), jnp.float32),
+        ],
+        axis=0,
+    )
+    grad = grad * scale
+    back_ref[...] = (
+        (
+            grad
+            - jnp.mean(grad, axis=-1, keepdims=True)
+            - normed * jnp.mean(grad * normed, axis=-1, keepdims=True)
+        )
+        * inverse
+    ).astype(jnp.bfloat16)
+
+
+def time_sublayer(*args):
+    wide = (128, 3 * WIDTH)
+    return local_call(
+        time_kernel,
+        [ROWS, (wide, jnp.bfloat16), ROWS, ((8, WIDTH), jnp.float32)],
+        [WIDE_ROWS, (wide, jnp.float32), (wide, jnp.bfloat16), WIDE_ROWS],
+        40,
+        *args,
+    )
+
+
 def front_kernel(
-    mixed_ref, hidden_ref, proj_ref, qkv_ref, rows_ref, proj_full, qkv_full, *scratch
+    query_ref, key_ref, value_ref, hidden_ref, angles_ref, proj_ref, qkv_ref,
+    rows_ref, mixed_ref, turned_query, turned_key, weights_ref, proj_full, qkv_full,
+    wide, *scratch,
 ):
     proj = Gather(proj_ref, proj_full, 640, *scratch[:3])
     qkv = Gather(qkv_ref, qkv_full, 1792, *scratch[3:6])
@@ -428,14 +599,19 @@
     proj.start()
     qkv.start()
     proj.spread()
+    space_forward(
+        query_ref, key_ref, value_ref, angles_ref, turned_query, turned_key, weights_ref, wide
+    )
+    mixed_ref[...] = wide[...].astype(jnp.bfloat16)
     proj.pass_on()
     proj.last()
     proj.arrive()
-    weight = proj_full[...].reshape(-1, proj_full.shape[3])
-    resid = hidden_ref[...].astype(jnp.float32) + jnp.dot(
-        mixed_ref[...], weight, preferred_element_type=jnp.float32
-    )
-    exchange.start_plane(resid.astype(jnp.bfloat16))
+    for block in range(3):
+        columns = slice(block * 384, block * 384 + 384)
+        wide[:, columns] = hidden_ref[:, columns].astype(jnp.float32) + jnp.dot(
+            mixed_ref[...], weight_rows(proj_full, columns), preferred_element_type=jnp.float32
+        )
+    exchange.start_plane(wide[...].astype(jnp.bfloat16))
     qkv.spread()
     exchange.start_line()
     qkv.pass_on()
@@ -446,23 +622,25 @@
     qkv.finish()
 
 
-def front(mixed, hidden, proj, qkv):
+def front(query, key, value, hidden, angles, proj, qkv):
     def whole(weight):
-        return jax.ShapeDtypeStruct((4,) + weight.shape, weight.dtype)
+        return jax.ShapeDtypeStruct((4, 4, 80, weight.shape[1]), weight.dtype)
 
     vmem, anywhere = pl.BlockSpec(memory_space=pltpu.VMEM), pl.BlockSpec(memory_space=pl.ANY)
+    rows = jax.ShapeDtypeStruct(*ROWS)
     return pl.pallas_call(
         front_kernel,
         out_shape=(
-            jax.ShapeDtypeStruct(hidden.shape, jnp.bfloat16), whole(proj), whole(qkv)
+            rows, rows, rows, rows, jax.ShapeDtypeStruct((HEADS, 128, 128), jnp.float32),
+            whole(proj), whole(qkv),
         ),
-        in_specs=[vmem, vmem, anywhere, anywhere],
-        out_specs=(vmem, vmem, anywhere),
-        scratch_shapes=GATHER_SCRATCH + GATHER_SCRATCH + EXCHANGE_SCRATCH,
+        in_specs=[vmem] * 5 + [anywhere] * 2,
+        out_specs=(vmem,) * 7,
+        scratch_shapes=[pltpu.VMEM(*WIDE_ROWS)] + GATHER_SCRATCH * 2 + EXCHANGE_SCRATCH,
         compiler_params=pltpu.CompilerParams(
-            collective_id=1, has_side_effects=True, vmem_limit_bytes=24 * 1024 * 1024
+            collective_id=1, has_side_effects=True, vmem_limit_bytes=32 * 1024 * 1024
         ),
-    )(mixed, hidden, proj, qkv)
+    )(query, key, value, hidden, angles, proj, qkv)
 
 
 def back_kernel(rows_ref, sums_ref, out_ref, total_ref, plane_sums, line_sums, *scratch):
@@ -517,18 +695,10 @@
     )(rows, sums)
 
 
-def pad_rows(weight):
-    return jnp.pad(weight.reshape(4, -1, weight.shape[1]), ((0, 0), (0, 8), (0, 0)))
-
-
-def pad_columns(rows):
-    count = rows.shape[0]
-    return jnp.pad(rows.reshape(count, 16, -1), ((0, 0), (0, 0), (0, 8))).reshape(count, -1)
-
-
-def cut_columns(rows):
-    count = rows.shape[0]
-    return rows.reshape(count, 16, -1)[:, :, :-8].reshape(count, -1)
+def turn_angles(places, half):
+    frequency = 10000.0 ** (-jnp.arange(half, dtype=jnp.float32) / half)
+    angles = (places.astype(jnp.float32)[:, :, None] * frequency).reshape(128, 36)
+    return jnp.pad(jnp.concatenate([jnp.cos(angles), jnp.sin(angles)], axis=1), ((0, 0), (0, 56)))
 
 
 def body(
@@ -544,109 +714,41 @@
     grad_attn_time,
     grad_resid,
 ):
-    frames_dev, spot_count, model_width = (hidden.shape[1], hidden.shape[2], hidden.shape[3])
-    frames, spots_dev = (grad_attn_time.shape[1], grad_attn_time.shape[2])
-    head_count = HEADS
-    head_size = model_width // head_count
-    token_count = frames * spots_dev
     seq_place = lax.axis_index("seq")
-    row_places = lax.dynamic_slice_in_dim(positions[1, 0], seq_place * frames_dev, frames_dev, 0)
-    col_places = lax.dynamic_slice_in_dim(positions[2, 0], seq_place * frames_dev, frames_dev, 0)
-    frame_places = lax.dynamic_slice_in_dim(positions[0, 0], seq_place * spots_dev, spots_dev, 1).T
-    per_frame = (frames_dev, spot_count, head_count, head_size)
-    space_query = rotate_space(
-        query_space.reshape(per_frame).astype(jnp.float32), row_places, col_places, 1.0
-    ).astype(jnp.bfloat16)
-    space_key = rotate_space(
-        key_space.reshape(per_frame).astype(jnp.float32), row_places, col_places, 1.0
-    ).astype(jnp.bfloat16)
-    space_value = value_space.reshape(per_frame)
-    space_weights, space_rounded, space_out = attend(space_query, space_key, space_value)
-    space_mixed = space_out.astype(jnp.bfloat16).reshape(frames_dev * spot_count, model_width)
-    resid_space, proj_full, qkv_full = front(
-        pad_columns(space_mixed), hidden.reshape(-1, model_width), pad_rows(proj_space), pad_rows(qkv_time)
-    )
-    proj_full = proj_full.reshape(-1, model_width)
-    qkv_full = qkv_full.reshape(-1, qkv_time.shape[1])
-    resid_wide = resid_space.astype(jnp.float32)
-    centered = resid_wide - jnp.mean(resid_wide, axis=-1, keepdims=True)
-    inverse = lax.rsqrt(jnp.mean(centered * centered, axis=-1, keepdims=True) + epsilon)
-    normed = centered * inverse
-    modulated = (normed * (1.0 + scale_time) + shift_time).astype(jnp.bfloat16)
-    projected = add_columns(pad_columns(modulated), qkv_full)
-
-    def arrange(values):
-        return jnp.transpose(values.reshape(frames, spots_dev, head_count, head_size), (1, 0, 2, 3))
-
-    def restore(values):
-        return jnp.transpose(values, (1, 0, 2, 3)).reshape(token_count, model_width)
-
-    time_query = rotate(arrange(projected[:, :model_width]), frame_places, 1.0).astype(jnp.bfloat16)
-    time_key = rotate(
-        arrange(projected[:, model_width : 2 * model_width]), frame_places, 1.0
-    ).astype(jnp.bfloat16)
-    time_value = arrange(projected[:, 2 * model_width :]).astype(jnp.bfloat16)
-    time_weights, time_rounded, time_out = attend(time_query, time_key, time_value)
-    grad_time = arrange(grad_attn_time.reshape(token_count, model_width))
-    grad_time_query, grad_time_key, grad_time_value = attend_back(
-        time_query, time_key, time_value, time_weights, time_rounded, time_out, grad_time
-    )
-    grad_projected = jnp.concatenate(
-        [
-            restore(rotate(grad_time_query, frame_places, -1.0)),
-            restore(rotate(grad_time_key, frame_places, -1.0)),
-            restore(grad_time_value),
-        ],
-        axis=-1,
-    ).astype(jnp.bfloat16)
-    grad_modulated = cut_columns(place_columns(grad_projected, qkv_full))
-    sums = jnp.stack([jnp.sum(grad_modulated, axis=0), jnp.sum(grad_modulated * normed, axis=0)])
-    grad_normed = grad_modulated * (1.0 + scale_time)
-    resid_back = (
-        (
-            grad_normed
-            - jnp.mean(grad_normed, axis=-1, keepdims=True)
-            - normed * jnp.mean(grad_normed * normed, axis=-1, keepdims=True)
-        )
-        * inverse
-    ).astype(jnp.bfloat16)
-    back_frames, sums = back(resid_back, sums.reshape(8, -1))
-    sums = sums.reshape(2, model_width)
-    grad_shift, grad_scale = sums[:1], sums[1:]
-    grad_hidden = (
-        grad_resid.astype(jnp.float32) + back_frames.reshape(grad_resid.shape).astype(jnp.float32)
-    ).astype(jnp.bfloat16)
-    grad_flat = grad_hidden.reshape(-1, model_width)
-    grad_space_out = cut_columns(
-        place_columns(grad_flat, proj_full).astype(jnp.bfloat16)
-    ).reshape(per_frame)
-    grad_space_query, grad_space_key, grad_space_value = attend_back(
-        space_query, space_key, space_value, space_weights, space_rounded, space_out, grad_space_out
-    )
-    full_shape = hidden.shape
-    grad_query = (
-        rotate_space(grad_space_query, row_places, col_places, -1.0)
-        .astype(jnp.bfloat16)
-        .reshape(full_shape)
-    )
-    grad_key = (
-        rotate_space(grad_space_key, row_places, col_places, -1.0)
-        .astype(jnp.bfloat16)
-        .reshape(full_shape)
-    )
-    grad_value = grad_space_value.astype(jnp.bfloat16).reshape(full_shape)
+    frame_places = lax.dynamic_slice_in_dim(positions[0, 0], seq_place * 2, 2, 1).reshape(128, 1)
+    spot_places = lax.dynamic_slice_in_dim(positions[1:, 0], seq_place, 1, 1).reshape(2, 128).T
+    space_angles = turn_angles(spot_places, HEAD // 4)
+    time_angles = turn_angles(frame_places, HEAD // 2)
+
+    def flat(values):
+        return values.reshape(128, WIDTH)
+
+    rows, space_mixed, space_query, space_key, space_weights, proj_full, qkv_full = front(
+        flat(query_space), flat(key_space), flat(value_space), flat(hidden), space_angles,
+        proj_space, qkv_time,
+    )
+    modulated, grad_projected, resid_back, sums = time_sublayer(
+        rows, qkv_full, scale_time, shift_time, flat(grad_attn_time), time_angles
+    )
+    back_frames, sums = back(resid_back, sums[:2].reshape(8, -1))
+    sums = sums.reshape(2, WIDTH)
+    grad_hidden, grad_query, grad_key, grad_value = space_back(
+        back_frames, flat(grad_resid), proj_full, space_query, space_key, flat(value_space),
+        space_weights, space_angles,
+    )
     grad_proj_space, grad_qkv_time = weight_gradients(
-        grad_projected, modulated, grad_flat, space_mixed
-    )
+        grad_projected, modulated, grad_hidden, space_mixed
+    )
+    shape = hidden.shape
     return (
-        grad_hidden,
-        grad_query,
-        grad_key,
-        grad_value,
+        grad_hidden.reshape(shape),
+        grad_query.reshape(shape),
+        grad_key.reshape(shape),
+        grad_value.reshape(shape),
         grad_proj_space,
         grad_qkv_time,
-        grad_shift,
-        grad_scale,
+        sums[:1],
+        sums[1:],
     )
 
 

time: 227 us -> 199 us (0.88)
  matrix products: 26.3 us -> 0 us
  Pallas kernels: 146 us -> 166 us
  other arithmetic: 14.5 us -> 3.85 us
  local copies, waits for them, and re-layouts: 37.2 us -> 27.1 us
    dot_general x13 -> x0, matrix products: 22.3 us -> none  [the longest x2 8.14 us: place_columns(): lax.dot_general(right_side, piece_rows, (((1,), (1,)), ((), ())), preferr...]
    pallas_call x1 -> x3, Pallas kernels: 56.5 us -> 76.7 us  [the longest x1 56.5 us: front(): pl.pallas_call(front_kernel, out_shape=(rows, rows, rows, rows, jax.Shape...]
    unnamed x93 -> x52, local copies, waits for them, and re-layouts: 9.16 us -> 17.4 us
    reshape x10 -> x2, local copies, waits for them, and re-layouts: 8.32 us -> 1.16 us  [the longest x1 1.07 us: flat(): return values.reshape(128, WIDTH)]
    convert_element_type x5 -> x1, local copies, waits for them, and re-layouts: 4.45 us -> 0.14 us  [turn_angles(): places.astype(jnp.float32)[:, :, None] * frequency]
    sub x2 -> x0, matrix products: 4.01 us -> none  [attend(): exponent = jnp.exp(scores - jnp.max(scores, axis=-1, keepdims=True))]
    another operation x5 -> x0, other arithmetic: 3.54 us -> none
    another operation x3 -> x0, local copies, waits for them, and re-layouts: 2.96 us -> none  [the longest x1 2.87 us: arrange(): values.reshape(frames, spots_dev, head_count, head_size)]
where the time goes in v3:
time: 199 us; the launch traced here: 198 us
  Pallas kernels  166 us (83%)
  local copies, waits for them, and re-layouts  27.1 us (14%)
  other arithmetic  3.85 us (2%)
    pallas_call x1, Pallas kernels, sum_products(): pl.pallas_call(sum_kernel, out_shape=jax.ShapeDtypeStruct((PIECE_ROWS, KE...  71.6 us
    pallas_call x1, Pallas kernels, front(): pl.pallas_call(front_kernel, out_shape=(rows, rows, rows, rows, jax.Shape...  56.5 us
    pallas_call x2, Pallas kernels, local_call(): pl.pallas_call(kernel, out_shape=tuple((jax.ShapeDtypeStruct(shape, kind)...  20.2 us
    pallas_call x1, Pallas kernels, back(): pl.pallas_call(back_kernel, out_shape=(jax.ShapeDtypeStruct(rows.shape, r...  18 us
    unnamed x52, local copies, waits for them, and re-layouts  17.4 us

profile of v3, /device:TPU:1, one launch (start us, length us, event | category | flops | bytes accessed | tf_op | source)
XLA Modules:
  0.0 198.2 jit_solution(10548859884196839044)
XLA Ops:
  1.8 0.8 slice.27
  4.1 1.1 reshape.119.grad_ref
  5.2 1.5 copy-done
  6.8 1.0 copy-done.1
  7.7 1.1 copy-done.7
  8.8 1.0 copy-done.15
  9.8 1.0 copy-done.16
  10.8 1.0 copy-done.17
  11.7 56.5 %shard_map.170 = (bf16[128,1152]{1,0:T(8,128)(2,1)S(1)}, bf16[128,1152]{1,0:T(8,128)(2,1)S(1)}, bf16[128,1152]{1,0:T(8,128)(2,1)S(1)}, bf16[128,1152]{1,0:T(8,12...) custom-call(bf16[128,1152]{1,0:T(8,128)(2,1)S(1)} %bitcast.27, ...), custom_call_target="tpu_custom_call" | custom-call | tf_op jit(solution)/shard_map/pallas_call | solution.py:631
  70.4 13.0 %shard_map.171 = (bf16[128,1152]{1,0:T(8,128)(2,1)S(1)}, bf16[128,3456]{1,0:T(8,128)(2,1)S(1)}, bf16[128,1152]{1,0:T(8,128)(2,1)S(1)}, f32[8,1152]{1,0:T(8,128)S(1)}) custom-call(bf16[128,1152]{1,0:T(8,128)(2,1)S(1)} %get-tuple-element.25.rows_ref, bf16[4,4,80,3456]{3,2,1,0:T(8,128)(2,1)S(1)} %get-tuple-element.26.qkv_full, f32[1,1152]{1,0:T(1,128)S(1)} %copy-done.24, ...), custom_call_target="tpu_custom_call" | custom-call | tf_op jit(solution)/shard_map/pallas_call | solution.py:490
  83.4 0.9 copy-done.5
  85.9 1.0 copy-done.11
  86.8 18.0 %shard_map.172 = (bf16[128,1152]{1,0:T(8,128)(2,1)S(1)}, f32[8,288]{1,0:T(8,128)S(1)}) custom-call(bf16[128,1152]{1,0:T(8,128)(2,1)S(1)} %copy-done.11, f32[8,288]{1,0:T(8,128)S(1)} %reshape.120.sums_ref), custom_call_target="tpu_custom_call" | custom-call | tf_op jit(solution)/shard_map/pallas_call | solution.py:678
  104.9 1.2 copy-done.4
  107.0 1.0 copy-done.18
  107.9 1.0 copy-done.20
  108.9 1.0 copy-done.22
  109.8 7.2 %shard_map.173 = (bf16[128,1152]{1,0:T(8,128)(2,1)}, bf16[128,1152]{1,0:T(8,128)(2,1)}, bf16[128,1152]{1,0:T(8,128)(2,1)}, bf16[128,1152]{1,0:T(8,128)(2,1)}) custom-call(bf16[128,1152]{1,0:T(8,128)(2,1)S(1)} %get-tuple-element.29.back_ref, bf16[128,1152]{1,0:T(8,128)(2,1)S(1)} %bitcast.30, bf16[4,4,80,1152]{3,2,1,0:T(8,128)(2,1)S(1)} %get-tuple-element.30.proj_full, ...), custom_call_target="tpu_custom_call" | custom-call | tf_op jit(solution)/shard_map/pallas_call | solution.py:490
  118.4 1.2 copy.33
  119.6 0.9 reshape.127
  120.4 1.0 pad_maximum_fusion
  122.6 1.0 copy.32
  123.8 1.4 fusion.2.left_ref
  125.2 71.6 %shard_map.174 = f32[80,384]{1,0:T(8,128)S(1)} custom-call(bf16[64,80,256]{2,1,0:T(8,128)(2,1)S(1)} %fusion.2.left_ref, bf16[2,256,640]{2,1,0:T(8,128)(2,1)S(1)} %pad.23.right_ref), custom_call_target="tpu_custom_call" | custom-call | tf_op jit(solution)/shard_map/pallas_call | solution.py:171
  (68 shorter events, 11.2 us)
Async XLA Ops:
  2.7 67.6 %copy-start.24 = (f32[1,1152]{1,0:T(1,128)S(1)}, f32[1,1152]{1,0:T(1,128)}, u32[]{:S(2)}) copy-start(f32[1,1152]{1,0:T(1,128)} %scale_ref.1) | copy-start | bytes 13828
  2.8 67.6 %copy-start.25 = (f32[1,1152]{1,0:T(1,128)S(1)}, f32[1,1152]{1,0:T(1,128)}, u32[]{:S(2)}) copy-start(f32[1,1152]{1,0:T(1,128)} %shift_ref.1) | copy-start | bytes 13828
  3.1 67.2 %copy-start.8 = (f32[128,128]{1,0:T(8,128)}, f32[128,128]{1,0:T(8,128)S(1)}, u32[]{:S(2)}) copy-start(f32[128,128]{1,0:T(8,128)S(1)} %select_maximum_fusion.1.angles_ref) | copy-start | bytes 196612
  5.2 1.6 copy-start
  6.8 1.0 copy-start.1
  7.7 1.1 copy-start.7
  8.8 1.0 copy-start.15
  9.8 1.0 copy-start.16
  10.8 1.0 copy-start.17
  11.7 58.6 %copy-start.23 = (f32[128,128]{1,0:T(8,128)S(1)}, f32[128,128]{1,0:T(8,128)}, u32[]{:S(2)}) copy-start(f32[128,128]{1,0:T(8,128)} %select_maximum_fusion.angles_ref) | copy-start | bytes 196612
  69.6 0.7 copy-start.21
  70.3 13.1 %copy-start.3 = (f32[16,128,128]{2,1,0:T(8,128)}, f32[16,128,128]{2,1,0:T(8,128)S(1)}, u32[]{:S(2)}) copy-start(f32[16,128,128]{2,1,0:T(8,128)S(1)} %get-tuple-element.33.weights_ref) | copy-start | bytes 3145732
  70.4 34.5 %copy-start.2 = (bf16[1,1,128,1152]{3,2,1,0:T(8,128)(2,1)S(1)}, bf16[1,1,128,1152]{3,2,1,0:T(8,128)(2,1)}, u32[]{:S(2)}) copy-start(bf16[1,1,128,1152]{3,2,1,0:T(8,128)(2,1)} %param.14) | copy-start | bytes 884740
  83.4 0.9 copy-start.5
  84.3 0.7 copy-start.10
  85.1 0.7 copy-start.14
  85.9 1.0 copy-start.11
  104.9 1.2 copy-start.4
  106.1 0.8 copy-start.9
  107.0 1.0 copy-start.18
  107.9 1.0 copy-start.20
  108.9 1.0 copy-start.22
  109.8 10.6 %copy-start.13 = (bf16[128,1152]{1,0:T(8,128)(2,1)S(1)}, bf16[128,1152]{1,0:T(8,128)(2,1)}, u32[]{:S(2)}) copy-start(bf16[128,1152]{1,0:T(8,128)(2,1)} %copy-done.12) | copy-start | bytes 884740
  121.5 1.2 copy-start.6
  (2 other events, 1.4 us)

commit v4 on v3

--- a/solution.py
+++ b/solution.py
@@ -15,10 +15,14 @@
 
 MESH = pl.DeviceIdType.MESH
 
-PIECE_ROWS = 80
 HALF_LANES = 640
 KEEP_LANES = 384
 ORDER = ("x_near", "y_near", "x_far", "z_near")
+GROUPS = (
+    (0, 0, 64, 0), (0, 64, 128, 1), (0, 128, 176, 2), (0, 176, 224, 3), (1, 0, 48, 2), (1, 48, 80, 3)
+)
+QKV_ROWS, PROJ_ROWS = 224, 80
+QKV_WINDOW, PROJ_WINDOW = 80, 32
 
 
 def place():
@@ -49,174 +53,93 @@
 
 
 def order_of(group):
-    return [ORDER[(group + step) % 4] for step in range(4)]
-
-
-def piece_of(group, block):
+    return [ORDER[(GROUPS[group][3] + step) % 4] for step in range(4)]
+
+
+def combination(group, block):
     bits = {name: (block // (8 >> step)) % 2 for step, name in enumerate(order_of(group))}
     x = bits["x_far"] * 2 + (bits["x_near"] + bits["x_far"]) % 2
-    return (group * 2 + bits["z_near"]) * 8 + bits["y_near"] * 4 + x
-
-
-def sum_kernel(
-    left_ref, right_ref, out_ref, twin_left, twin_right, work, got0, got1, got2, got3, last, final,
-    twin_send, twin_recv, step_send, step_recv, final_send, final_recv,
-):
-    hi, core, z, lo, x = place()
-    near, pair = z % 2, z // 2
-    bits = {"x_near": (x % 2 + x // 2) % 2, "x_far": x // 2, "y_near": lo, "z_near": near}
-    partners = {
-        "x_near": device(hi, core, z, lo, x + 1 - 2 * (x % 2)),
-        "x_far": device(hi, core, z, lo, 3 - x),
-        "y_near": device(hi, core, z, 1 - lo, x),
-        "z_near": device(hi, core, z + 1 - 2 * near, lo, x),
-    }
-    twin = device(hi, 1 - core, z, lo, x)
-    others = []
-    for step_hi in range(2):
-        for step_pair in range(4):
-            if step_hi + step_pair > 0:
-                to_hi, to_pair = (hi + step_hi) % 2, (pair + step_pair) % 4
-                others.append(
-                    (step_hi * 4 + step_pair, to_hi, to_pair,
-                     device(to_hi, core, to_pair * 2 + near, lo, x))
-                )
-
-    meet([twin] + list(partners.values()) + [other[3] for other in others])
-    twin_copies = [
-        send(right_ref.at[1 - core], twin_right, twin_send, twin_recv, 0, twin),
-        send(left_ref, twin_left, twin_send, twin_recv, 1, twin),
-    ]
-    for copy in twin_copies:
-        copy.wait_recv()
-
-    got = [got0, got1, got2, got3]
-    copies = {}
-
-    def fill(group, start):
-        def quarter(at, _):
+    return bits["z_near"] * 8 + bits["y_near"] * 4 + x
+
+
+class Halving:
+    def __init__(self, right, left, twin_left, work, got, sends, recvs):
+        self.right, self.left, self.twin_left = right, left, twin_left
+        self.work, self.got, self.sends, self.recvs = work, got, sends, recvs
+        hi, core, z, lo, x = place()
+        near = z % 2
+        self.bits = {"x_near": (x % 2 + x // 2) % 2, "x_far": x // 2, "y_near": lo, "z_near": near}
+        self.partners = {
+            "x_near": device(hi, core, z, lo, x + 1 - 2 * (x % 2)),
+            "x_far": device(hi, core, z, lo, 3 - x),
+            "y_near": device(hi, core, z, 1 - lo, x),
+            "z_near": device(hi, core, z + 1 - 2 * near, lo, x),
+        }
+        self.base = [0] * len(GROUPS)
+        self.copies = {}
+
+    def fill(self, group, start):
+        kind, first_row, last_row, _ = GROUPS[group]
+        count, rows = last_row - first_row, slice(first_row, last_row)
+        left, other = self.left[kind], self.twin_left[kind]
+        work, right = self.work[group], self.right[kind]
+
+        def four(at, _):
             first = start + at * 4
-            pieces = [piece_of(group, first + j) for j in range(4)]
-            own = jnp.concatenate([left_ref[piece] for piece in pieces], axis=0)
-            other = jnp.concatenate([twin_left[piece] for piece in pieces], axis=0)
-            total = jnp.dot(own, right_ref[core], preferred_element_type=jnp.float32)
-            total += jnp.dot(other, twin_right[...], preferred_element_type=jnp.float32)
-            work[group, pl.ds(first, 4)] = total.astype(jnp.bfloat16).reshape(
-                4, PIECE_ROWS, HALF_LANES
+            parts = []
+            for j in range(4):
+                block = combination(group, first + j)
+                parts.append(jnp.concatenate([left[block, rows], other[block, rows]], axis=1))
+            total = jnp.dot(
+                jnp.concatenate(parts, axis=0), right[...], preferred_element_type=jnp.float32
             )
+            work[pl.ds(first, 4)] = total.astype(jnp.bfloat16).reshape(4, count, HALF_LANES)
             return 0
 
-        lax.fori_loop(0, 2, quarter, 0)
-
-    def take(group, step, start, count, offset):
+        lax.fori_loop(0, 2, four, 0)
+
+    def send(self, group, step, first):
+        name = order_of(group)[step]
+        self.copies[group, step] = send(
+            self.work[group].at[pl.ds(first, 8 >> step)], self.got[group][step],
+            self.sends, self.recvs, (group, step), self.partners[name],
+        )
+
+    def begin(self, group):
+        bit = self.bits[order_of(group)[0]]
+        self.fill(group, (1 - bit) * 8)
+        self.send(group, 0, (1 - bit) * 8)
+
+    def keep(self, group):
+        self.base[group] = self.bits[order_of(group)[0]] * 8
+        self.fill(group, self.base[group])
+
+    def take(self, group, step, start, count, offset):
+        work, got = self.work[group], self.got[group][step]
+
         def one(at, _):
-            total = work[group, start + at].astype(jnp.float32)
-            total += got[step][group, offset + at].astype(jnp.float32)
-            work[group, start + at] = total.astype(jnp.bfloat16)
+            total = work[start + at].astype(jnp.float32) + got[offset + at].astype(jnp.float32)
+            work[start + at] = total.astype(jnp.bfloat16)
             return 0
 
         lax.fori_loop(0, count, one, 0)
 
-    base = [0, 0, 0, 0]
-    for group in range(4):
-        name = order_of(group)[0]
-        away = (1 - bits[name]) * 8
-        fill(group, away)
-        copies[group, 0] = send(
-            work.at[group, pl.ds(away, 8)], got[0].at[group],
-            step_send, step_recv, (group, 0), partners[name],
-        )
-    for group in range(4):
-        base[group] = bits[order_of(group)[0]] * 8
-        fill(group, base[group])
-    for step in range(1, 4):
-        half = 8 >> step
-        for group in range(4):
-            name = order_of(group)[step]
-            away = (1 - bits[name]) * half
-            copies[group, step - 1].wait_recv()
-            take(group, step - 1, base[group] + away, half, away)
-            copies[group, step] = send(
-                work.at[group, pl.ds(base[group] + away, half)], got[step].at[group],
-                step_send, step_recv, (group, step), partners[name],
-            )
-            mine = bits[name] * half
-            take(group, step - 1, base[group] + mine, half, mine)
-            base[group] = base[group] + mine
-    for group in range(4):
-        copies[group, 3].wait_recv()
-        total = work[group, base[group]].astype(jnp.float32) + got3[group, 0].astype(jnp.float32)
-        total = total.astype(jnp.bfloat16)
-        last[group, 0] = total[:, :KEEP_LANES]
-        last[group, 1] = total[:, HALF_LANES - KEEP_LANES :]
-    ends = []
-    for slot, to_hi, to_pair, peer in others:
-        ends.append(
-            send(
-                last.at[to_pair, to_hi], final.at[slot], final_send, final_recv, slot, peer
-            )
-        )
-    total = last[pair, hi].astype(jnp.float32)
-    for (slot, _, _, _), copy in zip(others, ends):
-        copy.wait_recv()
-        total += final[slot].astype(jnp.float32)
-    out_ref[...] = total
-    for copy in twin_copies + list(copies.values()) + ends:
-        copy.wait_send()
-
-
-def sum_products(left, right):
-    depth = left.shape[2]
-    block = (PIECE_ROWS, HALF_LANES)
-    return pl.pallas_call(
-        sum_kernel,
-        out_shape=jax.ShapeDtypeStruct((PIECE_ROWS, KEEP_LANES), jnp.float32),
-        in_specs=[pl.BlockSpec(memory_space=pltpu.VMEM)] * 2,
-        out_specs=pl.BlockSpec(memory_space=pltpu.VMEM),
-        scratch_shapes=[
-            pltpu.VMEM(left.shape, jnp.bfloat16),
-            pltpu.VMEM((depth, HALF_LANES), jnp.bfloat16),
-            pltpu.VMEM((4, 16) + block, jnp.bfloat16),
-            pltpu.VMEM((4, 8) + block, jnp.bfloat16),
-            pltpu.VMEM((4, 4) + block, jnp.bfloat16),
-            pltpu.VMEM((4, 2) + block, jnp.bfloat16),
-            pltpu.VMEM((4, 1) + block, jnp.bfloat16),
-            pltpu.VMEM((4, 2, PIECE_ROWS, KEEP_LANES), jnp.bfloat16),
-            pltpu.VMEM((8, PIECE_ROWS, KEEP_LANES), jnp.bfloat16),
-            pltpu.SemaphoreType.DMA((2,)),
-            pltpu.SemaphoreType.DMA((2,)),
-            pltpu.SemaphoreType.DMA((4, 4)),
-            pltpu.SemaphoreType.DMA((4, 4)),
-            pltpu.SemaphoreType.DMA((8,)),
-            pltpu.SemaphoreType.DMA((8,)),
-        ],
-        compiler_params=pltpu.CompilerParams(
-            collective_id=3, has_side_effects=True, vmem_limit_bytes=40 * 1024 * 1024
-        ),
-    )(left, right)
-
-
-def weight_gradients(grad_projected, modulated, grad_flat, space_mixed):
-    tokens, width = modulated.shape
-    qkv_rows = grad_projected.T.reshape(64, -1, tokens)
-    proj_rows = grad_flat.T.reshape(64, -1, tokens)
-    n_qkv, n_proj = qkv_rows.shape[1], proj_rows.shape[1]
-    left = jnp.concatenate(
-        [
-            jnp.pad(qkv_rows, ((0, 0), (0, PIECE_ROWS - n_qkv), (0, 0))),
-            jnp.pad(proj_rows, ((0, 0), (n_qkv, PIECE_ROWS - n_qkv - n_proj), (0, 0))),
-        ],
-        axis=2,
-    )
-    part = width // 4
-    right = jnp.concatenate([modulated, space_mixed], axis=0).reshape(2 * tokens, 2, 2, part)
-    right = jnp.transpose(right, (2, 0, 1, 3)).reshape(2, 2 * tokens, 2 * part)
-    right = jnp.pad(right, ((0, 0), (0, 0), (0, HALF_LANES - 2 * part)))
-    summed = sum_products(left, right)
-    hi = lax.axis_index("dp") // 2
-    start = hi * (part + KEEP_LANES - HALF_LANES)
-    kept = lax.dynamic_slice(summed, (0, start), (n_qkv + n_proj, part)).T
-    return kept[:, n_qkv:], kept[:, :n_qkv]
+    def advance(self, group, step):
+        half, bit = 8 >> step, self.bits[order_of(group)[step]]
+        away, mine = (1 - bit) * half, bit * half
+        self.copies[group, step - 1].wait_recv()
+        self.take(group, step - 1, self.base[group] + away, half, away)
+        self.send(group, step, self.base[group] + away)
+        self.take(group, step - 1, self.base[group] + mine, half, mine)
+        self.base[group] = self.base[group] + mine
+
+    def last(self, group, target):
+        _, first_row, last_row, _ = GROUPS[group]
+        self.copies[group, 3].wait_recv()
+        total = self.work[group][self.base[group]].astype(jnp.float32)
+        total = (total + self.got[group][3][0].astype(jnp.float32)).astype(jnp.bfloat16)
+        target[0, first_row:last_row] = total[:, :KEEP_LANES]
+        target[1, first_row:last_row] = total[:, HALF_LANES - KEEP_LANES :]
 
 
 def near_peers():
@@ -437,53 +360,43 @@
     )
 
 
-def space_forward(query_ref, key_ref, value_ref, angles_ref, turned_query, turned_key, weights_ref, mixed):
-    cosine, sine = turn_tables(angles_ref[...], HEAD // 4)
-    for source, target in ((query_ref, turned_query), (key_ref, turned_key)):
-        values = source[...].astype(jnp.float32)
-        target[...] = turn(values, cosine, sine, HEAD // 4, 1.0).astype(jnp.bfloat16)
-    mixed[...] = jnp.zeros_like(mixed)
-    for head in range(HEADS):
+def space_forward(heads, turned_query, turned_key, value, weights_ref, mixed):
+    for head in heads:
         window, mask = head_window(head)
         scores = across_rows(turned_query[:, window] * mask, turned_key[:, window]) * FACTOR
         weights = softmax_rows(scores)
         weights_ref[head] = weights
         mixed[:, window] += jnp.dot(
-            weights.astype(jnp.bfloat16), value_ref[:, window] * mask,
+            weights.astype(jnp.bfloat16), value[:, window] * mask,
             preferred_element_type=jnp.float32,
         )
 
 
-def space_back_kernel(
-    back_ref, resid_ref, proj_full, query_ref, key_ref, value_ref, weights_ref, angles_ref,
-    hidden_out, query_out, key_out, value_out, total_query, total_key, total_value, grad,
-):
-    hidden = resid_ref[...].astype(jnp.float32) + back_ref[...].astype(jnp.float32)
-    hidden = hidden.astype(jnp.bfloat16)
-    hidden_out[...] = hidden
-    for block in range(3):
-        columns = slice(block * 384, block * 384 + 384)
-        part = across_rows(hidden[:, columns], weight_rows(proj_full, columns))
-        if block == 0:
-            total_query[...] = part
-        else:
-            total_query[...] += part
-    grad[...] = total_query[...].astype(jnp.bfloat16)
-    totals = (total_query, total_key, total_value)
-    for total in totals:
-        total[...] = jnp.zeros_like(total)
-    for head in range(HEADS):
+def space_back_heads(heads, weights, turned_query, turned_key, value, grad, totals):
+    for head in heads:
         window, mask = head_window(head)
         parts = head_back(
-            weights_ref[head], query_ref[:, window], key_ref[:, window], value_ref[:, window],
+            weights[head], turned_query[:, window], turned_key[:, window], value[:, window],
             grad[:, window], mask,
         )
         for total, part in zip(totals, parts):
             total[:, window] += part
-    cosine, sine = turn_tables(angles_ref[...], HEAD // 4)
-    for total, out in ((total_query, query_out), (total_key, key_out)):
-        out[...] = turn(total[...], cosine, sine, HEAD // 4, -1.0).astype(jnp.bfloat16)
-    value_out[...] = total_value[...].astype(jnp.bfloat16)
+
+
+def core_columns(rows, core):
+    part = WIDTH // 4
+    pieces = [rows[:, (hi * 2 + core) * part : (hi * 2 + core + 1) * part] for hi in range(2)]
+    rest = jnp.zeros((rows.shape[0], HALF_LANES - 2 * part), rows.dtype)
+    return jnp.concatenate(pieces + [rest], axis=1)
+
+
+def stage(pairs, sems):
+    copies = [
+        pltpu.make_async_copy(source, target, sems.at[at]) for at, (source, target) in enumerate(pairs)
+    ]
+    for copy in copies:
+        copy.start()
+    return copies
 
 
 def local_call(kernel, outs, scratch, megabytes, *args):
@@ -499,18 +412,13 @@
 
 ROWS = ((128, WIDTH), jnp.bfloat16)
 WIDE_ROWS = ((128, WIDTH), jnp.float32)
-
-
-def space_back(*args):
-    return local_call(
-        space_back_kernel, [ROWS] * 4, [WIDE_ROWS] * 3 + [ROWS], 24, *args
-    )
+RIGHT = ((2, 128, HALF_LANES), jnp.bfloat16)
 
 
 def time_kernel(
     rows_ref, qkv_full, scale_ref, shift_ref, grad_ref, angles_ref,
-    modulated_ref, projected_ref, back_ref, sums_ref,
-    normed_ref, wide, turned, total_back,
+    right_ref, projected_ref, back_ref, sums_ref,
+    normed_ref, wide, turned, total_back, modulated_ref,
 ):
     rows = rows_ref[...].astype(jnp.float32)
     centered = rows - jnp.mean(rows, axis=-1, keepdims=True)
@@ -518,7 +426,10 @@
     normed = centered * inverse
     normed_ref[...] = normed
     scale = 1.0 + scale_ref[...]
-    modulated_ref[...] = (normed * scale + shift_ref[...]).astype(jnp.bfloat16)
+    modulated = (normed * scale + shift_ref[...]).astype(jnp.bfloat16)
+    modulated_ref[...] = modulated
+    for core in range(2):
+        right_ref[core] = core_columns(modulated, core)
     for block in range(9):
         columns = slice(block * 384, block * 384 + 384)
         wide[:, columns] = jnp.dot(
@@ -580,31 +491,62 @@
     wide = (128, 3 * WIDTH)
     return local_call(
         time_kernel,
-        [ROWS, (wide, jnp.bfloat16), ROWS, ((8, WIDTH), jnp.float32)],
-        [WIDE_ROWS, (wide, jnp.float32), (wide, jnp.bfloat16), WIDE_ROWS],
+        [RIGHT, (wide, jnp.bfloat16), ROWS, ((8, WIDTH), jnp.float32)],
+        [WIDE_ROWS, (wide, jnp.float32), (wide, jnp.bfloat16), WIDE_ROWS, ROWS],
         40,
         *args,
     )
 
 
 def front_kernel(
-    query_ref, key_ref, value_ref, hidden_ref, angles_ref, proj_ref, qkv_ref,
-    rows_ref, mixed_ref, turned_query, turned_key, weights_ref, proj_full, qkv_full,
-    wide, *scratch,
+    query_in, key_in, value_in, hidden_in, angles_ref, proj_ref, qkv_ref,
+    rows_ref, right_ref, turned_query, turned_key, weights_ref, proj_full, qkv_full,
+    query_ref, key_ref, value_ref, hidden_ref, wide, mixed_ref, stage_sems, *scratch,
 ):
+    staged = stage(
+        [(query_in, query_ref), (key_in, key_ref), (value_in, value_ref), (hidden_in, hidden_ref)],
+        stage_sems,
+    )
     proj = Gather(proj_ref, proj_full, 640, *scratch[:3])
-    qkv = Gather(qkv_ref, qkv_full, 1792, *scratch[3:6])
-    exchange = Exchange(*scratch[6:])
+    thirds = []
+    for third in range(3):
+        columns = pl.ds(third * WIDTH, WIDTH)
+        thirds.append(
+            Gather(
+                qkv_ref.at[:, columns], qkv_full.at[:, :, :, columns], 640,
+                *scratch[3 * third + 3 : 3 * third + 6],
+            )
+        )
+    one, two, three = thirds
+    exchange = Exchange(*scratch[12:])
     meet([proj.twin, proj.across] + exchange.plane + exchange.line)
-    proj.start()
-    qkv.start()
+    for gather in (proj, one, two, three):
+        gather.start()
+    for copy in staged:
+        copy.wait()
+    cosine, sine = turn_tables(angles_ref[...], HEAD // 4)
+    for source, target in ((query_ref, turned_query), (key_ref, turned_key)):
+        values = source[...].astype(jnp.float32)
+        target[...] = turn(values, cosine, sine, HEAD // 4, 1.0).astype(jnp.bfloat16)
+    wide[...] = jnp.zeros_like(wide)
+
+    def heads(first):
+        space_forward(
+            range(first, first + 4), turned_query, turned_key, value_ref, weights_ref, wide
+        )
+
     proj.spread()
-    space_forward(
-        query_ref, key_ref, value_ref, angles_ref, turned_query, turned_key, weights_ref, wide
-    )
-    mixed_ref[...] = wide[...].astype(jnp.bfloat16)
+    heads(0)
+    one.spread()
+    heads(4)
     proj.pass_on()
+    heads(8)
+    two.spread()
     proj.last()
+    heads(12)
+    one.pass_on()
+    mixed = wide[...].astype(jnp.bfloat16)
+    mixed_ref[...] = mixed
     proj.arrive()
     for block in range(3):
         columns = slice(block * 384, block * 384 + 384)
@@ -612,50 +554,105 @@
             mixed_ref[...], weight_rows(proj_full, columns), preferred_element_type=jnp.float32
         )
     exchange.start_plane(wide[...].astype(jnp.bfloat16))
-    qkv.spread()
+    three.spread()
+    one.last()
+    for core in range(2):
+        right_ref[core] = core_columns(mixed_ref[...], core)
     exchange.start_line()
-    qkv.pass_on()
-    qkv.last()
+    two.pass_on()
+    two.last()
+    three.pass_on()
+    three.last()
     rows_ref[...] = exchange.finish()
-    qkv.arrive()
-    proj.finish()
-    qkv.finish()
+    for gather in thirds:
+        gather.arrive()
+    for gather in (proj, one, two, three):
+        gather.finish()
 
 
 def front(query, key, value, hidden, angles, proj, qkv):
     def whole(weight):
         return jax.ShapeDtypeStruct((4, 4, 80, weight.shape[1]), weight.dtype)
 
-    vmem, anywhere = pl.BlockSpec(memory_space=pltpu.VMEM), pl.BlockSpec(memory_space=pl.ANY)
+    vmem, away = pl.BlockSpec(memory_space=pltpu.VMEM), pl.BlockSpec(memory_space=pltpu.HBM)
     rows = jax.ShapeDtypeStruct(*ROWS)
     return pl.pallas_call(
         front_kernel,
         out_shape=(
-            rows, rows, rows, rows, jax.ShapeDtypeStruct((HEADS, 128, 128), jnp.float32),
-            whole(proj), whole(qkv),
+            rows, jax.ShapeDtypeStruct(*RIGHT), rows, rows,
+            jax.ShapeDtypeStruct((HEADS, 128, 128), jnp.float32), whole(proj), whole(qkv),
         ),
-        in_specs=[vmem] * 5 + [anywhere] * 2,
+        in_specs=[away] * 4 + [vmem] + [away] * 2,
         out_specs=(vmem,) * 7,
-        scratch_shapes=[pltpu.VMEM(*WIDE_ROWS)] + GATHER_SCRATCH * 2 + EXCHANGE_SCRATCH,
+        scratch_shapes=[pltpu.VMEM(*ROWS)] * 4
+        + [pltpu.VMEM(*WIDE_ROWS), pltpu.VMEM(*ROWS), pltpu.SemaphoreType.DMA((4,))]
+        + GATHER_SCRATCH * 4
+        + EXCHANGE_SCRATCH,
         compiler_params=pltpu.CompilerParams(
             collective_id=1, has_side_effects=True, vmem_limit_bytes=32 * 1024 * 1024
         ),
     )(query, key, value, hidden, angles, proj, qkv)
 
 
-def back_kernel(rows_ref, sums_ref, out_ref, total_ref, plane_sums, line_sums, *scratch):
-    sum_sends, sum_recvs = scratch[:2]
-    exchange = Exchange(*scratch[2:])
-    z, group = exchange.z, exchange.group
-    meet(exchange.plane + exchange.line)
-    exchange.start_plane(rows_ref[...])
-    copies = [
-        send(sums_ref, plane_sums.at[group], sum_sends, sum_recvs, step, exchange.plane[step - 1])
+def tail_kernel(
+    left_qkv, right_qkv, back_rows, sums_ref, angles_ref,
+    right_proj, resid_in, query_in, key_in, value_in, weights_in, proj_in,
+    hidden_out, query_out, key_out, value_out, total_ref, qkv_out, proj_out,
+    resid_ref, query_ref, key_ref, value_ref, weights_ref, proj_full, stage_sems,
+    left_proj, both_qkv, both_proj, twin_qkv, twin_proj, twin_send, twin_recv,
+    total_query, total_key, total_value, grad,
+    plane_sums, line_sums, sum_sends, sum_recvs,
+    step_send, step_recv, qkv_last, proj_last, qkv_final, proj_final, final_send, final_recv,
+    *scratch,
+):
+    count = len(GROUPS)
+    exchange = Exchange(*scratch[:6])
+    work, got = scratch[6 : 6 + count], scratch[6 + count :]
+    got = [got[4 * group : 4 * group + 4] for group in range(count)]
+    hi, core, z, lo, x = place()
+    near, pair, group_at = z % 2, z // 2, exchange.group
+    twin = device(hi, 1 - core, z, lo, x)
+    halving = Halving(
+        (both_qkv, both_proj), (left_qkv, left_proj), (twin_qkv, twin_proj), work, got,
+        step_send, step_recv,
+    )
+    others = []
+    for step_hi in range(2):
+        for step_pair in range(4):
+            if step_hi + step_pair > 0:
+                to_hi, to_pair = (hi + step_hi) % 2, (pair + step_pair) % 4
+                others.append(
+                    (step_hi * 4 + step_pair, to_hi, to_pair,
+                     device(to_hi, core, to_pair * 2 + near, lo, x))
+                )
+    staged = stage(
+        [
+            (resid_in, resid_ref), (proj_in, proj_full), (query_in, query_ref), (key_in, key_ref),
+            (value_in, value_ref), (weights_in, weights_ref),
+            (right_proj.at[core], both_proj.at[pl.ds(0, 128)]),
+        ],
+        stage_sems,
+    )
+    meet([twin] + [other[3] for other in others[3:]] + exchange.plane + exchange.line)
+    own, other = pl.ds(0, 128), pl.ds(128, 128)
+    twins = [
+        send(right_qkv.at[1 - core], both_qkv.at[other], twin_send, twin_recv, 0, twin),
+        send(left_qkv, twin_qkv, twin_send, twin_recv, 1, twin),
+        send(right_proj.at[1 - core], both_proj.at[other], twin_send, twin_recv, 2, twin),
+    ]
+    exchange.start_plane(back_rows[...])
+    sums = [
+        send(sums_ref, plane_sums.at[group_at], sum_sends, sum_recvs, step, exchange.plane[step - 1])
         for step in range(1, 8)
     ]
-    plane_sums[group] = sums_ref[...]
+    plane_sums[group_at] = sums_ref[...]
+    both_qkv[own] = right_qkv[core]
+    twins[0].wait_recv()
+    twins[1].wait_recv()
+    for group in range(2):
+        halving.begin(group)
     exchange.start_line()
-    for copy in copies:
+    for copy in sums:
         copy.wait_recv()
     line_sums[z] = jnp.sum(plane_sums[...], axis=0)
     more = [
@@ -665,34 +662,134 @@
         )
         for step in range(1, 8)
     ]
-    out_ref[...] = exchange.finish()
+    for group in range(2, 4):
+        halving.begin(group)
+    for group in range(4):
+        halving.keep(group)
+    row = lax.broadcasted_iota(jnp.int32, (PROJ_ROWS, WIDTH), 0)
+    column = lax.broadcasted_iota(jnp.int32, (PROJ_ROWS, WIDTH), 1)
+    piece = WIDTH // 64
+    wanted = jnp.where(row < 4 * piece, row // piece * (16 * piece) + row % piece, -WIDTH)
+    ahead = column - wanted
+    for copy in staged:
+        copy.wait()
+    frames = exchange.finish()
+    hidden = resid_ref[...].astype(jnp.float32) + frames.astype(jnp.float32)
+    hidden_out[...] = hidden.astype(jnp.bfloat16)
+    for block in range(16):
+        chosen = jnp.where(ahead == block * piece, 1.0, 0.0).astype(jnp.bfloat16)
+        left_proj[block] = across_rows(chosen, hidden_out[...]).astype(jnp.bfloat16)
+    twins.append(send(left_proj, twin_proj, twin_send, twin_recv, 3, twin))
+    for block in range(3):
+        columns = slice(block * 384, block * 384 + 384)
+        part = across_rows(hidden_out[:, columns], weight_rows(proj_full, columns))
+        if block == 0:
+            total_query[...] = part
+        else:
+            total_query[...] += part
+    grad[...] = total_query[...].astype(jnp.bfloat16)
+    twins[2].wait_recv()
+    twins[3].wait_recv()
+    for group in range(4, 6):
+        halving.begin(group)
+    for group in range(4, 6):
+        halving.keep(group)
+    for group in range(4):
+        halving.advance(group, 1)
+    totals = (total_query, total_key, total_value)
+    for total in totals:
+        total[...] = jnp.zeros_like(total)
+
+    def heads(first, end):
+        space_back_heads(
+            range(first, end), weights_ref, query_ref, key_ref, value_ref, grad, totals
+        )
+
+    heads(0, 10)
+    for group in range(4):
+        halving.advance(group, 2)
+    heads(10, 16)
+    for group in range(4, 6):
+        halving.advance(group, 1)
+    for group in range(4):
+        halving.advance(group, 3)
+    cosine, sine = turn_tables(angles_ref[...], HEAD // 4)
+    for total, out in ((total_query, query_out), (total_key, key_out)):
+        out[...] = turn(total[...], cosine, sine, HEAD // 4, -1.0).astype(jnp.bfloat16)
+    value_out[...] = total_value[...].astype(jnp.bfloat16)
     for copy in more:
         copy.wait_recv()
     total_ref[...] = jnp.sum(line_sums[...], axis=0)
-    for copy in copies + more:
+    for group in range(4, 6):
+        halving.advance(group, 2)
+    for group in range(4):
+        halving.last(group, qkv_last)
+    ends = []
+    for slot, to_hi, to_pair, peer in others:
+        rows = pl.ds(pl.multiple_of(to_pair * 48, 16), QKV_WINDOW)
+        ends.append(
+            send(qkv_last.at[to_hi, rows], qkv_final.at[slot], final_send, final_recv, slot, peer)
+        )
+    for group in range(4, 6):
+        halving.advance(group, 3)
+    for group in range(4, 6):
+        halving.last(group, proj_last)
+    for slot, to_hi, to_pair, peer in others:
+        rows = pl.ds(pl.multiple_of(to_pair * 16, 16), PROJ_WINDOW)
+        ends.append(
+            send(
+                proj_last.at[to_hi, rows], proj_final.at[slot], final_send, final_recv, 8 + slot,
+                peer,
+            )
+        )
+    total = qkv_last[hi, pl.ds(pl.multiple_of(pair * 48, 16), QKV_WINDOW)].astype(jnp.float32)
+    for (slot, _, _, _), copy in zip(others, ends[:7]):
+        copy.wait_recv()
+        total += qkv_final[slot].astype(jnp.float32)
+    qkv_out[...] = total
+    total = proj_last[hi, pl.ds(pl.multiple_of(pair * 16, 16), PROJ_WINDOW)].astype(jnp.float32)
+    for (slot, _, _, _), copy in zip(others, ends[7:]):
+        copy.wait_recv()
+        total += proj_final[slot].astype(jnp.float32)
+    proj_out[...] = total
+    for copy in twins + sums + more + list(halving.copies.values()) + ends:
         copy.wait_send()
 
 
-def back(rows, sums):
-    vmem = pl.BlockSpec(memory_space=pltpu.VMEM)
+def tail(left, right, back_rows, sums, angles, right_proj, resid, query, key, value, weights, proj):
+    vmem, away = pl.BlockSpec(memory_space=pltpu.VMEM), pl.BlockSpec(memory_space=pltpu.HBM)
+    b16, f32 = jnp.bfloat16, jnp.float32
+    shape, dma = pltpu.VMEM, pltpu.SemaphoreType.DMA
+    outs = [ROWS] * 4 + [
+        (sums.shape, f32), ((QKV_WINDOW, KEEP_LANES), f32), ((PROJ_WINDOW, KEEP_LANES), f32)
+    ]
+    counts = [last - first for _, first, last, _ in GROUPS]
+    scratch = [
+        shape(*ROWS), shape(*ROWS), shape(*ROWS), shape(*ROWS),
+        shape(weights.shape, f32), shape(proj.shape, b16), dma((7,)),
+        shape((16, PROJ_ROWS, 128), b16), shape((256, HALF_LANES), b16), shape((256, HALF_LANES), b16),
+        shape((16, QKV_ROWS, 128), b16), shape((16, PROJ_ROWS, 128), b16), dma((4,)), dma((4,)),
+        shape(*WIDE_ROWS), shape(*WIDE_ROWS), shape(*WIDE_ROWS), shape(*ROWS),
+        shape((8,) + sums.shape, f32), shape((8,) + sums.shape, f32), dma((16,)), dma((16,)),
+        dma((6, 4)), dma((6, 4)),
+        shape((2, QKV_ROWS, KEEP_LANES), b16), shape((2, PROJ_ROWS, KEEP_LANES), b16),
+        shape((8, QKV_WINDOW, KEEP_LANES), b16), shape((8, PROJ_WINDOW, KEEP_LANES), b16),
+        dma((16,)), dma((16,)),
+    ] + EXCHANGE_SCRATCH
+    scratch += [shape((16, count, HALF_LANES), b16) for count in counts]
+    scratch += [
+        shape((8 >> step, count, HALF_LANES), b16) for count in counts for step in range(4)
+    ]
     return pl.pallas_call(
-        back_kernel,
-        out_shape=(
-            jax.ShapeDtypeStruct(rows.shape, rows.dtype),
-            jax.ShapeDtypeStruct(sums.shape, sums.dtype),
+        tail_kernel,
+        out_shape=tuple(jax.ShapeDtypeStruct(*out) for out in outs),
+        in_specs=[vmem] * 5 + [away] * 7,
+        out_specs=(vmem,) * len(outs),
+        scratch_shapes=scratch,
+        compiler_params=pltpu.CompilerParams(
+            collective_id=2, has_side_effects=True, vmem_limit_bytes=44 * 1024 * 1024
         ),
-        in_specs=[vmem] * 2,
-        out_specs=(vmem, vmem),
-        scratch_shapes=[
-            pltpu.VMEM((8,) + sums.shape, sums.dtype),
-            pltpu.VMEM((8,) + sums.shape, sums.dtype),
-            pltpu.SemaphoreType.DMA((16,)),
-            pltpu.SemaphoreType.DMA((16,)),
-        ] + EXCHANGE_SCRATCH,
-        compiler_params=pltpu.CompilerParams(
-            collective_id=2, has_side_effects=True, vmem_limit_bytes=16 * 1024 * 1024
-        ),
-    )(rows, sums)
+    )(left, right, back_rows, sums, angles, right_proj, resid, query, key, value, weights, proj)
 
 
 def turn_angles(places, half):
@@ -723,22 +820,24 @@
     def flat(values):
         return values.reshape(128, WIDTH)
 
-    rows, space_mixed, space_query, space_key, space_weights, proj_full, qkv_full = front(
+    rows, right_proj, space_query, space_key, space_weights, proj_full, qkv_full = front(
         flat(query_space), flat(key_space), flat(value_space), flat(hidden), space_angles,
         proj_space, qkv_time,
     )
-    modulated, grad_projected, resid_back, sums = time_sublayer(
+    right_qkv, grad_projected, resid_back, sums = time_sublayer(
         rows, qkv_full, scale_time, shift_time, flat(grad_attn_time), time_angles
     )
-    back_frames, sums = back(resid_back, sums[:2].reshape(8, -1))
+    left = jnp.transpose(grad_projected.T.reshape(4, 16, 54, 128), (1, 0, 2, 3)).reshape(16, 216, 128)
+    left = jnp.pad(left, ((0, 0), (0, QKV_ROWS - 216), (0, 0)))
+    grad_hidden, grad_query, grad_key, grad_value, sums, qkv_block, proj_block = tail(
+        left, right_qkv, resid_back, sums[:2].reshape(8, -1), space_angles, right_proj,
+        flat(grad_resid), space_query, space_key, flat(value_space), space_weights, proj_full,
+    )
     sums = sums.reshape(2, WIDTH)
-    grad_hidden, grad_query, grad_key, grad_value = space_back(
-        back_frames, flat(grad_resid), proj_full, space_query, space_key, flat(value_space),
-        space_weights, space_angles,
-    )
-    grad_proj_space, grad_qkv_time = weight_gradients(
-        grad_projected, modulated, grad_hidden, space_mixed
-    )
+    hi, pair = lax.axis_index("dp") // 2, seq_place // 16
+    column = hi * (WIDTH // 4 + KEEP_LANES - HALF_LANES)
+    grad_qkv_time = lax.dynamic_slice(qkv_block, (pair * 6, column), (54, WIDTH // 4)).T
+    grad_proj_space = lax.dynamic_slice(proj_block, (pair * 2, column), (18, WIDTH // 4)).T
     shape = hidden.shape
     return (
         grad_hidden.reshape(shape),

time: 199 us -> 175 us (0.88)
  Pallas kernels: 166 us -> 140 us
  local copies, waits for them, and re-layouts: 27.1 us -> 31.2 us
  other arithmetic: 3.85 us -> 0.82 us
    pallas_call x3 -> x2, Pallas kernels: 146 us -> 127 us  [the longest x1 74.7 us: tail(): pl.pallas_call(tail_kernel, out_shape=tuple((jax.ShapeDtypeStruct(*out) f...]
    pallas_call x2 -> x1, Pallas kernels: 20.2 us -> 13 us  [local_call(): pl.pallas_call(kernel, out_shape=tuple((jax.ShapeDtypeStruct(shape, kind)...]
    transpose x4, local copies, waits for them, and re-layouts: 2.28 us -> 5.09 us  [the longest x1 2.22 us: body(): grad_projected.T.reshape(4, 16, 54, 128)]
    concatenate x2 -> x0, other arithmetic: 2.39 us -> none  [the longest x1 1.38 us: weight_gradients(): jnp.concatenate([jnp.pad(qkv_rows, ((0, 0), (0, PIECE_ROWS - n_qkv), (0,...]
    unnamed x52 -> x56, local copies, waits for them, and re-layouts: 17.4 us -> 19.2 us
where the time goes in v4:
time: 175 us; the launch traced here: 173 us
  Pallas kernels  140 us (80%)
  local copies, waits for them, and re-layouts  31.2 us (18%)
    pallas_call x1, Pallas kernels, tail(): pl.pallas_call(tail_kernel, out_shape=tuple((jax.ShapeDtypeStruct(*out) f...  74.7 us
    pallas_call x1, Pallas kernels, front(): pl.pallas_call(front_kernel, out_shape=(rows, jax.ShapeDtypeStruct(*RIGHT...  52.4 us
    unnamed x56, local copies, waits for them, and re-layouts  19.2 us
    pallas_call x1, Pallas kernels, local_call(): pl.pallas_call(kernel, out_shape=tuple((jax.ShapeDtypeStruct(shape, kind)...  13 us

profile of v4, /device:TPU:1, one launch (start us, length us, event | category | flops | bytes accessed | tf_op | source)
XLA Modules:
  0.0 173.1 jit_solution(1346254385663770545)
XLA Ops:
  0.8 0.8 slice.22
  1.8 0.8 slice.21
  3.5 1.1 reshape.113.grad_ref
  4.6 1.5 copy-done
  6.2 1.0 copy-done.1
  7.1 1.1 copy-done.6
  8.2 1.0 copy-done.14
  9.2 1.0 copy-done.15
  10.1 1.0 copy-done.16
  11.1 52.4 %shard_map.170 = (bf16[128,1152]{1,0:T(8,128)(2,1)S(1)}, bf16[2,128,640]{2,1,0:T(8,128)(2,1)S(1)}, bf16[128,1152]{1,0:T(8,128)(2,1)S(1)}, bf16[128,1152]{1,0:T(8...) custom-call(bf16[128,1152]{1,0:T(8,128)(2,1)S(1)} %bitcast.30, ...), custom_call_target="tpu_custom_call" | custom-call | tf_op jit(solution)/shard_map/pallas_call | solution.py:579
  63.5 0.7 copy-done.7
  64.2 0.7 copy-done.18
  65.6 13.0 %shard_map.171 = (bf16[2,128,640]{2,1,0:T(8,128)(2,1)S(1)}, bf16[128,3456]{1,0:T(8,128)(2,1)S(1)}, bf16[128,1152]{1,0:T(8,128)(2,1)S(1)}, f32[8,1152]{1,0:T(8,128)S(1)}) custom-call(bf16[128,1152]{1,0:T(8,128)(2,1)S(1)} %get-tuple-element.26.rows_ref, bf16[4,4,80,3456]{3,2,1,0:T(8,128)(2,1)S(1)} %get-tuple-element.27.qkv_full, f32[1,1152]{1,0:T(1,128)S(1)} %copy-done.24, ...), custom_call_target="tpu_custom_call" | custom-call | tf_op jit(solution)/shard_map/pallas_call | solution.py:403
  78.7 0.9 copy-done.5
  80.3 0.7 copy-done.22
  81.0 2.2 %copy.28 = bf16[3456,128]{1,0:T(8,128)(2,1)} copy(bf16[3456,128]{0,1:T(8,128)(2,1)} %bitcast.25) | data formatting | bytes 1769472 | tf_op jit(solution)/shard_map/transpose | solution.py:830
  83.3 2.1 %reshape.114 = bf16[4,16,54,128]{3,2,1,0:T(8,128)(2,1)} reshape(bf16[3456,128]{1,0:T(8,128)(2,1)} %copy.28) | data formatting | bytes 1769472 | tf_op jit(solution)/shard_map/reshape | solution.py:830
  85.5 1.4 copy.29
  87.6 74.7 %shard_map.172 = (bf16[128,1152]{1,0:T(8,128)(2,1)S(1)}, bf16[128,1152]{1,0:T(8,128)(2,1)S(1)}, bf16[128,1152]{1,0:T(8,128)(2,1)S(1)}, bf16[128,1152]{1,0:T(8,12...) custom-call(bf16[16,224,128]{2,1,0:T(8,128)(2,1)S(1)} %pad.13.left_qkv, ...), custom_call_target="tpu_custom_call" | custom-call | tf_op jit(solution)/shard_map/pallas_call | solution.py:783
  166.5 0.7 dynamic-slice_bitcast_fusion
  167.3 1.7 copy.35
  168.9 1.7 copy.36
  170.6 1.7 copy.37
  172.3 0.7 copy.38
  (64 shorter events, 7.5 us)
Async XLA Ops:
  0.6 65.0 %copy-start.24 = (f32[1,1152]{1,0:T(1,128)S(1)}, f32[1,1152]{1,0:T(1,128)}, u32[]{:S(2)}) copy-start(f32[1,1152]{1,0:T(1,128)} %scale_ref.1) | copy-start | bytes 13828
  0.6 65.0 %copy-start.25 = (f32[1,1152]{1,0:T(1,128)S(1)}, f32[1,1152]{1,0:T(1,128)}, u32[]{:S(2)}) copy-start(f32[1,1152]{1,0:T(1,128)} %shift_ref.1) | copy-start | bytes 13828
  4.6 1.6 copy-start
  6.2 1.0 copy-start.1
  7.1 1.1 copy-start.6
  8.2 1.0 copy-start.14
  9.2 1.0 copy-start.15
  10.1 1.0 copy-start.16
  63.5 0.7 copy-start.7
  64.2 0.7 copy-start.18
  64.9 0.7 copy-start.20
  65.6 13.0 %copy-start.3 = (f32[16,128,128]{2,1,0:T(8,128)}, f32[16,128,128]{2,1,0:T(8,128)S(1)}, u32[]{:S(2)}) copy-start(f32[16,128,128]{2,1,0:T(8,128)S(1)} %get-tuple-element.35.weights_in) | copy-start | bytes 3145732
  78.7 0.9 copy-start.5
  80.3 0.7 copy-start.22
  85.5 1.8 %copy-start.2 = (bf16[1,1,128,1152]{3,2,1,0:T(8,128)(2,1)S(1)}, bf16[1,1,128,1152]{3,2,1,0:T(8,128)(2,1)}, u32[]{:S(2)}) copy-start(bf16[1,1,128,1152]{3,2,1,0:T(8,128)(2,1)} %param.14) | copy-start | bytes 884740
  85.5 1.8 %copy-start.4 = (f32[16,128,128]{2,1,0:T(8,128)S(1)}, f32[16,128,128]{2,1,0:T(8,128)}, u32[]{:S(2)}) copy-start(f32[16,128,128]{2,1,0:T(8,128)} %copy-done.3) | copy-start | bytes 3145732
  85.5 1.8 %copy-start.8 = (bf16[2,128,640]{2,1,0:T(8,128)(2,1)S(1)}, bf16[2,128,640]{2,1,0:T(8,128)(2,1)}, u32[]{:S(2)}) copy-start(bf16[2,128,640]{2,1,0:T(8,128)(2,1)} %copy-done.7) | copy-start | bytes 983044
  85.5 1.8 %copy-start.10 = (bf16[2,128,640]{2,1,0:T(8,128)(2,1)S(1)}, bf16[2,128,640]{2,1,0:T(8,128)(2,1)}, u32[]{:S(2)}) copy-start(bf16[2,128,640]{2,1,0:T(8,128)(2,1)} %copy-done.9) | copy-start | bytes 983044
  85.5 1.9 %copy-start.17 = (bf16[1,1,128,1152]{3,2,1,0:T(8,128)(2,1)S(1)}, bf16[1,1,128,1152]{3,2,1,0:T(8,128)(2,1)}, u32[]{:S(2)}) copy-start(bf16[1,1,128,1152]{3,2,1,0:T(8,128)(2,1)} %param.21) | copy-start | bytes 884740
  85.5 1.9 %copy-start.19 = (bf16[128,1152]{1,0:T(8,128)(2,1)S(1)}, bf16[128,1152]{1,0:T(8,128)(2,1)}, u32[]{:S(2)}) copy-start(bf16[128,1152]{1,0:T(8,128)(2,1)} %copy-done.18) | copy-start | bytes 884740
  85.5 2.0 %copy-start.21 = (bf16[128,1152]{1,0:T(8,128)(2,1)S(1)}, bf16[128,1152]{1,0:T(8,128)(2,1)}, u32[]{:S(2)}) copy-start(bf16[128,1152]{1,0:T(8,128)(2,1)} %copy-done.20) | copy-start | bytes 884740
  85.5 2.1 %copy-start.23 = (bf16[128,1152]{1,0:T(8,128)(2,1)S(1)}, bf16[128,1152]{1,0:T(8,128)(2,1)}, u32[]{:S(2)}) copy-start(bf16[128,1152]{1,0:T(8,128)(2,1)} %copy-done.22) | copy-start | bytes 884740
  163.0 0.7 copy-start.12
  163.7 0.7 copy-start.13
  (2 other events, 1.4 us)

commit v5 on v4

--- a/solution.py
+++ b/solution.py
@@ -415,12 +415,12 @@
 RIGHT = ((2, 128, HALF_LANES), jnp.bfloat16)
 
 
-def time_kernel(
-    rows_ref, qkv_full, scale_ref, shift_ref, grad_ref, angles_ref,
-    right_ref, projected_ref, back_ref, sums_ref,
+def time_sublayer(
+    rows, qkv_full, scale_ref, shift_ref, grad_ref, angles_ref,
+    right_ref, projected_ref, sums_ref,
     normed_ref, wide, turned, total_back, modulated_ref,
 ):
-    rows = rows_ref[...].astype(jnp.float32)
+    rows = rows.astype(jnp.float32)
     centered = rows - jnp.mean(rows, axis=-1, keepdims=True)
     inverse = lax.rsqrt(jnp.mean(centered * centered, axis=-1, keepdims=True) + epsilon)
     normed = centered * inverse
@@ -468,16 +468,10 @@
             total_back[...] += part
     grad = total_back[...]
     normed = normed_ref[...]
-    sums_ref[...] = jnp.concatenate(
-        [
-            jnp.sum(grad, axis=0, keepdims=True),
-            jnp.sum(grad * normed, axis=0, keepdims=True),
-            jnp.zeros((6, WIDTH), jnp.float32),
-        ],
-        axis=0,
-    )
+    sums_ref[0:1] = jnp.sum(grad, axis=0, keepdims=True)
+    sums_ref[1:2] = jnp.sum(grad * normed, axis=0, keepdims=True)
     grad = grad * scale
-    back_ref[...] = (
+    return (
         (
             grad
             - jnp.mean(grad, axis=-1, keepdims=True)
@@ -487,26 +481,42 @@
     ).astype(jnp.bfloat16)
 
 
-def time_sublayer(*args):
-    wide = (128, 3 * WIDTH)
-    return local_call(
-        time_kernel,
-        [RIGHT, (wide, jnp.bfloat16), ROWS, ((8, WIDTH), jnp.float32)],
-        [WIDE_ROWS, (wide, jnp.float32), (wide, jnp.bfloat16), WIDE_ROWS, ROWS],
-        40,
-        *args,
-    )
-
-
-def front_kernel(
-    query_in, key_in, value_in, hidden_in, angles_ref, proj_ref, qkv_ref,
-    rows_ref, right_ref, turned_query, turned_key, weights_ref, proj_full, qkv_full,
-    query_ref, key_ref, value_ref, hidden_ref, wide, mixed_ref, stage_sems, *scratch,
+def piece_rows(values_ref, turned_rows, tall):
+    for block in range(27):
+        rows = slice(block * 128, block * 128 + 128)
+        tall[rows] = values_ref[:, rows].astype(jnp.float32).T
+    piece = 3 * WIDTH // 64
+    for at in range(16):
+        parts = [tall[(16 * k + at) * piece : (16 * k + at + 1) * piece] for k in range(4)]
+        parts.append(jnp.zeros((QKV_ROWS - 4 * piece, 128), jnp.float32))
+        turned_rows[at] = jnp.concatenate(parts, axis=0).astype(jnp.bfloat16)
+
+
+def whole_kernel(
+    angles_ref, time_angles, scale_ref, shift_ref,
+    query_in, key_in, value_in, hidden_in, grad_time_in, resid_in, proj_ref, qkv_ref,
+    hidden_out, query_out, key_out, value_out, total_ref, qkv_out, proj_out,
+    query_ref, key_ref, value_ref, hidden_ref, grad_time, resid_ref, stage_sems,
+    turned_query, turned_key, weights_ref, proj_full, qkv_full,
+    wide, mixed_ref, right_qkv, right_proj, projected, sums_ref, normed, time_wide, turned,
+    total_back, modulated, tall,
+    left_qkv, left_proj, both_qkv, both_proj, twin_qkv, twin_proj, twin_send, twin_recv,
+    total_query, total_key, total_value, grad,
+    plane_sums, line_sums, sum_sends, sum_recvs,
+    step_send, step_recv, qkv_last, proj_last, qkv_final, proj_final, final_send, final_recv,
+    *scratch,
 ):
     staged = stage(
-        [(query_in, query_ref), (key_in, key_ref), (value_in, value_ref), (hidden_in, hidden_ref)],
+        [
+            (query_in, query_ref), (key_in, key_ref), (value_in, value_ref),
+            (hidden_in, hidden_ref), (grad_time_in, grad_time), (resid_in, resid_ref),
+        ],
         stage_sems,
     )
+    hi, core, z, lo, x = place()
+    near, pair = z % 2, z // 2
+    twin = device(hi, 1 - core, z, lo, x)
+    count = len(GROUPS)
     proj = Gather(proj_ref, proj_full, 640, *scratch[:3])
     thirds = []
     for third in range(3):
@@ -518,8 +528,27 @@
             )
         )
     one, two, three = thirds
-    exchange = Exchange(*scratch[12:])
-    meet([proj.twin, proj.across] + exchange.plane + exchange.line)
+    exchange = Exchange(*scratch[12:18])
+    exchange_back = Exchange(*scratch[18:24])
+    group_at = exchange.group
+    work, got = scratch[24 : 24 + count], scratch[24 + count :]
+    got = [got[4 * group : 4 * group + 4] for group in range(count)]
+    halving = Halving(
+        (both_qkv, both_proj), (left_qkv, left_proj), (twin_qkv, twin_proj), work, got,
+        step_send, step_recv,
+    )
+    others = []
+    for step_hi in range(2):
+        for step_pair in range(4):
+            if step_hi + step_pair > 0:
+                to_hi, to_pair = (hi + step_hi) % 2, (pair + step_pair) % 4
+                others.append(
+                    (step_hi * 4 + step_pair, to_hi, to_pair,
+                     device(to_hi, core, to_pair * 2 + near, lo, x))
+                )
+    meet(
+        [twin, proj.across] + [other[3] for other in others[3:]] + exchange.plane + exchange.line
+    )
     for gather in (proj, one, two, three):
         gather.start()
     for copy in staged:
@@ -556,102 +585,39 @@
     exchange.start_plane(wide[...].astype(jnp.bfloat16))
     three.spread()
     one.last()
-    for core in range(2):
-        right_ref[core] = core_columns(mixed_ref[...], core)
+    for side in range(2):
+        right_proj[side] = core_columns(mixed_ref[...], side)
     exchange.start_line()
     two.pass_on()
     two.last()
     three.pass_on()
     three.last()
-    rows_ref[...] = exchange.finish()
     for gather in thirds:
         gather.arrive()
-    for gather in (proj, one, two, three):
-        gather.finish()
-
-
-def front(query, key, value, hidden, angles, proj, qkv):
-    def whole(weight):
-        return jax.ShapeDtypeStruct((4, 4, 80, weight.shape[1]), weight.dtype)
-
-    vmem, away = pl.BlockSpec(memory_space=pltpu.VMEM), pl.BlockSpec(memory_space=pltpu.HBM)
-    rows = jax.ShapeDtypeStruct(*ROWS)
-    return pl.pallas_call(
-        front_kernel,
-        out_shape=(
-            rows, jax.ShapeDtypeStruct(*RIGHT), rows, rows,
-            jax.ShapeDtypeStruct((HEADS, 128, 128), jnp.float32), whole(proj), whole(qkv),
-        ),
-        in_specs=[away] * 4 + [vmem] + [away] * 2,
-        out_specs=(vmem,) * 7,
-        scratch_shapes=[pltpu.VMEM(*ROWS)] * 4
-        + [pltpu.VMEM(*WIDE_ROWS), pltpu.VMEM(*ROWS), pltpu.SemaphoreType.DMA((4,))]
-        + GATHER_SCRATCH * 4
-        + EXCHANGE_SCRATCH,
-        compiler_params=pltpu.CompilerParams(
-            collective_id=1, has_side_effects=True, vmem_limit_bytes=32 * 1024 * 1024
-        ),
-    )(query, key, value, hidden, angles, proj, qkv)
-
-
-def tail_kernel(
-    left_qkv, right_qkv, back_rows, sums_ref, angles_ref,
-    right_proj, resid_in, query_in, key_in, value_in, weights_in, proj_in,
-    hidden_out, query_out, key_out, value_out, total_ref, qkv_out, proj_out,
-    resid_ref, query_ref, key_ref, value_ref, weights_ref, proj_full, stage_sems,
-    left_proj, both_qkv, both_proj, twin_qkv, twin_proj, twin_send, twin_recv,
-    total_query, total_key, total_value, grad,
-    plane_sums, line_sums, sum_sends, sum_recvs,
-    step_send, step_recv, qkv_last, proj_last, qkv_final, proj_final, final_send, final_recv,
-    *scratch,
-):
-    count = len(GROUPS)
-    exchange = Exchange(*scratch[:6])
-    work, got = scratch[6 : 6 + count], scratch[6 + count :]
-    got = [got[4 * group : 4 * group + 4] for group in range(count)]
-    hi, core, z, lo, x = place()
-    near, pair, group_at = z % 2, z // 2, exchange.group
-    twin = device(hi, 1 - core, z, lo, x)
-    halving = Halving(
-        (both_qkv, both_proj), (left_qkv, left_proj), (twin_qkv, twin_proj), work, got,
-        step_send, step_recv,
-    )
-    others = []
-    for step_hi in range(2):
-        for step_pair in range(4):
-            if step_hi + step_pair > 0:
-                to_hi, to_pair = (hi + step_hi) % 2, (pair + step_pair) % 4
-                others.append(
-                    (step_hi * 4 + step_pair, to_hi, to_pair,
-                     device(to_hi, core, to_pair * 2 + near, lo, x))
-                )
-    staged = stage(
-        [
-            (resid_in, resid_ref), (proj_in, proj_full), (query_in, query_ref), (key_in, key_ref),
-            (value_in, value_ref), (weights_in, weights_ref),
-            (right_proj.at[core], both_proj.at[pl.ds(0, 128)]),
-        ],
-        stage_sems,
-    )
-    meet([twin] + [other[3] for other in others[3:]] + exchange.plane + exchange.line)
+    back_rows = time_sublayer(
+        exchange.finish(), qkv_full, scale_ref, shift_ref, grad_time, time_angles,
+        right_qkv, projected, sums_ref, normed, time_wide, turned, total_back, modulated,
+    )
     own, other = pl.ds(0, 128), pl.ds(128, 128)
+    exchange_back.start_plane(back_rows)
+    sums = [
+        send(sums_ref, plane_sums.at[group_at], sum_sends, sum_recvs, step, exchange.plane[step - 1])
+        for step in range(1, 8)
+    ]
+    plane_sums[group_at] = sums_ref[...]
+    piece_rows(projected, left_qkv, tall)
     twins = [
         send(right_qkv.at[1 - core], both_qkv.at[other], twin_send, twin_recv, 0, twin),
         send(left_qkv, twin_qkv, twin_send, twin_recv, 1, twin),
         send(right_proj.at[1 - core], both_proj.at[other], twin_send, twin_recv, 2, twin),
     ]
-    exchange.start_plane(back_rows[...])
-    sums = [
-        send(sums_ref, plane_sums.at[group_at], sum_sends, sum_recvs, step, exchange.plane[step - 1])
-        for step in range(1, 8)
-    ]
-    plane_sums[group_at] = sums_ref[...]
     both_qkv[own] = right_qkv[core]
+    both_proj[own] = right_proj[core]
     twins[0].wait_recv()
     twins[1].wait_recv()
     for group in range(2):
         halving.begin(group)
-    exchange.start_line()
+    exchange_back.start_line()
     for copy in sums:
         copy.wait_recv()
     line_sums[z] = jnp.sum(plane_sums[...], axis=0)
@@ -671,9 +637,7 @@
     piece = WIDTH // 64
     wanted = jnp.where(row < 4 * piece, row // piece * (16 * piece) + row % piece, -WIDTH)
     ahead = column - wanted
-    for copy in staged:
-        copy.wait()
-    frames = exchange.finish()
+    frames = exchange_back.finish()
     hidden = resid_ref[...].astype(jnp.float32) + frames.astype(jnp.float32)
     hidden_out[...] = hidden.astype(jnp.bfloat16)
     for block in range(16):
@@ -702,7 +666,7 @@
 
     def heads(first, end):
         space_back_heads(
-            range(first, end), weights_ref, query_ref, key_ref, value_ref, grad, totals
+            range(first, end), weights_ref, turned_query, turned_key, value_ref, grad, totals
         )
 
     heads(0, 10)
@@ -746,50 +710,80 @@
     for (slot, _, _, _), copy in zip(others, ends[:7]):
         copy.wait_recv()
         total += qkv_final[slot].astype(jnp.float32)
+    total = pltpu.roll(pltpu.roll(total, (QKV_WINDOW - pair * 6) % QKV_WINDOW, 0), (KEEP_LANES - hi * 32) % KEEP_LANES, 1)
     qkv_out[...] = total
     total = proj_last[hi, pl.ds(pl.multiple_of(pair * 16, 16), PROJ_WINDOW)].astype(jnp.float32)
     for (slot, _, _, _), copy in zip(others, ends[7:]):
         copy.wait_recv()
         total += proj_final[slot].astype(jnp.float32)
+    total = pltpu.roll(pltpu.roll(total, (PROJ_WINDOW - pair * 2) % PROJ_WINDOW, 0), (KEEP_LANES - hi * 32) % KEEP_LANES, 1)
     proj_out[...] = total
     for copy in twins + sums + more + list(halving.copies.values()) + ends:
         copy.wait_send()
-
-
-def tail(left, right, back_rows, sums, angles, right_proj, resid, query, key, value, weights, proj):
+    for gather in (proj, one, two, three):
+        gather.finish()
+
+
+def whole(angles, time_angles, scale, shift, query, key, value, hidden, grad_time, resid, proj, qkv):
     vmem, away = pl.BlockSpec(memory_space=pltpu.VMEM), pl.BlockSpec(memory_space=pltpu.HBM)
     b16, f32 = jnp.bfloat16, jnp.float32
     shape, dma = pltpu.VMEM, pltpu.SemaphoreType.DMA
+    wide, sums = (128, 3 * WIDTH), (2, WIDTH)
     outs = [ROWS] * 4 + [
-        (sums.shape, f32), ((QKV_WINDOW, KEEP_LANES), f32), ((PROJ_WINDOW, KEEP_LANES), f32)
+        (sums, f32), ((QKV_WINDOW, KEEP_LANES), f32), ((PROJ_WINDOW, KEEP_LANES), f32)
     ]
     counts = [last - first for _, first, last, _ in GROUPS]
-    scratch = [
-        shape(*ROWS), shape(*ROWS), shape(*ROWS), shape(*ROWS),
-        shape(weights.shape, f32), shape(proj.shape, b16), dma((7,)),
-        shape((16, PROJ_ROWS, 128), b16), shape((256, HALF_LANES), b16), shape((256, HALF_LANES), b16),
+    scratch = [shape(*ROWS)] * 6 + [
+        dma((6,)),
+        shape(*ROWS), shape(*ROWS), shape((HEADS, 128, 128), f32),
+        shape((4, 4, 80, WIDTH), b16), shape((4, 4, 80, 3 * WIDTH), b16),
+        shape(*WIDE_ROWS), shape(*ROWS), shape(*RIGHT), shape(*RIGHT), shape(wide, b16),
+        shape(sums, f32), shape(*WIDE_ROWS), shape(wide, f32), shape(wide, b16),
+        shape(*WIDE_ROWS), shape(*ROWS), shape((3 * WIDTH, 128), f32),
+        shape((16, QKV_ROWS, 128), b16), shape((16, PROJ_ROWS, 128), b16),
+        shape((256, HALF_LANES), b16), shape((256, HALF_LANES), b16),
         shape((16, QKV_ROWS, 128), b16), shape((16, PROJ_ROWS, 128), b16), dma((4,)), dma((4,)),
         shape(*WIDE_ROWS), shape(*WIDE_ROWS), shape(*WIDE_ROWS), shape(*ROWS),
-        shape((8,) + sums.shape, f32), shape((8,) + sums.shape, f32), dma((16,)), dma((16,)),
+        shape((8,) + sums, f32), shape((8,) + sums, f32), dma((16,)), dma((16,)),
         dma((6, 4)), dma((6, 4)),
         shape((2, QKV_ROWS, KEEP_LANES), b16), shape((2, PROJ_ROWS, KEEP_LANES), b16),
         shape((8, QKV_WINDOW, KEEP_LANES), b16), shape((8, PROJ_WINDOW, KEEP_LANES), b16),
         dma((16,)), dma((16,)),
-    ] + EXCHANGE_SCRATCH
+    ] + GATHER_SCRATCH * 4 + EXCHANGE_SCRATCH * 2
     scratch += [shape((16, count, HALF_LANES), b16) for count in counts]
     scratch += [
         shape((8 >> step, count, HALF_LANES), b16) for count in counts for step in range(4)
     ]
     return pl.pallas_call(
-        tail_kernel,
+        whole_kernel,
         out_shape=tuple(jax.ShapeDtypeStruct(*out) for out in outs),
-        in_specs=[vmem] * 5 + [away] * 7,
+        in_specs=[vmem] * 4 + [away] * 8,
         out_specs=(vmem,) * len(outs),
         scratch_shapes=scratch,
         compiler_params=pltpu.CompilerParams(
-            collective_id=2, has_side_effects=True, vmem_limit_bytes=44 * 1024 * 1024
+            collective_id=1, has_side_effects=True, vmem_limit_bytes=58 * 1024 * 1024
         ),
-    )(left, right, back_rows, sums, angles, right_proj, resid, query, key, value, weights, proj)
+    )(angles, time_angles, scale, shift, query, key, value, hidden, grad_time, resid, proj, qkv)
+
+
+def results_kernel(*refs):
+    given, outs = refs[:7], refs[7:]
+    for source, target in zip(given[:4], outs[:4]):
+        target[...] = source[...]
+    sums_ref, qkv_ref, proj_ref = given[4:]
+    part = WIDTH // 4
+    outs[4][...] = proj_ref[...].T[:part, : WIDTH // 64]
+    outs[5][...] = qkv_ref[...].T[:part, : 3 * WIDTH // 64]
+    outs[6][...] = sums_ref[0:1]
+    outs[7][...] = sums_ref[1:2]
+
+
+def results(*args):
+    f32, part = jnp.float32, WIDTH // 4
+    outs = [ROWS] * 4 + [
+        ((part, WIDTH // 64), f32), ((part, 3 * WIDTH // 64), f32), ((1, WIDTH), f32), ((1, WIDTH), f32)
+    ]
+    return local_call(results_kernel, outs, [], 16, *args)
 
 
 def turn_angles(places, half):
@@ -820,35 +814,12 @@
     def flat(values):
         return values.reshape(128, WIDTH)
 
-    rows, right_proj, space_query, space_key, space_weights, proj_full, qkv_full = front(
-        flat(query_space), flat(key_space), flat(value_space), flat(hidden), space_angles,
-        proj_space, qkv_time,
-    )
-    right_qkv, grad_projected, resid_back, sums = time_sublayer(
-        rows, qkv_full, scale_time, shift_time, flat(grad_attn_time), time_angles
-    )
-    left = jnp.transpose(grad_projected.T.reshape(4, 16, 54, 128), (1, 0, 2, 3)).reshape(16, 216, 128)
-    left = jnp.pad(left, ((0, 0), (0, QKV_ROWS - 216), (0, 0)))
-    grad_hidden, grad_query, grad_key, grad_value, sums, qkv_block, proj_block = tail(
-        left, right_qkv, resid_back, sums[:2].reshape(8, -1), space_angles, right_proj,
-        flat(grad_resid), space_query, space_key, flat(value_space), space_weights, proj_full,
-    )
-    sums = sums.reshape(2, WIDTH)
-    hi, pair = lax.axis_index("dp") // 2, seq_place // 16
-    column = hi * (WIDTH // 4 + KEEP_LANES - HALF_LANES)
-    grad_qkv_time = lax.dynamic_slice(qkv_block, (pair * 6, column), (54, WIDTH // 4)).T
-    grad_proj_space = lax.dynamic_slice(proj_block, (pair * 2, column), (18, WIDTH // 4)).T
-    shape = hidden.shape
-    return (
-        grad_hidden.reshape(shape),
-        grad_query.reshape(shape),
-        grad_key.reshape(shape),
-        grad_value.reshape(shape),
-        grad_proj_space,
-        grad_qkv_time,
-        sums[:1],
-        sums[1:],
-    )
+    sums_and_grads = whole(
+        space_angles, time_angles, scale_time, shift_time, flat(query_space), flat(key_space),
+        flat(value_space), flat(hidden), flat(grad_attn_time), flat(grad_resid), proj_space, qkv_time,
+    )
+    outs = results(*sums_and_grads)
+    return tuple(out.reshape(hidden.shape) for out in outs[:4]) + tuple(outs[4:])
 
 
 def solution(mesh):

time: 175 us -> 155 us (0.89)
  the two profiles are of different devices: /device:TPU:1 before, /device:TPU:32 now
where the time goes in v5:
time: 155 us; the launch traced here: 154 us
  Pallas kernels  141 us (91%)
  local copies, waits for them, and re-layouts  11.5 us (7%)
    pallas_call x1, Pallas kernels, whole(): pl.pallas_call(whole_kernel, out_shape=tuple((jax.ShapeDtypeStruct(*out)...  139 us
    unnamed x16, local copies, waits for them, and re-layouts  7.72 us

profile of v5, /device:TPU:32, one launch (start us, length us, event | category | flops | bytes accessed | tf_op | source)
XLA Modules:
  0.0 154.1 jit_solution(3283106193041742926)
XLA Ops:
  0.7 0.1 mul.42
  0.8 0.8 slice.7
  1.5 0.1 dynamic-slice_convert_fusion
  1.6 0.1 convert_element_type.28
  1.7 0.8 slice.6
  2.6 0.1 copy.25
  2.7 0.2 multiply_cosine_fusion.1
  3.0 0.3 multiply_cosine_fusion
  3.3 0.8 select_maximum_fusion
  4.0 1.8 %reshape.100.grad_time_in = bf16[128,1152]{1,0:T(8,128)(2,1)} reshape(bf16[1,64,2,1152]{3,2,1,0:T(2,128)(2,1)} %param.20) | data formatting | bytes 589824 | tf_op jit(solution)/shard_map/reshape | solution.py:815
  5.8 139.5 %shard_map.170 = (bf16[128,1152]{1,0:T(8,128)(2,1)}, bf16[128,1152]{1,0:T(8,128)(2,1)}, bf16[128,1152]{1,0:T(8,128)(2,1)}, bf16[128,1152]{1,0:T(8,128)(2,1)}, f3...) custom-call(f32[128,128]{1,0:T(8,128)} %get-tuple-element.67.angles_ref, ...), custom_call_target="tpu_custom_call" | custom-call | tf_op jit(solution)/shard_map/pallas_call | solution.py:757
  145.3 0.0 copy-start
  145.3 1.0 copy-done
  146.3 0.0 copy-start.1
  146.3 1.0 copy-done.1
  147.2 0.0 copy-start.2
  147.2 1.0 copy-done.2
  148.2 1.0 copy-done.3
  149.1 0.9 copy-done.4
  150.0 0.8 copy-done.5
  150.8 0.7 copy-done.6
  151.5 1.1 shard_map.171
  152.6 0.7 copy.28
  153.4 0.8 copy.29
  (10 shorter events, 0.0 us)
Async XLA Ops:
  145.3 1.0 copy-start
  146.3 1.0 copy-start.1
  147.2 1.0 copy-start.2
  148.2 1.0 copy-start.3
  149.1 0.9 copy-start.4
  150.0 0.8 copy-start.5
  150.8 0.7 copy-start.6

commit v6 on v5

--- a/solution.py
+++ b/solution.py
@@ -2,6 +2,7 @@
 
 import jax
 import jax.numpy as jnp
+import numpy as np
 from jax import lax
 from jax.experimental import pallas as pl
 from jax.experimental.pallas import tpu as pltpu
@@ -19,7 +20,8 @@
 KEEP_LANES = 384
 ORDER = ("x_near", "y_near", "x_far", "z_near")
 GROUPS = (
-    (0, 0, 64, 0), (0, 64, 128, 1), (0, 128, 176, 2), (0, 176, 224, 3), (1, 0, 48, 2), (1, 48, 80, 3)
+    (0, 0, 64, 0), (0, 64, 128, 1), (0, 128, 176, 2), (0, 176, 224, 3), (1, 0, 16, 0), (1, 16, 32, 1),
+    (1, 32, 48, 2), (1, 48, 80, 3),
 )
 QKV_ROWS, PROJ_ROWS = 224, 80
 QKV_WINDOW, PROJ_WINDOW = 80, 32
@@ -45,11 +47,10 @@
     return copy
 
 
-def meet(peers):
+def greet(peers):
     barrier = pltpu.get_barrier_semaphore()
     for peer in peers:
         pl.semaphore_signal(barrier, inc=1, device_id=peer, device_id_type=MESH)
-    pl.semaphore_wait(barrier, len(peers))
 
 
 def order_of(group):
@@ -211,16 +212,24 @@
 
 
 class Gather:
-    def __init__(self, own, full, cut, sends, recvs, local):
+    def __init__(self, own, full, cut, along_x, sends, recvs, local):
         self.own, self.full, self.cut = own, full, cut
         self.sends, self.recvs, self.local = sends, recvs, local
-        self.hi, self.core, z, lo, self.x = place()
-        hi, core, x = self.hi, self.core, self.x
+        hi, core, z, lo, x = place()
         self.mine, self.far = hi * 2 + core, (1 - hi) * 2 + core
         self.twin = device(hi, 1 - core, z, lo, x)
         self.across = device(1 - hi, core, z, 1 - lo, x)
-        self.right = device(hi, core, z, lo, (x + 1) % 4)
-        self.left = device(hi, core, z, lo, (x + 3) % 4)
+        if along_x:
+            self.spot, self.there = x, x
+            self.right = device(hi, core, z, lo, (x + 1) % 4)
+            self.left = device(hi, core, z, lo, (x + 3) % 4)
+        else:
+            self.spot = lo * 2 + (lo + z) % 2
+            self.there = 3 - self.spot
+            self.right, self.left = [
+                device(hi, core, z // 2 * 2 + (at % 2 + at // 2) % 2, at // 2, x)
+                for at in ((self.spot + 1) % 4, (self.spot + 3) % 4)
+            ]
         self.copies = {}
 
     def go(self, at, source, target, peer):
@@ -230,8 +239,8 @@
         self.go(at, ref, ref, peer)
 
     def start(self):
-        start = pl.multiple_of(self.x * 64 + self.x // 2 * 16, 16)
-        self.go(0, self.own.at[pl.ds(start, 80)], self.full.at[self.mine, self.x], self.across)
+        start = pl.multiple_of(self.there * 64 + self.there // 2 * 16, 16)
+        self.go(0, self.own.at[pl.ds(start, 80)], self.full.at[self.mine, self.there], self.across)
         self.locals = []
         for quarter, first in enumerate(STARTS):
             source, target = self.own.at[pl.ds(first, 80)], self.full.at[self.mine, quarter]
@@ -242,7 +251,7 @@
 
     def spread(self):
         self.copies[0].wait_recv()
-        piece = self.full.at[self.far, self.x]
+        piece = self.full.at[self.far, self.spot]
         self.same(2, piece, self.right)
         self.same(3, piece, self.left)
         self.same(4, piece, self.twin)
@@ -250,18 +259,18 @@
     def pass_on(self):
         cut, width = self.cut, self.full.shape[3]
         self.copies[2].wait_recv()
-        from_left = (self.far, (self.x + 3) % 4)
+        from_left = (self.far, (self.spot + 3) % 4)
         self.same(5, self.full.at[from_left + (slice(None), pl.ds(0, cut))], self.right)
         self.same(6, self.full.at[from_left], self.twin)
         self.copies[3].wait_recv()
-        from_right = (self.far, (self.x + 1) % 4)
+        from_right = (self.far, (self.spot + 1) % 4)
         self.same(7, self.full.at[from_right + (slice(None), pl.ds(cut, width - cut))], self.left)
         self.same(8, self.full.at[from_right], self.twin)
 
     def last(self):
         self.copies[5].wait_recv()
         self.copies[7].wait_recv()
-        self.same(9, self.full.at[self.far, (self.x + 2) % 4], self.twin)
+        self.same(9, self.full.at[self.far, (self.spot + 2) % 4], self.twin)
 
     def arrive(self):
         for copy in self.locals:
@@ -327,6 +336,26 @@
     return cosine, sine
 
 
+def make_angles(positions, rates, space_angles, time_angles):
+    lane = lax.broadcasted_iota(jnp.int32, (128, 128), 1)
+    token = lax.broadcasted_iota(jnp.int32, (128, 128), 0)
+    frame = pl.ds(lax.axis_index("seq"), 1)
+
+    def spots(axis):
+        places = positions[axis, 0, frame, :].astype(jnp.float32)
+        return jnp.broadcast_to(places, (128, 128)).T
+
+    stride = positions[0, 0, 1:2, 0:1].astype(jnp.float32)
+    frames = jnp.broadcast_to(stride, (128, 128)) * (token // 2).astype(jnp.float32)
+    by_row = lane % (HEAD // 2) < HEAD // 4
+    for at, places, out in (
+        (0, jnp.where(by_row, spots(1), spots(2)), space_angles), (1, frames, time_angles)
+    ):
+        angles = places * rates[at : at + 1]
+        turned = jnp.where(lane < HEAD // 2, jnp.cos(angles), jnp.sin(angles))
+        out[...] = jnp.where(lane < HEAD, turned, 0.0)
+
+
 def turn(values, cosine, sine, half, direction):
     lane = lax.broadcasted_iota(jnp.int32, (1, WIDTH), 1) % (2 * half)
     partner = jnp.where(
@@ -397,17 +426,6 @@
     for copy in copies:
         copy.start()
     return copies
-
-
-def local_call(kernel, outs, scratch, megabytes, *args):
-    return pl.pallas_call(
-        kernel,
-        out_shape=tuple(jax.ShapeDtypeStruct(shape, kind) for shape, kind in outs),
-        in_specs=[pl.BlockSpec(memory_space=pltpu.VMEM)] * len(args),
-        out_specs=tuple(pl.BlockSpec(memory_space=pltpu.VMEM) for _ in outs),
-        scratch_shapes=[pltpu.VMEM(shape, kind) for shape, kind in scratch],
-        compiler_params=pltpu.CompilerParams(vmem_limit_bytes=megabytes * 1024 * 1024),
-    )(*args)
 
 
 ROWS = ((128, WIDTH), jnp.bfloat16)
@@ -493,10 +511,11 @@
 
 
 def whole_kernel(
-    angles_ref, time_angles, scale_ref, shift_ref,
+    scale_in, shift_in, positions_in, rates_in,
     query_in, key_in, value_in, hidden_in, grad_time_in, resid_in, proj_ref, qkv_ref,
     hidden_out, query_out, key_out, value_out, total_ref, qkv_out, proj_out,
-    query_ref, key_ref, value_ref, hidden_ref, grad_time, resid_ref, stage_sems,
+    query_ref, key_ref, value_ref, hidden_ref, grad_time, resid_ref,
+    scale_ref, shift_ref, positions, rates, angles_ref, time_angles, stage_sems,
     turned_query, turned_key, weights_ref, proj_full, qkv_full,
     wide, mixed_ref, right_qkv, right_proj, projected, sums_ref, normed, time_wide, turned,
     total_back, modulated, tall,
@@ -510,6 +529,7 @@
         [
             (query_in, query_ref), (key_in, key_ref), (value_in, value_ref),
             (hidden_in, hidden_ref), (grad_time_in, grad_time), (resid_in, resid_ref),
+            (scale_in, scale_ref), (shift_in, shift_ref), (positions_in, positions), (rates_in, rates),
         ],
         stage_sems,
     )
@@ -517,13 +537,13 @@
     near, pair = z % 2, z // 2
     twin = device(hi, 1 - core, z, lo, x)
     count = len(GROUPS)
-    proj = Gather(proj_ref, proj_full, 640, *scratch[:3])
+    proj = Gather(proj_ref, proj_full, 640, True, *scratch[:3])
     thirds = []
     for third in range(3):
         columns = pl.ds(third * WIDTH, WIDTH)
         thirds.append(
             Gather(
-                qkv_ref.at[:, columns], qkv_full.at[:, :, :, columns], 640,
+                qkv_ref.at[:, columns], qkv_full.at[:, :, :, columns], 640, third == 1,
                 *scratch[3 * third + 3 : 3 * third + 6],
             )
         )
@@ -546,18 +566,19 @@
                     (step_hi * 4 + step_pair, to_hi, to_pair,
                      device(to_hi, core, to_pair * 2 + near, lo, x))
                 )
-    meet(
-        [twin, proj.across] + [other[3] for other in others[3:]] + exchange.plane + exchange.line
-    )
-    for gather in (proj, one, two, three):
-        gather.start()
+    peers = [twin, proj.across] + [other[3] for other in others[3:]] + exchange.plane + exchange.line
+    greet(peers)
     for copy in staged:
         copy.wait()
+    make_angles(positions, rates, angles_ref, time_angles)
     cosine, sine = turn_tables(angles_ref[...], HEAD // 4)
     for source, target in ((query_ref, turned_query), (key_ref, turned_key)):
         values = source[...].astype(jnp.float32)
         target[...] = turn(values, cosine, sine, HEAD // 4, 1.0).astype(jnp.bfloat16)
     wide[...] = jnp.zeros_like(wide)
+    pl.semaphore_wait(pltpu.get_barrier_semaphore(), len(peers))
+    for gather in (proj, one, two, three):
+        gather.start()
 
     def heads(first):
         space_forward(
@@ -654,9 +675,9 @@
     grad[...] = total_query[...].astype(jnp.bfloat16)
     twins[2].wait_recv()
     twins[3].wait_recv()
-    for group in range(4, 6):
+    for group in range(4, 8):
         halving.begin(group)
-    for group in range(4, 6):
+    for group in range(4, 8):
         halving.keep(group)
     for group in range(4):
         halving.advance(group, 1)
@@ -673,7 +694,7 @@
     for group in range(4):
         halving.advance(group, 2)
     heads(10, 16)
-    for group in range(4, 6):
+    for group in range(4, 8):
         halving.advance(group, 1)
     for group in range(4):
         halving.advance(group, 3)
@@ -684,7 +705,7 @@
     for copy in more:
         copy.wait_recv()
     total_ref[...] = jnp.sum(line_sums[...], axis=0)
-    for group in range(4, 6):
+    for group in range(4, 8):
         halving.advance(group, 2)
     for group in range(4):
         halving.last(group, qkv_last)
@@ -694,9 +715,9 @@
         ends.append(
             send(qkv_last.at[to_hi, rows], qkv_final.at[slot], final_send, final_recv, slot, peer)
         )
-    for group in range(4, 6):
+    for group in range(4, 8):
         halving.advance(group, 3)
-    for group in range(4, 6):
+    for group in range(4, 8):
         halving.last(group, proj_last)
     for slot, to_hi, to_pair, peer in others:
         rows = pl.ds(pl.multiple_of(to_pair * 16, 16), PROJ_WINDOW)
@@ -724,7 +745,7 @@
         gather.finish()
 
 
-def whole(angles, time_angles, scale, shift, query, key, value, hidden, grad_time, resid, proj, qkv):
+def whole(scale, shift, positions, rates, query, key, value, hidden, grad_time, resid, proj, qkv):
     vmem, away = pl.BlockSpec(memory_space=pltpu.VMEM), pl.BlockSpec(memory_space=pltpu.HBM)
     b16, f32 = jnp.bfloat16, jnp.float32
     shape, dma = pltpu.VMEM, pltpu.SemaphoreType.DMA
@@ -734,7 +755,8 @@
     ]
     counts = [last - first for _, first, last, _ in GROUPS]
     scratch = [shape(*ROWS)] * 6 + [
-        dma((6,)),
+        shape(scale.shape, f32), shape(scale.shape, f32), shape(positions.shape, positions.dtype),
+        shape(rates.shape, f32), shape((128, 128), f32), shape((128, 128), f32), dma((10,)),
         shape(*ROWS), shape(*ROWS), shape((HEADS, 128, 128), f32),
         shape((4, 4, 80, WIDTH), b16), shape((4, 4, 80, 3 * WIDTH), b16),
         shape(*WIDE_ROWS), shape(*ROWS), shape(*RIGHT), shape(*RIGHT), shape(wide, b16),
@@ -745,7 +767,7 @@
         shape((16, QKV_ROWS, 128), b16), shape((16, PROJ_ROWS, 128), b16), dma((4,)), dma((4,)),
         shape(*WIDE_ROWS), shape(*WIDE_ROWS), shape(*WIDE_ROWS), shape(*ROWS),
         shape((8,) + sums, f32), shape((8,) + sums, f32), dma((16,)), dma((16,)),
-        dma((6, 4)), dma((6, 4)),
+        dma((8, 4)), dma((8, 4)),
         shape((2, QKV_ROWS, KEEP_LANES), b16), shape((2, PROJ_ROWS, KEEP_LANES), b16),
         shape((8, QKV_WINDOW, KEEP_LANES), b16), shape((8, PROJ_WINDOW, KEEP_LANES), b16),
         dma((16,)), dma((16,)),
@@ -757,39 +779,54 @@
     return pl.pallas_call(
         whole_kernel,
         out_shape=tuple(jax.ShapeDtypeStruct(*out) for out in outs),
-        in_specs=[vmem] * 4 + [away] * 8,
+        in_specs=[away] * 12,
         out_specs=(vmem,) * len(outs),
         scratch_shapes=scratch,
         compiler_params=pltpu.CompilerParams(
             collective_id=1, has_side_effects=True, vmem_limit_bytes=58 * 1024 * 1024
         ),
-    )(angles, time_angles, scale, shift, query, key, value, hidden, grad_time, resid, proj, qkv)
+    )(scale, shift, positions, rates, query, key, value, hidden, grad_time, resid, proj, qkv)
 
 
 def results_kernel(*refs):
-    given, outs = refs[:7], refs[7:]
-    for source, target in zip(given[:4], outs[:4]):
-        target[...] = source[...]
-    sums_ref, qkv_ref, proj_ref = given[4:]
+    given, outs, (sums_ref, qkv_ref, proj_ref, sems) = refs[:7], refs[7:15], refs[15:]
+    copies = stage(
+        list(zip(given[4:], (sums_ref, qkv_ref, proj_ref))) + list(zip(given[:4], outs[:4])), sems
+    )
+    for copy in copies[:3]:
+        copy.wait()
     part = WIDTH // 4
-    outs[4][...] = proj_ref[...].T[:part, : WIDTH // 64]
-    outs[5][...] = qkv_ref[...].T[:part, : 3 * WIDTH // 64]
+    outs[4][...] = proj_ref[: WIDTH // 64, :part]
+    outs[5][...] = qkv_ref[: 3 * WIDTH // 64, :part]
     outs[6][...] = sums_ref[0:1]
     outs[7][...] = sums_ref[1:2]
+    for copy in copies[3:]:
+        copy.wait()
 
 
 def results(*args):
     f32, part = jnp.float32, WIDTH // 4
     outs = [ROWS] * 4 + [
-        ((part, WIDTH // 64), f32), ((part, 3 * WIDTH // 64), f32), ((1, WIDTH), f32), ((1, WIDTH), f32)
+        ((WIDTH // 64, part), f32), ((3 * WIDTH // 64, part), f32), ((1, WIDTH), f32), ((1, WIDTH), f32)
     ]
-    return local_call(results_kernel, outs, [], 16, *args)
-
-
-def turn_angles(places, half):
-    frequency = 10000.0 ** (-jnp.arange(half, dtype=jnp.float32) / half)
-    angles = (places.astype(jnp.float32)[:, :, None] * frequency).reshape(128, 36)
-    return jnp.pad(jnp.concatenate([jnp.cos(angles), jnp.sin(angles)], axis=1), ((0, 0), (0, 56)))
+    vmem, away = pl.BlockSpec(memory_space=pltpu.VMEM), pl.BlockSpec(memory_space=pltpu.HBM)
+    return pl.pallas_call(
+        results_kernel,
+        out_shape=tuple(jax.ShapeDtypeStruct(shape, kind) for shape, kind in outs),
+        in_specs=[away] * 7,
+        out_specs=(away,) * 4 + (vmem,) * 4,
+        scratch_shapes=[pltpu.VMEM(arg.shape, arg.dtype) for arg in args[4:]]
+        + [pltpu.SemaphoreType.DMA((7,))],
+        compiler_params=pltpu.CompilerParams(vmem_limit_bytes=58 * 1024 * 1024),
+    )(*args)
+
+
+def turn_rates():
+    rows = []
+    for half in (HEAD // 4, HEAD // 2):
+        frequency = np.float32(10000.0) ** (-np.arange(half, dtype=np.float32) / np.float32(half))
+        rows.append(np.pad(np.tile(frequency, HEAD // half), (0, 56)))
+    return np.stack(rows + [np.zeros(128)] * 6).astype(np.float32)
 
 
 def body(
@@ -805,21 +842,18 @@
     grad_attn_time,
     grad_resid,
 ):
-    seq_place = lax.axis_index("seq")
-    frame_places = lax.dynamic_slice_in_dim(positions[0, 0], seq_place * 2, 2, 1).reshape(128, 1)
-    spot_places = lax.dynamic_slice_in_dim(positions[1:, 0], seq_place, 1, 1).reshape(2, 128).T
-    space_angles = turn_angles(spot_places, HEAD // 4)
-    time_angles = turn_angles(frame_places, HEAD // 2)
-
     def flat(values):
         return values.reshape(128, WIDTH)
 
-    sums_and_grads = whole(
-        space_angles, time_angles, scale_time, shift_time, flat(query_space), flat(key_space),
-        flat(value_space), flat(hidden), flat(grad_attn_time), flat(grad_resid), proj_space, qkv_time,
-    )
-    outs = results(*sums_and_grads)
-    return tuple(out.reshape(hidden.shape) for out in outs[:4]) + tuple(outs[4:])
+    outs = results(
+        *whole(
+            scale_time, shift_time, positions, turn_rates(), flat(query_space), flat(key_space),
+            flat(value_space), flat(hidden), flat(grad_attn_time), flat(grad_resid), proj_space,
+            qkv_time,
+        )
+    )
+    grads = tuple(out.reshape(hidden.shape) for out in outs[:4])
+    return grads + (outs[4].T, outs[5].T, outs[6], outs[7])
 
 
 def solution(mesh):

time: 155 us -> 173 us (1.12)
  the two profiles are of different devices: /device:TPU:32 before, /device:TPU:1 now
where the time goes in v6:
time: 173 us; the launch traced here: 170 us
  Pallas kernels  168 us (97%)
  local copies, waits for them, and re-layouts  1.79 us (1%)
    pallas_call x1, Pallas kernels, whole(): pl.pallas_call(whole_kernel, out_shape=tuple((jax.ShapeDtypeStruct(*out)...  130 us
    pallas_call x1, Pallas kernels, results(): pl.pallas_call(results_kernel, out_shape=tuple((jax.ShapeDtypeStruct(shap...  37.6 us

profile of v6, /device:TPU:1, one launch (start us, length us, event | category | flops | bytes accessed | tf_op | source)
XLA Modules:
  0.0 170.5 jit_solution(5923265832695877927)
XLA Ops:
  0.6 1.8 %reshape.50.grad_time_in = bf16[128,1152]{1,0:T(8,128)(2,1)} reshape(bf16[1,64,2,1152]{3,2,1,0:T(2,128)(2,1)} %param.21) | data formatting | bytes 589824 | tf_op jit(solution)/shard_map/reshape | solution.py:846
  2.4 130.3 %shard_map.179 = (bf16[128,1152]{1,0:T(8,128)(2,1)}, bf16[128,1152]{1,0:T(8,128)(2,1)}, bf16[128,1152]{1,0:T(8,128)(2,1)}, bf16[128,1152]{1,0:T(8,128)(2,1)}, f3...) custom-call(f32[1,1152]{1,0:T(1,128)} %scale_in.1, f32[1,1152]{1,0:T(1,128)} %shift_in.1, ...), custom_call_target="tpu_custom_call" | custom-call | tf_op jit(solution)/shard_map/pallas_call | solution.py:779
  132.8 37.6 %shard_map.180 = (bf16[128,1152]{1,0:T(8,128)(2,1)}, bf16[128,1152]{1,0:T(8,128)(2,1)}, bf16[128,1152]{1,0:T(8,128)(2,1)}, bf16[128,1152]{1,0:T(8,128)(2,1)}, f3...) custom-call(bf16[128,1152]{1,0:T(8,128)(2,1)} %get-tuple-element.23.refs_0_, ...), custom_call_target="tpu_custom_call" | custom-call | tf_op jit(solution)/shard_map/pallas_call | solution.py:813

commit v7 on v6

--- a/solution.py
+++ b/solution.py
@@ -814,7 +814,7 @@
         results_kernel,
         out_shape=tuple(jax.ShapeDtypeStruct(shape, kind) for shape, kind in outs),
         in_specs=[away] * 7,
-        out_specs=(away,) * 4 + (vmem,) * 4,
+        out_specs=(vmem,) * 8,
         scratch_shapes=[pltpu.VMEM(arg.shape, arg.dtype) for arg in args[4:]]
         + [pltpu.SemaphoreType.DMA((7,))],
         compiler_params=pltpu.CompilerParams(vmem_limit_bytes=58 * 1024 * 1024),

time: 173 us -> 138 us (0.80)
  Pallas kernels: 168 us -> 133 us
    pallas_call x1, Pallas kernels: 37.6 us -> 2.44 us  [results(): pl.pallas_call(results_kernel, out_shape=tuple((jax.ShapeDtypeStruct(shap...]
where the time goes in v7:
time: 138 us; the launch traced here: 135 us
  Pallas kernels  133 us (96%)
  local copies, waits for them, and re-layouts  1.79 us (1%)
    pallas_call x1, Pallas kernels, whole(): pl.pallas_call(whole_kernel, out_shape=tuple((jax.ShapeDtypeStruct(*out)...  130 us

profile of v7, /device:TPU:1, one launch (start us, length us, event | category | flops | bytes accessed | tf_op | source)
XLA Modules:
  0.0 135.4 jit_solution(14436227545155051241)
XLA Ops:
  0.6 1.8 %reshape.50.grad_time_in = bf16[128,1152]{1,0:T(8,128)(2,1)} reshape(bf16[1,64,2,1152]{3,2,1,0:T(2,128)(2,1)} %param.21) | data formatting | bytes 589824 | tf_op jit(solution)/shard_map/reshape | solution.py:846
  2.4 130.3 %shard_map.179 = (bf16[128,1152]{1,0:T(8,128)(2,1)}, bf16[128,1152]{1,0:T(8,128)(2,1)}, bf16[128,1152]{1,0:T(8,128)(2,1)}, bf16[128,1152]{1,0:T(8,128)(2,1)}, f3...) custom-call(f32[1,1152]{1,0:T(1,128)} %scale_in.1, f32[1,1152]{1,0:T(1,128)} %shift_in.1, ...), custom_call_target="tpu_custom_call" | custom-call | tf_op jit(solution)/shard_map/pallas_call | solution.py:779
  132.8 2.4 %shard_map.180 = (bf16[128,1152]{1,0:T(8,128)(2,1)}, bf16[128,1152]{1,0:T(8,128)(2,1)}, bf16[128,1152]{1,0:T(8,128)(2,1)}, bf16[128,1152]{1,0:T(8,128)(2,1)}, f3...) custom-call(bf16[128,1152]{1,0:T(8,128)(2,1)} %get-tuple-element.23.refs_0_, ...), custom_call_target="tpu_custom_call" | custom-call | tf_op jit(solution)/shard_map/pallas_call | solution.py:813

commit v8 on v7

--- a/solution.py
+++ b/solution.py
@@ -434,7 +434,7 @@
 
 
 def time_sublayer(
-    rows, qkv_full, scale_ref, shift_ref, grad_ref, angles_ref,
+    rows, gathers, qkv_full, scale_ref, shift_ref, grad_ref, angles_ref,
     right_ref, projected_ref, sums_ref,
     normed_ref, wide, turned, total_back, modulated_ref,
 ):
@@ -449,6 +449,8 @@
     for core in range(2):
         right_ref[core] = core_columns(modulated, core)
     for block in range(9):
+        if block % 3 == 0:
+            gathers[block // 3].arrive()
         columns = slice(block * 384, block * 384 + 384)
         wide[:, columns] = jnp.dot(
             modulated_ref[...], weight_rows(qkv_full, columns), preferred_element_type=jnp.float32
@@ -499,12 +501,15 @@
     ).astype(jnp.bfloat16)
 
 
-def piece_rows(values_ref, turned_rows, tall):
+def tall_rows(values_ref, tall):
     for block in range(27):
         rows = slice(block * 128, block * 128 + 128)
         tall[rows] = values_ref[:, rows].astype(jnp.float32).T
+
+
+def piece_rows(tall, turned_rows, combinations):
     piece = 3 * WIDTH // 64
-    for at in range(16):
+    for at in combinations:
         parts = [tall[(16 * k + at) * piece : (16 * k + at + 1) * piece] for k in range(4)]
         parts.append(jnp.zeros((QKV_ROWS - 4 * piece, 128), jnp.float32))
         turned_rows[at] = jnp.concatenate(parts, axis=0).astype(jnp.bfloat16)
@@ -613,10 +618,8 @@
     two.last()
     three.pass_on()
     three.last()
-    for gather in thirds:
-        gather.arrive()
     back_rows = time_sublayer(
-        exchange.finish(), qkv_full, scale_ref, shift_ref, grad_time, time_angles,
+        exchange.finish(), thirds, qkv_full, scale_ref, shift_ref, grad_time, time_angles,
         right_qkv, projected, sums_ref, normed, time_wide, turned, total_back, modulated,
     )
     own, other = pl.ds(0, 128), pl.ds(128, 128)
@@ -626,16 +629,22 @@
         for step in range(1, 8)
     ]
     plane_sums[group_at] = sums_ref[...]
-    piece_rows(projected, left_qkv, tall)
-    twins = [
+    to_right = [
         send(right_qkv.at[1 - core], both_qkv.at[other], twin_send, twin_recv, 0, twin),
-        send(left_qkv, twin_qkv, twin_send, twin_recv, 1, twin),
         send(right_proj.at[1 - core], both_proj.at[other], twin_send, twin_recv, 2, twin),
     ]
+    tall_rows(projected, tall)
+    to_left = []
+    for at, sem in ((0, 1), (8, 4)):
+        piece_rows(tall, left_qkv, range(at, at + 8))
+        half = pl.ds(at, 8)
+        to_left.append(send(left_qkv.at[half], twin_qkv.at[half], twin_send, twin_recv, sem, twin))
+    twins = [to_right[0], to_left[0], to_right[1]]
     both_qkv[own] = right_qkv[core]
     both_proj[own] = right_proj[core]
     twins[0].wait_recv()
     twins[1].wait_recv()
+    to_left[1].wait_recv()
     for group in range(2):
         halving.begin(group)
     exchange_back.start_line()
@@ -739,7 +748,7 @@
         total += proj_final[slot].astype(jnp.float32)
     total = pltpu.roll(pltpu.roll(total, (PROJ_WINDOW - pair * 2) % PROJ_WINDOW, 0), (KEEP_LANES - hi * 32) % KEEP_LANES, 1)
     proj_out[...] = total
-    for copy in twins + sums + more + list(halving.copies.values()) + ends:
+    for copy in twins + to_left[1:] + sums + more + list(halving.copies.values()) + ends:
         copy.wait_send()
     for gather in (proj, one, two, three):
         gather.finish()
@@ -764,7 +773,7 @@
         shape(*WIDE_ROWS), shape(*ROWS), shape((3 * WIDTH, 128), f32),
         shape((16, QKV_ROWS, 128), b16), shape((16, PROJ_ROWS, 128), b16),
         shape((256, HALF_LANES), b16), shape((256, HALF_LANES), b16),
-        shape((16, QKV_ROWS, 128), b16), shape((16, PROJ_ROWS, 128), b16), dma((4,)), dma((4,)),
+        shape((16, QKV_ROWS, 128), b16), shape((16, PROJ_ROWS, 128), b16), dma((5,)), dma((5,)),
         shape(*WIDE_ROWS), shape(*WIDE_ROWS), shape(*WIDE_ROWS), shape(*ROWS),
         shape((8,) + sums, f32), shape((8,) + sums, f32), dma((16,)), dma((16,)),
         dma((8, 4)), dma((8, 4)),

time: 138 us -> 138 us (level)
  no operation moved by 1% of the time
where the time goes in v8:
time: 138 us; the launch traced here: 136 us
  Pallas kernels  134 us (97%)
  local copies, waits for them, and re-layouts  1.79 us (1%)
    pallas_call x1, Pallas kernels, whole(): pl.pallas_call(whole_kernel, out_shape=tuple((jax.ShapeDtypeStruct(*out)...  131 us

profile of v8, /device:TPU:1, one launch (start us, length us, event | category | flops | bytes accessed | tf_op | source)
XLA Modules:
  0.0 136.1 jit_solution(2465347412477465483)
XLA Ops:
  0.6 1.8 %reshape.50.grad_time_in = bf16[128,1152]{1,0:T(8,128)(2,1)} reshape(bf16[1,64,2,1152]{3,2,1,0:T(2,128)(2,1)} %param.21) | data formatting | bytes 589824 | tf_op jit(solution)/shard_map/reshape | solution.py:855
  2.4 131.1 %shard_map.179 = (bf16[128,1152]{1,0:T(8,128)(2,1)}, bf16[128,1152]{1,0:T(8,128)(2,1)}, bf16[128,1152]{1,0:T(8,128)(2,1)}, bf16[128,1152]{1,0:T(8,128)(2,1)}, f3...) custom-call(f32[1,1152]{1,0:T(1,128)} %scale_in.1, f32[1,1152]{1,0:T(1,128)} %shift_in.1, ...), custom_call_target="tpu_custom_call" | custom-call | tf_op jit(solution)/shard_map/pallas_call | solution.py:788
  133.5 2.4 %shard_map.180 = (bf16[128,1152]{1,0:T(8,128)(2,1)}, bf16[128,1152]{1,0:T(8,128)(2,1)}, bf16[128,1152]{1,0:T(8,128)(2,1)}, bf16[128,1152]{1,0:T(8,128)(2,1)}, f3...) custom-call(bf16[128,1152]{1,0:T(8,128)(2,1)} %get-tuple-element.23.refs_0_, ...), custom_call_target="tpu_custom_call" | custom-call | tf_op jit(solution)/shard_map/pallas_call | solution.py:822
